TPU v7x, 512 devices: a whole 4x8x8 slice. The times are simulated.
512 devices in a mesh: tm: 32 (over x, z), row: 8 (over y), col: 2 (over core).
Axes of the slice: x: 4, y: 8, z: 8, core: 2. Of those that a mesh axis runs over, the one named last changes fastest.
Arguments:
- features: bfloat16 [64, 48, 32, 512], P('tm', 'row', 'col'), may hold values from -16 to 16, as said below
- gn1_gain: float32 [512], replicated, may hold values from 0.1 to 1.9
- gn1_bias: float32 [512], replicated, may hold values from -3 to 3
- conv1_weight: bfloat16 [27, 512, 256], P(None, ('row', 'col')), may hold values from -0.0546875 to 0.0546875
- conv1_bias: float32 [256], replicated, may hold values from -3 to 3
- skip_weight: bfloat16 [1, 512, 256], P(None, ('row', 'col')), may hold values from -0.25 to 0.25
- gn2_gain: float32 [256], replicated, may hold values from 0.1 to 1.9
- gn2_bias: float32 [256], replicated, may hold values from -3 to 3
- conv2_weight: bfloat16 [27, 256, 256], P(None, ('row', 'col')), may hold values from -0.078125 to 0.078125
- conv2_bias: float32 [256], replicated, may hold values from -3 to 3
Outputs:
- block_out: bfloat16 [64, 48, 32, 256], P('tm', 'row', 'col')
Inputs may be any that keep to these rules, and one draw needn't show every extreme that they name: Latent features of the decoder, of mixed scales over frames, positions and channels.
All inputs are finite; a program needn't handle non-finite values.
Results may differ from a plain program's by a relative error of at most 0.0065.
Values may be sent and summed in bfloat16 or wider, within the bound.
No kernel may reach another device: no remote copies, remote signals or barrier semaphores. Data moves between devices by JAX's collectives and lax.ppermute only.
A program may use at most 64 MiB of HBM per device.

v0:
```python
import jax
import jax.numpy as jnp
from jax import lax
from jax.sharding import PartitionSpec as P

GROUPS = 32


def passed_along(block, axis, distance):
    devices = range(lax.axis_size(axis))
    route = [(i - distance, i) for i in devices if i - distance in devices]
    return lax.ppermute(block, axis, route)


def with_halo(array, sides, width):
    for axis, dim in sides:
        size, length = (lax.axis_size(axis), array.shape[dim])
        up = [(i, (i + 1) % size) for i in range(size - 1)]
        down = [(j, i) for i, j in up]
        last = lax.slice_in_dim(array, length - width, length, axis=dim)
        leading = lax.slice_in_dim(array, 0, width, axis=dim)
        before = lax.ppermute(last, axis, up)
        after = lax.ppermute(leading, axis, down)
        array = jnp.concatenate([before, array, after], axis=dim)
    return array


def group_silu(values, gain, shift, groups, total_rows):
    chans = values.shape[-1]
    per_group = chans // groups
    grouped = values.reshape(-1, groups, per_group)
    count = float(total_rows * per_group)
    mean = lax.psum(jnp.sum(grouped, axis=(0, 2)), ("tm", "row", "col")) / count
    centred = grouped - mean[None, :, None]
    spread = lax.psum(jnp.sum(centred * centred, axis=(0, 2)), ("tm", "row", "col")) / count
    normed = (grouped - mean[None, :, None]) * lax.rsqrt(spread + 1e-06)[None, :, None]
    normed = normed.reshape(values.shape) * gain + shift
    return jax.nn.silu(normed).astype(jnp.bfloat16)


def conv_taps(padded, weight, frames, rows, cols):
    chans = padded.shape[3]
    total = jnp.zeros((frames * rows * cols, weight.shape[2]), jnp.float32)
    for dt in range(3):
        pieces = []
        for tap in range(9):
            dy, dx = (tap // 3, tap % 3)
            pieces.append(
                padded[dt : dt + frames, dy : dy + rows, dx : dx + cols].reshape(-1, chans)
            )
        stacked = jnp.concatenate(pieces, axis=1)
        flat_weight = weight[9 * dt : 9 * dt + 9].reshape(9 * chans, weight.shape[2])
        total = total + jnp.dot(stacked, flat_weight, preferred_element_type=jnp.float32)
    return total


def time_edge(earlier, volume):
    first_twice = jnp.concatenate([volume[:1], volume[:1]], axis=0)
    earlier = jnp.where(lax.axis_index("tm") == 0, first_twice, earlier)
    return jnp.concatenate([earlier, volume], axis=0)


def edge_rows(padded):
    place = lax.axis_index("row")
    last = lax.axis_size("row") - 1
    top = jnp.where(place == 0, padded[:, 1:2], padded[:, 0:1])
    bottom = jnp.where(place == last, padded[:, -2:-1], padded[:, -1:])
    return jnp.concatenate([top, padded[:, 1:-1], bottom], axis=1)


def edge_cols(padded):
    place = lax.axis_index("col")
    last = lax.axis_size("col") - 1
    left = jnp.where(place == 0, padded[:, :, 1:2], padded[:, :, 0:1])
    right = jnp.where(place == last, padded[:, :, -2:-1], padded[:, :, -1:])
    return jnp.concatenate([left, padded[:, :, 1:-1], right], axis=2)


def per_device(
    features,
    gn1_gain,
    gn1_bias,
    conv1_weight,
    conv1_bias,
    skip_weight,
    gn2_gain,
    gn2_bias,
    conv2_weight,
    conv2_bias,
):
    frames, rows, cols, chans_in = features.shape
    chans_out = conv1_weight.shape[2]
    groups = GROUPS
    nrow = lax.axis_size("row")
    ncol = lax.axis_size("col")
    total_rows = lax.axis_size("tm") * nrow * ncol * frames * rows * cols
    flat_features = features.reshape(-1, chans_in)
    hidden1 = group_silu(features.astype(jnp.float32), gn1_gain, gn1_bias, groups, total_rows)
    earlier = passed_along(hidden1, "tm", 1)
    extended = time_edge(earlier, hidden1)
    padded = with_halo(extended, (("row", 1), ("col", 2)), 1)
    padded = edge_cols(edge_rows(padded))
    window = padded
    first = conv_taps(
        window, lax.all_gather(conv1_weight, ("row", "col"), axis=1, tiled=True), frames, rows, cols
    )
    second = jnp.dot(
        flat_features,
        lax.all_gather(skip_weight, ("row", "col"), axis=1, tiled=True)[0],
        preferred_element_type=jnp.float32,
    )
    middle = (first + conv1_bias).reshape(frames, rows, cols, chans_out)
    hidden2 = group_silu(middle, gn2_gain, gn2_bias, groups, total_rows)
    earlier_mid = passed_along(hidden2, "tm", 1)
    extended_mid = time_edge(earlier_mid, hidden2)
    padded_mid = with_halo(extended_mid, (("row", 1), ("col", 2)), 1)
    padded_mid = edge_cols(edge_rows(padded_mid))
    window = padded_mid
    conv_second = conv_taps(
        window, lax.all_gather(conv2_weight, ("row", "col"), axis=1, tiled=True), frames, rows, cols
    )
    block_out = (second + conv_second + conv2_bias).astype(jnp.bfloat16)
    return block_out.reshape(frames, rows, cols, chans_out)


def solution(mesh):
    in_specs = (
        P("tm", "row", "col", None),
        P(),
        P(),
        P(None, ("row", "col"), None),
        P(),
        P(None, ("row", "col"), None),
        P(),
        P(),
        P(None, ("row", "col"), None),
        P(),
    )
    out_specs = P("tm", "row", "col", None)
    return jax.shard_map(
        per_device, mesh=mesh, in_specs=in_specs, out_specs=out_specs, check_vma=False
    )
```

profile of v0, /device:TPU:1, one launch (start us, length us, event | category | flops | bytes accessed | tf_op | source)
XLA Modules:
  0.0 484.7 jit_solution(6953915214572819488)
XLA Ops:
  6.5 0.7 all-gather.3.cloned.1.call-update
  7.3 1.0 convert_reduce_fusion
  8.3 0.1 reduce_sum.47
  8.4 0.1 reduce_sum.51
  8.5 107.7 %psum.28 = f32[32]{0:T(128)S(1)} all-reduce(f32[32]{0:T(128)S(1)} %reduce_sum.51), channel_id=1, replica_groups=mesh['tm'=32,'row'=8,'col'=2] {'tm','row','col'}, use_global_device_ids=true, to_apply=%region_2.0 | all-reduce | flops 32 | bytes 256 | tf_op jit(solution)/shard_map/psum | solution.py:33
  116.2 0.1 sub.42
  116.3 1.0 fusion.5
  117.4 0.1 reduce_sum.54
  117.5 93.4 %psum.29 = f32[32]{0:T(128)S(1)} all-reduce(f32[32]{0:T(128)S(1)} %reduce_sum.54), channel_id=1, replica_groups=mesh['tm'=32,'row'=8,'col'=2] {'tm','row','col'}, use_global_device_ids=true, to_apply=%region_5.6 | all-reduce | flops 32 | bytes 256 | tf_op jit(solution)/shard_map/psum | solution.py:35
  211.0 0.1 mul.73
  211.1 1.1 fusion.13
  212.2 2.4 collective-permute-start
  214.6 3.5 collective-permute-done
  218.2 2.4 collective-permute-start.1
  220.6 1.3 collective-permute-start.2
  222.0 4.3 collective-permute-done.2
  226.3 0.1 pad_maximum_fusion.25
  226.4 1.3 collective-permute-start.3
  227.7 4.6 collective-permute-start.4
  232.3 0.8 collective-permute-done.4
  233.2 0.5 pad_maximum_fusion
  233.6 0.1 maximum_select_fusion.2
  233.7 0.1 maximum_select_fusion.1
  233.9 0.1 pad_maximum_fusion.1
  234.0 0.2 slice.442
  234.2 0.2 broadcast_select_fusion
  234.4 0.5 pad_maximum_fusion.6
  234.9 0.2 pad_maximum_fusion.5
  235.2 0.6 pad_maximum_fusion.4
  236.2 1.0 copy-done.2
  237.3 0.6 copy-done
  237.9 3.8 fusion.47
  241.8 0.6 fusion.50
  242.4 0.8 copy-done.1
  243.2 0.6 convolution_add_fusion.4
  243.9 0.9 copy-done.3
  244.8 0.6 fusion.49
  245.5 0.1 reduce_sum.72
  245.6 100.0 %psum.30 = f32[32]{0:T(128)S(1)} all-reduce(f32[32]{0:T(128)S(1)} %reduce_sum.72), channel_id=1, replica_groups=mesh['tm'=32,'row'=8,'col'=2] {'tm','row','col'}, use_global_device_ids=true, to_apply=%region_8.9 | all-reduce | flops 32 | bytes 256 | tf_op jit(solution)/shard_map/psum | solution.py:33
  345.7 0.1 sub.46
  345.8 0.1 reduce_sum.74
  345.9 0.1 reduce_sum.75
  346.1 94.4 %psum.31 = f32[32]{0:T(128)S(1)} all-reduce(f32[32]{0:T(128)S(1)} %reduce_sum.75), channel_id=1, replica_groups=mesh['tm'=32,'row'=8,'col'=2] {'tm','row','col'}, use_global_device_ids=true, to_apply=%region_11.12 | all-reduce | flops 32 | bytes 256 | tf_op jit(solution)/shard_map/psum | solution.py:35
  440.5 0.1 mul.81
  440.7 2.7 collective-permute-start.5
  443.5 16.5 %all_gather.9 = bf16[1,512,256]{2,1,0:T(8,128)(2,1)S(1)} all-gather(bf16[1,32,256]{2,1,0:T(8,128)(2,1)S(1)} %copy-done.5), channel_id=1, replica_groups=mesh['tm'=32,'row'=8,'col'=2] {'row','col'}, dimensions={1}, use_global_device_ids=true | all-gather | bytes 278528 | tf_op jit(solution)/shard_map/all_gather | solution.py:109
  460.1 3.0 collective-permute-start.6
  463.0 1.3 collective-permute-start.7
  464.4 2.2 fusion.48
  466.6 1.1 collective-permute-done.7
  467.8 1.3 collective-permute-start.8
  469.1 3.7 collective-permute-start.9
  472.8 0.6 collective-permute-done.9
  473.4 0.2 pad_maximum_fusion.2
  473.8 0.1 pad_maximum_fusion.14
  473.9 0.1 broadcast_select_fusion.2
  474.1 0.1 slice.480
  474.2 0.2 pad_maximum_fusion.15
  474.4 0.3 pad_maximum_fusion.13
  475.2 0.4 fusion.51
  475.6 0.4 convolution_add_fusion.2
  476.1 0.4 convolution_add_fusion.1
  476.5 0.5 copy-done.4
  477.0 0.9 fusion.2
  (105 shorter events, 1.8 us)
Async XLA Ops:
  6.5 231.4 %all-gather.3.cloned.1.call-start = ((), (), s32[]{:S(2)}) async-start(), calls=%async_computation | async-start | bytes 7520256 | tf_op jit(solution)/shard_map/all_gather | solution.py:105
  7.3 457.1 %all-gather.5.cloned.1.call-start = ((), (), s32[]{:S(2)}) async-start(), calls=%async_computation.1 | async-start | bytes 3760128 | tf_op jit(solution)/shard_map/all_gather | solution.py:120
  212.2 6.0 %collective-permute-start = (bf16[2,6,16,512]{3,2,1,0:T(8,128)(2,1)S(1)}, bf16[2,6,16,512]{3,2,1,0:T(8,128)(2,1)S(1)}, u32[]{:S(2)}, u32[]{:S(2)}) collective-permute-start(bf16[2,6,16,512]{3,2,1,0:T(8,128)(2,1)S(1)} %fusion.13), channel_id=1, source_target_pairs={{0,16},{16,32},{32,48},{48,64},{64,80},{80,96},{96,112},{112,128},... | collective-permute-start | bytes 589832 | tf_op jit(solution)/shard_map/ppermute | solution.py:12
  218.2 3.8 collective-permute-start.1
  220.6 5.6 %collective-permute-start.2 = (bf16[4,1,16,512]{3,2,1,0:T(8,128)(2,1)S(1)}, bf16[4,1,16,512]{3,2,1,0:T(8,128)(2,1)S(1)}, u32[]{:S(2)}, u32[]{:S(2)}) collective-permute-start(bf16[4,1,16,512]{3,2,1,0:T(8,128)(2,1)S(1)} %get-tuple-element.45), channel_id=1, source_target_pairs={{2,0},{4,2},{6,4},{8,6},{10,8},{12,10},{14,12},{3,1},{5,3},{7,5},{... | collective-permute-start | bytes 196616 | tf_op jit(solution)/shard_map/ppermute | solution.py:23
  226.4 6.0 %collective-permute-start.3 = (bf16[4,8,1,512]{3,2,1,0:T(2,128)(2,1)S(1)}, bf16[4,8,1,512]{3,2,1,0:T(2,128)(2,1)S(1)}, u32[]{:S(2)}, u32[]{:S(2)}) collective-permute-start(bf16[4,8,1,512]{3,2,1,0:T(2,128)(2,1)S(1)} %get-tuple-element.40), channel_id=1, source_target_pairs={{0,1},{2,3},{4,5},{6,7},{8,9},{10,11},{12,13},{14,15},{16,17},{18,... | collective-permute-start | bytes 98312 | tf_op jit(solution)/shard_map/ppermute | solution.py:22
  227.7 5.5 %collective-permute-start.4 = (bf16[4,8,1,512]{3,2,1,0:T(2,128)(2,1)S(1)}, bf16[4,8,1,512]{3,2,1,0:T(2,128)(2,1)S(1)}, u32[]{:S(2)}, u32[]{:S(2)}) collective-permute-start(bf16[4,8,1,512]{3,2,1,0:T(2,128)(2,1)S(1)} %get-tuple-element.41), channel_id=1, source_target_pairs={{1,0},{3,2},{5,4},{7,6},{9,8},{11,10},{13,12},{15,14},{17,16},{19,... | collective-permute-start | bytes 98312 | tf_op jit(solution)/shard_map/ppermute | solution.py:23
  236.0 1.2 copy-start.2
  236.2 1.7 copy-start
  241.7 1.5 copy-start.1
  243.2 1.5 copy-start.3
  243.2 1.5 copy-start.6
  244.7 195.9 %copy-start.7 = (f32[256]{0:T(256)S(1)}, f32[256]{0:T(256)}, u32[]{:S(2)}) copy-start(f32[256]{0:T(256)} %param.17) | copy-start | bytes 3076
  244.7 195.9 %copy-start.8 = (f32[256]{0:T(256)S(1)}, f32[256]{0:T(256)}, u32[]{:S(2)}) copy-start(f32[256]{0:T(256)} %param.16) | copy-start | bytes 3076
  244.7 198.7 %copy-start.5 = (bf16[1,32,256]{2,1,0:T(8,128)(2,1)S(1)}, bf16[1,32,256]{2,1,0:T(8,128)(2,1)}, u32[]{:S(2)}) copy-start(bf16[1,32,256]{2,1,0:T(8,128)(2,1)} %param.15) | copy-start | bytes 49156
  440.7 19.3 %collective-permute-start.5 = (bf16[2,6,16,256]{3,2,1,0:T(8,128)(2,1)S(1)}, bf16[2,6,16,256]{3,2,1,0:T(8,128)(2,1)S(1)}, u32[]{:S(2)}, u32[]{:S(2)}) collective-permute-start(bf16[2,6,16,256]{3,2,1,0:T(8,128)(2,1)S(1)} %multiply_convert_fusion.1), channel_id=1, source_target_pairs={{0,16},{16,32},{32,48},{48,64},{64,80},{80,96},{96,112},{112,128},... | collective-permute-start | bytes 294920 | tf_op jit(solution)/shard_map/ppermute | solution.py:12
  460.1 6.5 %collective-permute-start.6 = (bf16[4,1,16,256]{3,2,1,0:T(8,128)(2,1)S(1)}, bf16[4,1,16,256]{3,2,1,0:T(8,128)(2,1)S(1)}, u32[]{:S(2)}, u32[]{:S(2)}) collective-permute-start(bf16[4,1,16,256]{3,2,1,0:T(8,128)(2,1)S(1)} %get-tuple-element.75), channel_id=1, source_target_pairs={{0,2},{2,4},{4,6},{6,8},{8,10},{10,12},{12,14},{1,3},{3,5},{5,7},{... | collective-permute-start | bytes 98312 | tf_op jit(solution)/shard_map/ppermute | solution.py:22
  463.0 4.7 collective-permute-start.7
  467.8 5.0 %collective-permute-start.8 = (bf16[4,8,1,256]{3,2,1,0:T(2,128)(2,1)S(1)}, bf16[4,8,1,256]{3,2,1,0:T(2,128)(2,1)S(1)}, u32[]{:S(2)}, u32[]{:S(2)}) collective-permute-start(bf16[4,8,1,256]{3,2,1,0:T(2,128)(2,1)S(1)} %get-tuple-element.73), channel_id=1, source_target_pairs={{0,1},{2,3},{4,5},{6,7},{8,9},{10,11},{12,13},{14,15},{16,17},{18,... | collective-permute-start | bytes 49160 | tf_op jit(solution)/shard_map/ppermute | solution.py:22
  469.1 4.3 collective-permute-start.9
  476.0 0.9 copy-start.4
  476.0 0.9 copy-start.9
Sparse Core Ops, SparseCore 0:
  9.5 58.7 all-gather.2
  222.1 45.9 all-gather.4
where the time goes:
time: 487 us; the launch traced here: 485 us
  blocking collectives  412 us (85%)
  starting transfers between devices  24.1 us (5%)
  between operations  14.3 us (3%)
  local copies, waits for them, and re-layouts  11.7 us (2%)
  waiting for transfers between devices  11.2 us (2%)
  other arithmetic  7.36 us (2%)
    psum x2, blocking collectives, group_silu(): mean = lax.psum(jnp.sum(grouped, axis=(0, 2)), ('tm', 'row', 'col')) / count  208 us
    psum x2, blocking collectives, group_silu(): lax.psum(jnp.sum(centred * centred, axis=(0, 2)), ('tm', 'row', 'col'))  188 us
    all_gather x1, blocking collectives, per_device(): lax.all_gather(skip_weight, ('row', 'col'), axis=1, tiled=True)[0]  16.5 us
    ppermute x4, starting transfers between devices, with_halo(): after = lax.ppermute(leading, axis, down)  10.9 us
  transfers between devices with their start and end apart: 12, of which 5 were waited for; matrix products, arithmetic and copies ran while one was open for 3% of the time, Pallas kernels for 0%

commit v1 on v0

v1 whole, which is shorter than its diff:
```python
import jax
import jax.numpy as jnp
from jax import lax
from jax.sharding import PartitionSpec as P

GROUPS = 32


def moved(block, axis, distance):
    size = lax.axis_size(axis)
    route = [(i, i + distance) for i in range(size) if 0 <= i + distance < size]
    return lax.ppermute(block, axis, route)


def swapped(block, axis):
    return lax.ppermute(block, axis, [(0, 1), (1, 0)])


def spread_to_all(stats, axes, size):
    copies = jnp.broadcast_to(stats[None, None, :], (size, 1, stats.shape[0]))
    return lax.all_to_all(copies, axes, 0, 0, tiled=True)[:, 0]


def merged(parts, count):
    means, squares = parts[:, :GROUPS], parts[:, GROUPS : 2 * GROUPS]
    mean = jnp.mean(means, axis=0)
    off = means - mean[None]
    return mean, jnp.sum(squares, axis=0) + count * jnp.sum(off * off, axis=0)


def local_stats(flat):
    n, c = flat.shape
    per_group = c // GROUPS
    mean = jnp.sum(jnp.sum(flat, axis=0).reshape(GROUPS, per_group), axis=1) / (n * per_group)
    centred = flat - jnp.repeat(mean, per_group)[None]
    squares = jnp.sum(jnp.sum(centred * centred, axis=0).reshape(GROUPS, per_group), axis=1)
    return jnp.concatenate([mean, squares, jnp.zeros((128 - 2 * GROUPS,), jnp.float32)])


def normed_silu(values, mean, squares, total, gain, shift):
    per_group = values.shape[-1] // GROUPS
    scale = lax.rsqrt(squares / total + 1e-06)
    mean, scale = jnp.repeat(mean, per_group), jnp.repeat(scale, per_group)
    normed = (values - mean) * scale * gain + shift
    return jax.nn.silu(normed).astype(jnp.bfloat16)


def conv(padded, weight):
    frames = padded.shape[0] - 2
    weight = weight.reshape(3, 3, 3, *weight.shape[1:])
    total = 0.0
    for dt in range(3):
        total = total + lax.conv_general_dilated(
            padded[dt : dt + frames],
            weight[dt],
            (1, 1),
            "VALID",
            dimension_numbers=("NHWC", "HWIO", "NHWC"),
            preferred_element_type=jnp.float32,
        )
    return total


def per_device(
    features,
    gn1_gain,
    gn1_bias,
    conv1_weight,
    conv1_bias,
    skip_weight,
    gn2_gain,
    gn2_bias,
    conv2_weight,
    conv2_bias,
):
    frames, rows, cols, chans_in = features.shape
    chans_out = conv1_weight.shape[2]
    ntm, nrow, ncol = (lax.axis_size(a) for a in ("tm", "row", "col"))
    tm, row, col = (lax.axis_index(a) for a in ("tm", "row", "col"))
    positions = frames * rows * cols
    plane = nrow * ncol

    first_weight = lax.all_gather(conv1_weight, ("row", "col"), axis=1, tiled=True)
    share = conv2_weight.shape[1]
    halves = skip_weight.reshape(2, share, chans_out)
    later = lax.all_gather(
        jnp.concatenate([conv2_weight, halves], axis=0), ("row", "col"), axis=1, tiled=True
    )
    second_weight = later[:27]
    skip = later[27:].reshape(2, plane, share, chans_out).transpose(1, 0, 2, 3)
    skip = skip.reshape(chans_in, chans_out)

    back_one = moved(features, "tm", 1)
    back_two = moved(features, "tm", 2)
    first_twice = jnp.concatenate([features[:1], features[:1]], axis=0)
    back_one = jnp.where(tm == 0, first_twice, back_one)
    earliest = jnp.concatenate([back_one[:1], back_one[:1]], axis=0)
    back_two = jnp.where(tm <= 1, earliest, back_two)
    volume = jnp.concatenate([back_two, back_one, features], axis=0)

    stats = local_stats(features.reshape(positions, chans_in).astype(jnp.float32))
    count = float(positions * (chans_in // GROUPS))
    mean, squares = merged(spread_to_all(stats, ("row", "col"), plane), count)
    stats = jnp.concatenate([mean, squares, jnp.zeros((128 - 2 * GROUPS,), jnp.float32)])
    mean, squares = merged(spread_to_all(stats, "tm", ntm), count * plane)

    above = moved(volume[:, -2:], "row", 1)
    below = moved(volume[:, :2], "row", -1)
    above = jnp.where(row == 0, volume[:, :1], above)
    below = jnp.where(row == nrow - 1, volume[:, -1:], below)
    volume = jnp.concatenate([above, volume, below], axis=1)
    border = jnp.where(col == 0, volume[:, :, -2:], volume[:, :, :2])
    border = swapped(border, "col")
    left = jnp.where(col == 0, volume[:, :, :1], border)
    right = jnp.where(col == 0, border, volume[:, :, -1:])
    volume = jnp.concatenate([left, volume, right], axis=2)

    hidden1 = normed_silu(
        volume.astype(jnp.float32), mean, squares, count * plane * ntm, gn1_gain, gn1_bias
    )
    middle = conv(hidden1, first_weight) + conv1_bias

    own = middle[2:, 1:-1, 1:-1].reshape(positions, chans_out)
    stats = local_stats(own)
    count = float(positions * (chans_out // GROUPS))
    mean, squares = merged(spread_to_all(stats, ("row", "col"), plane), count)
    stats = jnp.concatenate([mean, squares, jnp.zeros((128 - 2 * GROUPS,), jnp.float32)])
    mean, squares = merged(spread_to_all(stats, "tm", ntm), count * plane)
    hidden2 = normed_silu(middle, mean, squares, count * plane * ntm, gn2_gain, gn2_bias)

    top = jnp.where(row == 0, hidden2[:, 1:2], hidden2[:, :1])
    bottom = jnp.where(row == nrow - 1, hidden2[:, -2:-1], hidden2[:, -1:])
    hidden2 = jnp.concatenate([top, hidden2[:, 1:-1], bottom], axis=1)
    left = jnp.where(col == 0, hidden2[:, :, 1:2], hidden2[:, :, :1])
    right = jnp.where(col == ncol - 1, hidden2[:, :, -2:-1], hidden2[:, :, -1:])
    hidden2 = jnp.concatenate([left, hidden2[:, :, 1:-1], right], axis=2)
    early = jnp.where(tm == 0, hidden2[2:3], hidden2[:2])
    hidden2 = jnp.concatenate([early, hidden2[2:]], axis=0)

    shortcut = jnp.dot(
        features.reshape(positions, chans_in), skip, preferred_element_type=jnp.float32
    )
    second = conv(hidden2, second_weight)
    block_out = shortcut.reshape(second.shape) + second + conv2_bias
    return block_out.astype(jnp.bfloat16)


def solution(mesh):
    in_specs = (
        P("tm", "row", "col", None),
        P(),
        P(),
        P(None, ("row", "col"), None),
        P(),
        P(None, ("row", "col"), None),
        P(),
        P(),
        P(None, ("row", "col"), None),
        P(),
    )
    out_specs = P("tm", "row", "col", None)
    return jax.shard_map(
        per_device, mesh=mesh, in_specs=in_specs, out_specs=out_specs, check_vma=False
    )
```

time: 487 us -> 156 us (0.32)
  blocking collectives: 412 us -> 0 us
  starting transfers between devices: 24.1 us -> 56 us
  waiting for transfers between devices: 11.2 us -> 41.5 us
  other arithmetic: 7.36 us -> 15.7 us
  local copies, waits for them, and re-layouts: 11.7 us -> 19.5 us
    psum x4 -> x0, blocking collectives: 395 us -> none  [the longest x2 208 us: group_silu(): mean = lax.psum(jnp.sum(grouped, axis=(0, 2)), ('tm', 'row', 'col')) / count]
    all_to_all x0 -> x4, starting transfers between devices: none -> 38.3 us  [spread_to_all(): return lax.all_to_all(copies, axes, 0, 0, tiled=True)[:, 0]]
    all_gather x1 -> x0, blocking collectives: 16.5 us -> none  [per_device(): lax.all_gather(skip_weight, ('row', 'col'), axis=1, tiled=True)[0]]
    all_gather x1, waiting for transfers between devices: 0.02 us -> 16.2 us  [per_device(): lax.all_gather(jnp.concatenate([conv2_weight, halves], axis=0), ('row', '...]
    all_to_all x0 -> x4, waiting for transfers between devices: none -> 14.2 us  [spread_to_all(): return lax.all_to_all(copies, axes, 0, 0, tiled=True)[:, 0]]
    conv_general_dilated x0 -> x6, matrix products: none -> 7.57 us  [conv(): lax.conv_general_dilated(padded[dt:dt + frames], weight[dt], (1, 1), 'VAL...]
    ppermute x10 -> x5, starting transfers between devices: 24 us -> 17.6 us  [the longest x4 13.6 us: moved(): return lax.ppermute(block, axis, route)]
    slice x8 -> x13, local copies, waits for them, and re-layouts: 6.39 us -> 9.96 us  [the longest x2 7.26 us: conv(): weight[dt]]
  transfers between devices with their start and end apart: 12 -> 11, of which waited for: 5 -> 6; matrix products, arithmetic and copies ran while one was open for 3% -> 24% of each run, Pallas kernels for 0% -> 0%
where the time goes in v1:
time: 156 us
  starting transfers between devices  56 us (36%)
  waiting for transfers between devices  41.5 us (27%)
  local copies, waits for them, and re-layouts  19.5 us (12%)
  other arithmetic  15.7 us (10%)
  between operations  14.1 us (9%)
  matrix products  8.74 us (6%)
    all_to_all x4, starting transfers between devices, spread_to_all(): return lax.all_to_all(copies, axes, 0, 0, tiled=True)[:, 0]  38.3 us
    all_gather x1, waiting for transfers between devices, per_device(): lax.all_gather(jnp.concatenate([conv2_weight, halves], axis=0), ('row', '...  16.2 us
    all_to_all x4, waiting for transfers between devices, spread_to_all(): return lax.all_to_all(copies, axes, 0, 0, tiled=True)[:, 0]  14.2 us
    ppermute x4, starting transfers between devices, moved(): return lax.ppermute(block, axis, route)  13.6 us
    ppermute x4, waiting for transfers between devices, moved(): return lax.ppermute(block, axis, route)  9.97 us
    conv_general_dilated x6, matrix products, conv(): lax.conv_general_dilated(padded[dt:dt + frames], weight[dt], (1, 1), 'VAL...  7.57 us
    slice x2, local copies, waits for them, and re-layouts, conv(): weight[dt]  7.26 us
    conv_general_dilated x6, other arithmetic, conv(): lax.conv_general_dilated(padded[dt:dt + frames], weight[dt], (1, 1), 'VAL...  4.79 us
  transfers between devices with their start and end apart: 11, of which 6 were waited for; matrix products, arithmetic and copies ran while one was open for 24% of the time, Pallas kernels for 0%

profile of v1, /device:TPU:1, one launch (start us, length us, event | category | flops | bytes accessed | tf_op | source)
XLA Modules:
  0.0 155.6 jit_solution(14918636167085046220)
XLA Ops:
  6.5 0.7 all-gather.5.cloned.1.call-update
  7.3 1.0 convert_reduce_fusion
  8.3 0.1 reduce_sum.181
  8.6 1.0 fusion.39
  9.7 0.1 reduce_sum.183
  9.9 0.6 broadcast_in_dim.108
  10.5 10.1 %all-to-all-start = ((f32[16,1,128]{2,1,0:T(1,128)}), f32[16,1,128]{2,1,0:T(1,128)S(1)}, u32[]{:S(2)}, u32[]{:S(2)}) async-start(f32[16,1,128]{2,1,0:T(1,128)} %broadcast_in_dim.108), calls=%async_computation | async-start | bytes 16384 | tf_op jit(solution)/shard_map/all_to_all | solution.py:21
  20.6 1.1 copy.80
  21.8 4.3 %collective-permute-start.1 = (bf16[2,6,16,512]{3,0,2,1:T(2,128)(2,1)S(1)}, bf16[2,6,16,512]{3,0,2,1:T(2,128)(2,1)S(1)}, u32[]{:S(2)}, u32[]{:S(2)}) collective-permute-start(bf16[2,6,16,512]{3,0,2,1:T(2,128)(2,1)S(1)} %copy.80), channel_id=1, source_target_pairs={{0,32},{16,48},{32,64},{48,80},{64,96},{80,112},{96,128},{112,144}... | collective-permute-start | bytes 589832 | tf_op jit(solution)/shard_map/ppermute | solution.py:12
  26.1 4.0 %collective-permute-start = (bf16[2,6,16,512]{3,0,2,1:T(2,128)(2,1)S(1)}, bf16[2,6,16,512]{3,0,2,1:T(2,128)(2,1)S(1)}, u32[]{:S(2)}, u32[]{:S(2)}) collective-permute-start(bf16[2,6,16,512]{3,0,2,1:T(2,128)(2,1)S(1)} %copy.80), channel_id=1, source_target_pairs={{0,16},{16,32},{32,48},{48,64},{64,80},{80,96},{96,112},{112,128},... | collective-permute-start | bytes 589832 | tf_op jit(solution)/shard_map/ppermute | solution.py:12
  30.3 0.6 broadcast_in_dim.109
  31.0 10.1 %all-to-all-start.1 = ((f32[32,1,128]{2,1,0:T(1,128)}), f32[32,1,128]{2,1,0:T(1,128)S(1)}, u32[]{:S(2)}, u32[]{:S(2)}) async-start(f32[32,1,128]{2,1,0:T(1,128)} %broadcast_in_dim.109), calls=%async_computation.1 | async-start | bytes 32768 | tf_op jit(solution)/shard_map/all_to_all | solution.py:21
  41.2 1.7 %pad_maximum_fusion.4 = bf16[29,16,256]{2,1,0:T(8,128)(2,1)} fusion(bf16[2,16,256]{2,1,0:T(8,128)(2,1)} %bitcast.137, bf16[27,16,256]{2,1,0:T(8,128)(2,1)} %param.18), kind=kLoop, calls=%fused_computation.61 | loop fusion | flops 118784 | bytes 475136 | tf_op jit(solution)/shard_map/concatenate | solution.py:87
  42.9 6.8 %all-to-all-done.1 = f32[32,1,128]{2,1,0:T(1,128)S(1)} async-done(((f32[32,1,128]{2,1,0:T(1,128)}), f32[32,1,128]{2,1,0:T(1,128)S(1)}, u32[]{:S(2)}, u32[]{:S(2)}) %all-to-all-start.1) | async-done | bytes 16416 | tf_op jit(solution)/shard_map/all_to_all | solution.py:21
  49.8 0.5 broadcast_select_fusion
  50.3 0.5 broadcast_select_fusion.1
  50.8 0.2 pad_maximum_fusion.3
  51.1 1.3 collective-permute-start.3
  52.4 0.6 pad_maximum_fusion
  53.0 4.0 %collective-permute-start.2 = (bf16[6,2,16,512]{3,0,2,1:T(8,128)(2,1)S(1)}, bf16[6,2,16,512]{3,0,2,1:T(8,128)(2,1)S(1)}, u32[]{:S(2)}, u32[]{:S(2)}) collective-permute-start(bf16[6,2,16,512]{3,0,2,1:T(8,128)(2,1)S(1)} %slice.203), channel_id=1, source_target_pairs={{0,2},{2,4},{4,6},{6,8},{8,10},{10,12},{12,14},{1,3},{3,5},{5,7},{... | collective-permute-start | bytes 589832 | tf_op jit(solution)/shard_map/ppermute | solution.py:12
  57.1 0.2 maximum_bitcast_fusion.1
  57.3 8.6 %collective-permute-done.3 = bf16[6,2,16,512]{3,0,2,1:T(8,128)(2,1)S(1)} collective-permute-done((bf16[6,2,16,512]{3,0,2,1:T(8,128)(2,1)S(1)}, bf16[6,2,16,512]{3,0,2,1:T(8,128)(2,1)S(1)}, u32[]{:S(2)}, u32[]{:S(2)}) %collective-permute-start.3) | collective-permute-done | bytes 196640 | tf_op jit(solution)/shard_map/ppermute | solution.py:12
  65.9 1.4 collective-permute-done.2
  67.3 0.2 maximum_select_fusion
  67.5 4.0 %collective-permute-start.4 = (bf16[6,10,2,512]{3,0,2,1:T(8,128)(2,1)S(1)}, bf16[6,10,2,512]{3,0,2,1:T(8,128)(2,1)S(1)}, u32[]{:S(2)}, u32[]{:S(2)}) collective-permute-start(bf16[6,10,2,512]{3,0,2,1:T(8,128)(2,1)S(1)} %maximum_select_fusion), channel_id=1, source_target_pairs={{0,1},{1,0},{2,3},{3,2},{4,5},{5,4},{6,7},{7,6},{8,9},{9,8},{10,11... | collective-permute-start | bytes 368648 | tf_op jit(solution)/shard_map/ppermute | solution.py:16
  71.9 0.4 collective-permute-done.4
  72.4 1.8 %multiply_convert_fusion = bf16[6,10,20,512]{3,0,2,1:T(8,128)(2,1)S(1)} fusion(bf16[6,10,2,512]{3,0,2,1:T(8,128)(2,1)S(1)} %get-tuple-element.34, bf16[6,2,16,512]{3,0,2,1:T(8,128)(2,1)S(1)} %broadcast_select_fusion.2, bf16[2,6,16,512]{3,0,2,1:T(2,128)(2,1)S(1)} %copy.80, bf16[2,6,16,512]{3,0,2,1:T(2,128)(2,1)S(1)} %broadcast_select_fusion, ...), kind=kLoop, calls=%fused_computation.4 | loop fusion | flops 14131200 | bytes 2465792 | tf_op jit(solution)/shard_map/convert_element_type | solution.py:45
  74.2 1.3 slice_bitcast_fusion.2
  75.5 0.4 pad
  75.9 0.2 slice.209
  76.1 0.4 pad.4
  76.6 0.2 slice.215
  76.8 0.4 pad.2
  77.2 0.2 slice.212
  77.4 0.8 fusion.3
  78.2 1.9 %fusion.5 = bf16[10,4,8,5,512]{4,1,3,2,0:T(4,128)(2,1)} fusion(bf16[10,4,7,2,512]{4,1,3,2,0:T(4,128)(2,1)S(1)} %slice.215, bf16[10,4,8,3,512]{4,1,3,2,0:T(4,128)(2,1)S(1)} %bitcast.108), kind=kLoop, calls=%fused_computation.7 | loop fusion | flops 4915200 | bytes 3194880 | tf_op jit(solution)/shard_map/conv_general_dilated | solution.py:53
  80.1 2.0 %fusion.4 = bf16[10,4,8,5,512]{4,1,3,2,0:T(4,128)(2,1)} fusion(bf16[10,4,7,2,512]{4,1,3,2,0:T(4,128)(2,1)S(1)} %slice.212, bf16[10,4,8,3,512]{4,1,3,2,0:T(4,128)(2,1)S(1)} %bitcast.110), kind=kLoop, calls=%fused_computation.6 | loop fusion | flops 4915200 | bytes 3194880 | tf_op jit(solution)/shard_map/conv_general_dilated | solution.py:53
  82.2 4.0 %fusion.54 = (bf16[9,512,256]{2,1,0:T(8,128)(2,1)S(1)}, bf16[9,512,256]{2,1,0:T(8,128)(2,1)S(1)}, bf16[9,512,256]{2,1,0:T(8,128)(2,1)S(1)}) fusion(bf16[27,512,256]{2,1,0:T(8,128)(2,1)} %all-gather.5.cloned.1.call-done), kind=kLoop, calls=%fused_computation.114 | loop fusion | bytes 14155776 | tf_op jit(solution)/shard_map/slice | solution.py:55
  86.1 2.0 %fusion.30 = f32[8,32,3,256]{3,1,2,0:T(8,128)S(1)} fusion(bf16[3,3,512,256]{3,2,1,0:T(8,128)(2,1)S(1)} %bitcast.116, bf16[10,4,8,5,512]{4,1,3,2,0:T(4,128)(2,1)S(1)} %copy-done.1, pred[32,3]{0,1:T(4,128)(4,1)S(1)} %copy-done.9), kind=kOutput, calls=%fused_computation.22 | convolution fusion | flops 1812135936 | bytes 4784224 | tf_op jit(solution)/shard_map/conv_general_dilated | solution.py:53
  88.2 2.0 %fusion.27 = f32[8,32,3,256]{3,1,2,0:T(8,128)S(1)} fusion(bf16[3,3,512,256]{3,2,1,0:T(8,128)(2,1)S(1)} %bitcast.115, bf16[10,4,8,5,512]{4,1,3,2,0:T(4,128)(2,1)S(1)} %copy-done.2, pred[32,3]{0,1:T(4,128)(4,1)S(1)} %copy-done.9), kind=kOutput, calls=%fused_computation.21 | convolution fusion | flops 1812135936 | bytes 4784224 | tf_op jit(solution)/shard_map/conv_general_dilated | solution.py:53
  90.2 2.0 %fusion.24 = f32[8,32,3,256]{3,1,2,0:T(8,128)S(1)} fusion(f32[8,32,3,256]{3,1,2,0:T(8,128)S(1)} %fusion.30, f32[8,32,3,256]{3,1,2,0:T(8,128)S(1)} %fusion.27, bf16[3,3,512,256]{3,2,1,0:T(8,128)(2,1)S(1)} %bitcast.114, bf16[10,4,8,5,512]{4,1,3,2,0:T(4,128)(2,1)S(1)} %fusion.3, f32[256]{0:T(256)S(1)} %copy-done.7, pred[32,3]{0,1:T(4,128)(4,1)S(1)} %copy-done.9), kind=kOutput, calls=%fused_computation.20 | convolution fusion | flops 1812725760 | bytes 6358112 | tf_op jit(solution)/shard_map/conv_general_dilated | solution.py:53
  92.2 0.5 copy.87
  92.9 0.1 reduce_sum.191
  93.4 0.1 reduce_sum.193
  93.6 0.6 broadcast_in_dim.113
  94.2 7.6 %all-to-all-start.2 = ((f32[16,1,128]{2,1,0:T(1,128)}), f32[16,1,128]{2,1,0:T(1,128)S(1)}, u32[]{:S(2)}, u32[]{:S(2)}) async-start(f32[16,1,128]{2,1,0:T(1,128)} %broadcast_in_dim.113), calls=%async_computation.2 | async-start | bytes 16384 | tf_op jit(solution)/shard_map/all_to_all | solution.py:21
  101.8 16.2 %all-gather.3.cloned.1.call-done = bf16[29,256,256]{2,1,0:T(8,128)(2,1)} async-done(((bf16[29,16,256]{2,1,0:T(8,128)(2,1)}), bf16[29,256,256]{2,1,0:T(8,128)(2,1)}) %all-gather.3.cloned.1.call-update) | async-done | bytes 3801104 | tf_op jit(solution)/shard_map/all_gather | solution.py:86
  118.0 3.3 %fusion.55 = (bf16[9,256,256]{2,1,0:T(8,128)(2,1)S(1)}, bf16[9,256,256]{2,1,0:T(8,128)(2,1)}, bf16[9,256,256]{2,1,0:T(8,128)(2,1)S(1)}) fusion(bf16[29,256,256]{2,1,0:T(8,128)(2,1)} %all-gather.3.cloned.1.call-done), kind=kLoop, calls=%fused_computation.115 | loop fusion | bytes 7077888 | tf_op jit(solution)/shard_map/slice | solution.py:55
  121.3 0.7 copy.79
  122.2 0.6 broadcast_in_dim.114
  122.8 10.5 %all-to-all-start.3 = ((f32[32,1,128]{2,1,0:T(1,128)}), f32[32,1,128]{2,1,0:T(1,128)S(1)}, u32[]{:S(2)}, u32[]{:S(2)}) async-start(f32[32,1,128]{2,1,0:T(1,128)} %broadcast_in_dim.114), calls=%async_computation.3 | async-start | bytes 32768 | tf_op jit(solution)/shard_map/all_to_all | solution.py:21
  133.3 1.2 fusion.56
  134.5 7.4 %all-to-all-done.3 = f32[32,1,128]{2,1,0:T(1,128)S(1)} async-done(((f32[32,1,128]{2,1,0:T(1,128)}), f32[32,1,128]{2,1,0:T(1,128)S(1)}, u32[]{:S(2)}, u32[]{:S(2)}) %all-to-all-start.3) | async-done | bytes 16416 | tf_op jit(solution)/shard_map/all_to_all | solution.py:21
  142.4 1.0 multiply_convert_fusion.1
  143.6 0.3 copy.89
  143.8 0.2 reshape.133
  144.4 0.2 pad_maximum_fusion.2
  145.2 0.9 copy-done.3
  146.1 0.5 convolution_select_fusion
  146.6 0.5 convolution_select_fusion.1
  147.1 0.5 fusion.34
  147.7 0.2 copy.97
  147.9 0.1 reshape.137
  148.1 0.6 copy.99
  (103 shorter events, 3.5 us)
Async XLA Ops:
  6.5 75.6 %all-gather.5.cloned.1.call-start = ((), (), s32[]{:S(2)}) async-start(), calls=%async_computation.5 | async-start | bytes 7520256 | tf_op jit(solution)/shard_map/all_gather | solution.py:83
  10.5 19.6 %all-to-all-start = ((f32[16,1,128]{2,1,0:T(1,128)}), f32[16,1,128]{2,1,0:T(1,128)S(1)}, u32[]{:S(2)}, u32[]{:S(2)}) async-start(f32[16,1,128]{2,1,0:T(1,128)} %broadcast_in_dim.108), calls=%async_computation | async-start | bytes 16384 | tf_op jit(solution)/shard_map/all_to_all | solution.py:21
  21.8 28.5 %collective-permute-start.1 = (bf16[2,6,16,512]{3,0,2,1:T(2,128)(2,1)S(1)}, bf16[2,6,16,512]{3,0,2,1:T(2,128)(2,1)S(1)}, u32[]{:S(2)}, u32[]{:S(2)}) collective-permute-start(bf16[2,6,16,512]{3,0,2,1:T(2,128)(2,1)S(1)} %copy.80), channel_id=1, source_target_pairs={{0,32},{16,48},{32,64},{48,80},{64,96},{80,112},{96,128},{112,144}... | collective-permute-start | bytes 589832 | tf_op jit(solution)/shard_map/ppermute | solution.py:12
  26.1 23.7 %collective-permute-start = (bf16[2,6,16,512]{3,0,2,1:T(2,128)(2,1)S(1)}, bf16[2,6,16,512]{3,0,2,1:T(2,128)(2,1)S(1)}, u32[]{:S(2)}, u32[]{:S(2)}) collective-permute-start(bf16[2,6,16,512]{3,0,2,1:T(2,128)(2,1)S(1)} %copy.80), channel_id=1, source_target_pairs={{0,16},{16,32},{32,48},{48,64},{64,80},{80,96},{96,112},{112,128},... | collective-permute-start | bytes 589832 | tf_op jit(solution)/shard_map/ppermute | solution.py:12
  31.0 18.7 %all-to-all-start.1 = ((f32[32,1,128]{2,1,0:T(1,128)}), f32[32,1,128]{2,1,0:T(1,128)S(1)}, u32[]{:S(2)}, u32[]{:S(2)}) async-start(f32[32,1,128]{2,1,0:T(1,128)} %broadcast_in_dim.109), calls=%async_computation.1 | async-start | bytes 32768 | tf_op jit(solution)/shard_map/all_to_all | solution.py:21
  41.1 76.9 %all-gather.3.cloned.1.call-start = ((), (), s32[]{:S(2)}) async-start(), calls=%async_computation.4 | async-start | bytes 4038656 | tf_op jit(solution)/shard_map/all_gather | solution.py:86
  51.1 14.8 %collective-permute-start.3 = (bf16[6,2,16,512]{3,0,2,1:T(8,128)(2,1)S(1)}, bf16[6,2,16,512]{3,0,2,1:T(8,128)(2,1)S(1)}, u32[]{:S(2)}, u32[]{:S(2)}) collective-permute-start(bf16[6,2,16,512]{3,0,2,1:T(8,128)(2,1)S(1)} %pad_maximum_fusion.3), channel_id=1, source_target_pairs={{2,0},{4,2},{6,4},{8,6},{10,8},{12,10},{14,12},{3,1},{5,3},{7,5},{... | collective-permute-start | bytes 589832 | tf_op jit(solution)/shard_map/ppermute | solution.py:12
  53.0 14.3 %collective-permute-start.2 = (bf16[6,2,16,512]{3,0,2,1:T(8,128)(2,1)S(1)}, bf16[6,2,16,512]{3,0,2,1:T(8,128)(2,1)S(1)}, u32[]{:S(2)}, u32[]{:S(2)}) collective-permute-start(bf16[6,2,16,512]{3,0,2,1:T(8,128)(2,1)S(1)} %slice.203), channel_id=1, source_target_pairs={{0,2},{2,4},{4,6},{6,8},{8,10},{10,12},{12,14},{1,3},{3,5},{5,7},{... | collective-permute-start | bytes 589832 | tf_op jit(solution)/shard_map/ppermute | solution.py:12
  57.3 15.1 %copy-start.4 = (f32[512]{0:T(512)S(1)}, f32[512]{0:T(512)}, u32[]{:S(2)}) copy-start(f32[512]{0:T(512)} %param.12) | copy-start | bytes 6148
  57.3 15.1 %copy-start.5 = (f32[512]{0:T(512)S(1)}, f32[512]{0:T(512)}, u32[]{:S(2)}) copy-start(f32[512]{0:T(512)} %param.11) | copy-start | bytes 6148
  67.5 4.8 %collective-permute-start.4 = (bf16[6,10,2,512]{3,0,2,1:T(8,128)(2,1)S(1)}, bf16[6,10,2,512]{3,0,2,1:T(8,128)(2,1)S(1)}, u32[]{:S(2)}, u32[]{:S(2)}) collective-permute-start(bf16[6,10,2,512]{3,0,2,1:T(8,128)(2,1)S(1)} %maximum_select_fusion), channel_id=1, source_target_pairs={{0,1},{1,0},{2,3},{3,2},{4,5},{5,4},{6,7},{7,6},{8,9},{9,8},{10,11... | collective-permute-start | bytes 368648 | tf_op jit(solution)/shard_map/ppermute | solution.py:16
  82.1 4.0 %copy-start.9 = (pred[32,3]{0,1:T(4,128)(4,1)S(1)}, pred[32,3]{0,1:T(4,128)(4,1)}, u32[]{:S(2)}) copy-start(pred[32,3]{0,1:T(4,128)(4,1)} %constant.82) | copy-start | bytes 292
  82.2 4.0 %copy-start.1 = (bf16[10,4,8,5,512]{4,1,3,2,0:T(4,128)(2,1)S(1)}, bf16[10,4,8,5,512]{4,1,3,2,0:T(4,128)(2,1)}, u32[]{:S(2)}) copy-start(bf16[10,4,8,5,512]{4,1,3,2,0:T(4,128)(2,1)} %fusion.5) | copy-start | bytes 4915204
  86.1 2.0 %copy-start.2 = (bf16[10,4,8,5,512]{4,1,3,2,0:T(4,128)(2,1)S(1)}, bf16[10,4,8,5,512]{4,1,3,2,0:T(4,128)(2,1)}, u32[]{:S(2)}) copy-start(bf16[10,4,8,5,512]{4,1,3,2,0:T(4,128)(2,1)} %fusion.4) | copy-start | bytes 4915204
  88.2 2.0 %copy-start.7 = (f32[256]{0:T(256)S(1)}, f32[256]{0:T(256)}, u32[]{:S(2)}) copy-start(f32[256]{0:T(256)} %param.14) | copy-start | bytes 3076
  94.2 27.8 %all-to-all-start.2 = ((f32[16,1,128]{2,1,0:T(1,128)}), f32[16,1,128]{2,1,0:T(1,128)S(1)}, u32[]{:S(2)}, u32[]{:S(2)}) async-start(f32[16,1,128]{2,1,0:T(1,128)} %broadcast_in_dim.113), calls=%async_computation.2 | async-start | bytes 16384 | tf_op jit(solution)/shard_map/all_to_all | solution.py:21
  101.8 31.6 %copy-start = (bf16[2,6,16,512]{3,2,1,0:T(8,128)(2,1)S(1)}, bf16[2,6,16,512]{3,2,1,0:T(8,128)(2,1)}, u32[]{:S(2)}) copy-start(bf16[2,6,16,512]{3,2,1,0:T(8,128)(2,1)} %param.10) | copy-start | bytes 589828
  118.0 3.3 %slice-start = ((bf16[29,256,256]{2,1,0:T(8,128)(2,1)}), bf16[2,256,256]{2,1,0:T(8,128)(2,1)S(1)}, s32[]{:S(2)}) async-start(bf16[29,256,256]{2,1,0:T(8,128)(2,1)} %all-gather.3.cloned.1.call-done), calls=%async_computation.6 | async-start | bytes 524288 | tf_op jit(solution)/shard_map/slice | solution.py:90
  122.8 19.0 %all-to-all-start.3 = ((f32[32,1,128]{2,1,0:T(1,128)}), f32[32,1,128]{2,1,0:T(1,128)S(1)}, u32[]{:S(2)}, u32[]{:S(2)}) async-start(f32[32,1,128]{2,1,0:T(1,128)} %broadcast_in_dim.114), calls=%async_computation.3 | async-start | bytes 32768 | tf_op jit(solution)/shard_map/all_to_all | solution.py:21
  144.8 1.3 copy-start.3
  144.8 1.3 copy-start.8
  147.1 0.9 copy-start.6
Sparse Core Ops, SparseCore 0:
  9.5 62.1 all-gather.4
  73.8 44.0 all-gather.2

commit v2 on v1

v2 whole, which is shorter than its diff:
```python
import functools

import jax
import jax.numpy as jnp
from jax import lax
from jax.experimental import pallas as pl
from jax.experimental.pallas import tpu as pltpu
from jax.sharding import PartitionSpec as P

GROUPS = 32
MIB = 1024 * 1024
VMEM = pltpu.VMEM
SMEM = pltpu.SMEM


def moved(block, axis, distance):
    size = lax.axis_size(axis)
    route = [(i, i + distance) for i in range(size) if 0 <= i + distance < size]
    return lax.ppermute(block, axis, route)


def swapped(block, axis):
    return lax.ppermute(block, axis, [(0, 1), (1, 0)])


def as_rows(row):
    return jnp.concatenate([row[:, 128 * j : 128 * (j + 1)] for j in range(row.shape[1] // 128)], axis=0)


def as_row(rows):
    return jnp.concatenate([rows[j : j + 1] for j in range(rows.shape[0])], axis=1)


def packed(mean, squares):
    half = 4
    mean, squares = as_rows(mean), as_rows(squares)
    if mean.shape[0] < half:
        blank = jnp.zeros((half - mean.shape[0], 128), jnp.float32)
        mean = jnp.concatenate([mean, blank], axis=0)
        squares = jnp.concatenate([squares, blank], axis=0)
    return jnp.concatenate([mean, squares], axis=0)


def merged(parts_ref, count):
    parts = parts_ref[...]
    total = jnp.sum(parts, axis=0)
    mean = total / parts.shape[0]
    off = parts - mean[None]
    between = jnp.sum(off * off, axis=0)
    return jnp.concatenate([mean[:4], total[4:] + count * between[:4]], axis=0)


def group_average(rows, size):
    lane = lax.broadcasted_iota(jnp.int32, rows.shape, 1)
    step = 1
    while step < size:
        up, down = pltpu.roll(rows, 128 - step, 1), pltpu.roll(rows, step, 1)
        rows = rows + jnp.where((lane & step) == 0, up, down)
        step *= 2
    return rows / size


def group_moments(tile, count, size, chans):
    mean, squares = tile[:4], tile[4:]
    centre = group_average(mean, size)
    off = mean - centre
    variance = group_average(squares / count + off * off, size)
    scale = lax.rsqrt(variance + 1e-06)
    k = chans // 128
    return as_row(centre[:k]), as_row(scale[:k])


def silu_of(values, mean, scale, gain, shift):
    return jax.nn.silu((values - mean) * scale * gain + shift)


def channel_stats(values, keep, count):
    if keep is not None:
        mean = jnp.sum(jnp.where(keep, values, 0.0), axis=0, keepdims=True) / count
        off = jnp.where(keep, values - mean, 0.0)
    else:
        mean = jnp.sum(values, axis=0, keepdims=True) / count
        off = values - mean
    return packed(mean, jnp.sum(off * off, axis=0, keepdims=True))


def stats_kernel(x_ref, out_ref):
    values = x_ref[...].astype(jnp.float32)
    tile = channel_stats(values, None, float(values.shape[0]))
    out_ref[...] = jnp.broadcast_to(tile[None], out_ref.shape)


def merge_kernel(count, parts_ref, out_ref):
    out_ref[...] = jnp.broadcast_to(merged(parts_ref, count)[None], out_ref.shape)


def hidden1_kernel(
    count, peers, place_ref, parts_ref, gain_ref, shift_ref, centre_ref, above_ref, below_ref, border_ref, out_ref, plain, side
):
    chans = centre_ref.shape[-1]
    tile = merged(parts_ref, count)
    mean, scale = group_moments(tile, count * peers, chans // GROUPS, chans)
    gain, shift = gain_ref[...], shift_ref[...]
    row, col = place_ref[0], place_ref[1]

    def normed(block):
        return silu_of(block.astype(jnp.float32), mean, scale, gain, shift)

    def put(y, block):
        for j in range(chans // 128):
            plain[j, 16 * y : 16 * y + 16, :] = block[:, 128 * j : 128 * (j + 1)]

    def frame(t, _):
        own = [normed(centre_ref[t, y]) for y in range(6)]
        for y in range(2):
            put(y, jnp.where(row == 0, own[0], normed(above_ref[t, y])))
            put(y + 8, jnp.where(row == 7, own[5], normed(below_ref[t, y])))
        for y in range(6):
            put(y + 2, own[y])
        for x in range(2):
            side[pl.ds(16 * x, 16), :] = normed(border_ref[t, x])
        for dy in range(3):

            def column(x):
                pieces = [plain[j, pl.ds(16 * dy + x, 8, stride=16), :] for j in range(chans // 128)]
                return jnp.concatenate(pieces, axis=1)

            inner = [column(x) for x in range(16)]
            outer = [side[pl.ds(16 * x + dy, 8), :] for x in range(2)]
            left = [jnp.where(col == 0, inner[0], o) for o in outer]
            right = [jnp.where(col == 0, o, inner[15]) for o in outer]
            columns = left + inner + right
            base = pl.multiple_of(t * 160, 16)
            for p in range(2):
                for i in range(10 - p):
                    pair = jnp.concatenate([columns[2 * i + p], columns[2 * i + p + 1]], axis=0)
                    out_ref[2 * dy + p, pl.ds(base + 16 * i, 16), :] = pair.astype(jnp.bfloat16)
            out_ref[2 * dy + 1, pl.ds(base + 144, 16), :] = jnp.zeros((16, chans), jnp.bfloat16)
        return 0

    lax.fori_loop(0, 6, frame, 0)


def conv1_kernel(count, copies_ref, weight_ref, bias_ref, middle_ref, stats_ref):
    dy, dt = pl.program_id(0), pl.program_id(1)

    @pl.when((dy == 0) & (dt == 0))
    def _():
        middle_ref[...] = jnp.broadcast_to(bias_ref[...], middle_ref.shape)

    def window(t, dx):
        start = pl.multiple_of((dt + t) * 160 + (dx // 2) * 16, 16)
        return copies_ref[dx % 2, pl.ds(start, 144), :]

    taps = [jnp.concatenate([window(t, dx) for t in range(4)], axis=0) for dx in range(3)]
    lhs = jnp.concatenate(taps, axis=1)
    weight = weight_ref[...].reshape(lhs.shape[1], weight_ref.shape[2])
    middle_ref[...] += jnp.dot(lhs, weight, preferred_element_type=jnp.float32)

    @pl.when((dy == 2) & (dt == 2))
    def _():
        values = middle_ref[288:, :]
        place = lax.broadcasted_iota(jnp.int32, values.shape, 0)
        y, x = place % 8, (place // 8) % 18
        keep = (y >= 1) & (y <= 6) & (x >= 1) & (x <= 16)
        tile = channel_stats(values, keep, count)
        stats_ref[...] = jnp.broadcast_to(tile[None], stats_ref.shape)


def conv2_kernel(
    count, peers, place_ref, parts_ref, gain_ref, shift_ref, bias_ref, middle_ref, features_ref, weight_ref, skip_a_ref, skip_b_ref,
    out_ref, copies, total
):
    dt = pl.program_id(0)
    chans = middle_ref.shape[1]

    @pl.when(dt == 0)
    def _():
        row, col, tm = place_ref[0], place_ref[1], place_ref[2]
        tile = merged(parts_ref, count)
        mean, scale = group_moments(tile, count * peers, chans // GROUPS, chans)
        gain, shift = gain_ref[...], shift_ref[...]
        y = lax.broadcasted_iota(jnp.int32, (8, chans), 0)
        for t in range(4):
            source = jnp.where((tm == 0) & (t < 2), 2, t) if t < 2 else t
            block = middle_ref[pl.ds(pl.multiple_of(source * 144, 16), 144), :]
            block = silu_of(block, mean, scale, gain, shift)
            columns = [block[8 * x : 8 * x + 8] for x in range(18)]
            columns[0] = jnp.where(col == 0, columns[1], columns[0])
            columns[17] = jnp.where(col == 1, columns[16], columns[17])
            for x in range(18):
                column = columns[x]
                column = jnp.where((y == 0) & (row == 0), pltpu.roll(column, 7, 0), column)
                columns[x] = jnp.where((y == 7) & (row == 7), pltpu.roll(column, 1, 0), column)
            for dy in range(3):
                turned = columns if dy == 0 else [pltpu.roll(c, 8 - dy, 0) for c in columns]
                for p in range(2):
                    for i in range(9 - p):
                        pair = jnp.concatenate([turned[2 * i + p], turned[2 * i + p + 1]], axis=0)
                        copies[2 * dy + p, pl.ds(144 * t + 16 * i, 16), :] = pair.astype(jnp.bfloat16)

    def window(t, dy, dx):
        start = pl.multiple_of((dt + t) * 144 + (dx // 2) * 16, 16)
        return copies[2 * dy + dx % 2, pl.ds(start, 128), :]

    sums = None
    for dy in range(3):
        taps = [jnp.concatenate([window(t, dy, dx) for t in range(2)], axis=0) for dx in range(3)]
        lhs = jnp.concatenate(taps, axis=1)
        weight = weight_ref[3 * dy : 3 * dy + 3].reshape(lhs.shape[1], chans)
        product = jnp.dot(lhs, weight, preferred_element_type=jnp.float32)
        sums = product if sums is None else sums + product

    halves = [sums[:, 128 * j : 128 * (j + 1)] for j in range(chans // 128)]

    @pl.when(dt == 0)
    def _():
        for j, half in enumerate(halves):
            total[j] = half

    @pl.when(dt > 0)
    def _():
        for j, half in enumerate(halves):
            total[j] += half

    @pl.when(dt == 2)
    def _():
        pieces = []
        for d in range(skip_a_ref.shape[1] // 16):
            pieces += [skip_a_ref[0, 16 * d : 16 * d + 16], skip_b_ref[0, 16 * d : 16 * d + 16]]
        skip = jnp.concatenate(pieces, axis=0)
        shortcut = jnp.dot(features_ref[...], skip, preferred_element_type=jnp.float32) + bias_ref[...]
        for t in range(2):
            for y in range(6):
                conv = [total[j, pl.ds(128 * t + y, 16, stride=8), :] for j in range(chans // 128)]
                conv = jnp.concatenate(conv, axis=1)
                at = (6 * t + y) * 16
                out_ref[pl.ds(at, 16), :] = (conv + shortcut[at : at + 16]).astype(jnp.bfloat16)


def whole(*_):
    return pl.BlockSpec(memory_space=VMEM)


def per_device(
    features,
    gn1_gain,
    gn1_bias,
    conv1_weight,
    conv1_bias,
    skip_weight,
    gn2_gain,
    gn2_bias,
    conv2_weight,
    conv2_bias,
):
    frames, rows, cols, chans_in = features.shape
    chans_out = conv1_weight.shape[2]
    ntm, nrow, ncol = (lax.axis_size(a) for a in ("tm", "row", "col"))
    tm, row, col = (lax.axis_index(a) for a in ("tm", "row", "col"))
    place = jnp.stack([row, col, tm]).astype(jnp.int32)
    positions = frames * rows * cols
    plane = nrow * ncol
    flat_features = features.reshape(positions, chans_in)
    tile = jax.ShapeDtypeStruct((8, 128), jnp.float32)

    first_weight = lax.all_gather(conv1_weight, ("row", "col"), axis=1, tiled=True)
    share = conv2_weight.shape[1]
    halves = skip_weight.reshape(2, share, chans_out)
    later = lax.all_gather(
        jnp.concatenate([conv2_weight, halves], axis=0), ("row", "col"), axis=1, tiled=True
    )

    def shared(stats, count):
        stats = lax.all_to_all(stats, ("row", "col"), 0, 0, tiled=True)
        stats = pl.pallas_call(
            functools.partial(merge_kernel, count),
            out_shape=jax.ShapeDtypeStruct((ntm, *tile.shape), tile.dtype),
            in_specs=[whole()],
            out_specs=whole(),
        )(stats)
        return lax.all_to_all(stats, "tm", 0, 0, tiled=True)

    stats = pl.pallas_call(
        stats_kernel,
        out_shape=jax.ShapeDtypeStruct((plane, *tile.shape), tile.dtype),
        in_specs=[whole()],
        out_specs=whole(),
    )(flat_features)
    parts = shared(stats, float(positions))

    back_one = moved(features, "tm", 1)
    back_two = moved(features, "tm", 2)
    first_twice = jnp.concatenate([features[:1], features[:1]], axis=0)
    back_one = jnp.where(tm == 0, first_twice, back_one)
    earliest = jnp.concatenate([back_one[:1], back_one[:1]], axis=0)
    back_two = jnp.where(tm <= 1, earliest, back_two)
    volume = jnp.concatenate([back_two, back_one, features], axis=0)

    above = moved(volume[:, -2:], "row", 1)
    below = moved(volume[:, :2], "row", -1)
    edge = [jnp.where(col == 0, part[:, :, -2:], part[:, :, :2]) for part in (above, volume, below)]
    edge[0] = jnp.where(row == 0, edge[1][:, :1], edge[0])
    edge[2] = jnp.where(row == nrow - 1, edge[1][:, -1:], edge[2])
    border = jnp.concatenate(edge, axis=1).transpose(0, 2, 1, 3)
    border = jnp.pad(border, ((0, 0), (0, 0), (0, 16 - border.shape[2]), (0, 0)))
    border = swapped(border, "col")

    copies = pl.pallas_call(
        functools.partial(hidden1_kernel, float(positions * plane), ntm),
        out_shape=jax.ShapeDtypeStruct((6, 960, chans_in), jnp.bfloat16),
        in_specs=[pl.BlockSpec(memory_space=SMEM)] + [whole()] * 7,
        out_specs=whole(),
        scratch_shapes=[VMEM((chans_in // 128, 160, 128), jnp.float32), VMEM((32, chans_in), jnp.float32)],
        compiler_params=pltpu.CompilerParams(vmem_limit_bytes=24 * MIB),
    )(place, parts, gn1_gain[None], gn1_bias[None], volume, above, below, border)

    middle, stats = pl.pallas_call(
        functools.partial(conv1_kernel, float(positions)),
        grid=(3, 3),
        out_shape=(
            jax.ShapeDtypeStruct((576, chans_out), jnp.float32),
            jax.ShapeDtypeStruct((plane, *tile.shape), tile.dtype),
        ),
        in_specs=[
            pl.BlockSpec((2, 960, chans_in), lambda dy, dt: (dy, 0, 0)),
            pl.BlockSpec((3, chans_in, chans_out), lambda dy, dt: (3 * dt + dy, 0, 0)),
            pl.BlockSpec((1, chans_out), lambda dy, dt: (0, 0)),
        ],
        out_specs=(
            pl.BlockSpec((576, chans_out), lambda dy, dt: (0, 0)),
            pl.BlockSpec((plane, 8, 128), lambda dy, dt: (0, 0, 0)),
        ),
        compiler_params=pltpu.CompilerParams(vmem_limit_bytes=32 * MIB),
    )(copies, first_weight, conv1_bias[None])

    parts = shared(stats, float(positions))

    out = pl.pallas_call(
        functools.partial(conv2_kernel, float(positions * plane), ntm),
        grid=(3,),
        out_shape=jax.ShapeDtypeStruct((positions, chans_out), jnp.bfloat16),
        in_specs=[
            pl.BlockSpec(memory_space=SMEM),
            pl.BlockSpec((ntm, 8, 128), lambda dt: (0, 0, 0)),
            pl.BlockSpec((1, chans_out), lambda dt: (0, 0)),
            pl.BlockSpec((1, chans_out), lambda dt: (0, 0)),
            pl.BlockSpec((1, chans_out), lambda dt: (0, 0)),
            pl.BlockSpec((576, chans_out), lambda dt: (0, 0)),
            pl.BlockSpec((positions, chans_in), lambda dt: (0, 0)),
            pl.BlockSpec((9, chans_out, chans_out), lambda dt: (dt, 0, 0)),
            pl.BlockSpec((1, chans_out, chans_out), lambda dt: (27, 0, 0)),
            pl.BlockSpec((1, chans_out, chans_out), lambda dt: (28, 0, 0)),
        ],
        out_specs=pl.BlockSpec((positions, chans_out), lambda dt: (0, 0)),
        scratch_shapes=[
            VMEM((6, 576, chans_out), jnp.bfloat16),
            VMEM((chans_out // 128, 256, 128), jnp.float32),
        ],
        compiler_params=pltpu.CompilerParams(vmem_limit_bytes=24 * MIB),
    )(place, parts, gn2_gain[None], gn2_bias[None], conv2_bias[None], middle, flat_features, later, later, later)
    return out.reshape(frames, rows, cols, chans_out)


def solution(mesh):
    in_specs = (
        P("tm", "row", "col", None),
        P(),
        P(),
        P(None, ("row", "col"), None),
        P(),
        P(None, ("row", "col"), None),
        P(),
        P(),
        P(None, ("row", "col"), None),
        P(),
    )
    out_specs = P("tm", "row", "col", None)
    return jax.shard_map(
        per_device, mesh=mesh, in_specs=in_specs, out_specs=out_specs, check_vma=False
    )
```

time: 156 us -> 134 us (0.86)
  Pallas kernels: 0 us -> 18 us
  waiting for transfers between devices: 41.5 us -> 24 us
  other arithmetic: 15.7 us -> 2.24 us
  blocking collectives: 0 us -> 13.1 us
  matrix products: 8.74 us -> 0 us
  local copies, waits for them, and re-layouts: 19.5 us -> 12.7 us
  starting transfers between devices: 56 us -> 50.1 us
    pallas_call x0 -> x6, Pallas kernels: none -> 18 us  [the longest x1 6.01 us: per_device(): pl.pallas_call(functools.partial(conv1_kernel, float(positions)), grid=(3...]
    all_to_all x0 -> x1, blocking collectives: none -> 13.1 us  [shared(): stats = lax.all_to_all(stats, ('row', 'col'), 0, 0, tiled=True)]
    all_gather x1, waiting for transfers between devices: 16.2 us -> 5.87 us  [per_device(): lax.all_gather(jnp.concatenate([conv2_weight, halves], axis=0), ('row', '...]
    unnamed x24 -> x26, local copies, waits for them, and re-layouts: 2.24 us -> 12.1 us
    slice x13 -> x4, local copies, waits for them, and re-layouts: 9.96 us -> 0.37 us  [the longest x1 0.32 us: per_device(): below = moved(volume[:, :2], 'row', -1)]
    all_to_all x4 -> x3, waiting for transfers between devices: 14.2 us -> 5.32 us  [the longest x2 3.29 us: shared(): return lax.all_to_all(stats, 'tm', 0, 0, tiled=True)]
    conv_general_dilated x6 -> x0, matrix products: 7.57 us -> none  [conv(): lax.conv_general_dilated(padded[dt:dt + frames], weight[dt], (1, 1), 'VAL...]
    all_to_all x4 -> x3, starting transfers between devices: 38.3 us -> 33 us  [the longest x2 24.9 us: shared(): return lax.all_to_all(stats, 'tm', 0, 0, tiled=True)]
  transfers between devices with their start and end apart: 11 -> 10, of which waited for: 6 -> 6; matrix products, arithmetic and copies ran while one was open for 24% -> 3% of each run, Pallas kernels for 0% -> 11%
where the time goes in v2:
time: 134 us
  starting transfers between devices  50.1 us (37%)
  waiting for transfers between devices  24 us (18%)
  Pallas kernels  18 us (13%)
  between operations  13.7 us (10%)
  blocking collectives  13.1 us (10%)
  local copies, waits for them, and re-layouts  12.7 us (9%)
  other arithmetic  2.24 us (2%)
    all_to_all x2, starting transfers between devices, shared(): return lax.all_to_all(stats, 'tm', 0, 0, tiled=True)  24.9 us
    ppermute x4, starting transfers between devices, moved(): return lax.ppermute(block, axis, route)  13.9 us
    all_to_all x1, blocking collectives, shared(): stats = lax.all_to_all(stats, ('row', 'col'), 0, 0, tiled=True)  13.1 us
    unnamed x26, local copies, waits for them, and re-layouts  12.1 us
    ppermute x4, waiting for transfers between devices, moved(): return lax.ppermute(block, axis, route)  11.3 us
    all_to_all x1, starting transfers between devices, shared(): stats = lax.all_to_all(stats, ('row', 'col'), 0, 0, tiled=True)  8.07 us
    pallas_call x1, Pallas kernels, per_device(): pl.pallas_call(functools.partial(conv1_kernel, float(positions)), grid=(3...  6.01 us
    all_gather x1, waiting for transfers between devices, per_device(): lax.all_gather(jnp.concatenate([conv2_weight, halves], axis=0), ('row', '...  5.87 us
  transfers between devices with their start and end apart: 10, of which 6 were waited for; matrix products, arithmetic and copies ran while one was open for 3% of the time, Pallas kernels for 11%

profile of v2, /device:TPU:1, one launch (start us, length us, event | category | flops | bytes accessed | tf_op | source)
XLA Modules:
  0.0 133.7 jit_solution(11554070829211317309)
XLA Ops:
  6.5 0.0 copy-start.5
  6.5 0.0 copy-start.6
  6.5 0.0 all-gather.3.cloned.1.call-start
  6.5 0.7 all-gather.3.cloned.1.call-update
  7.3 0.0 all-gather.5.cloned.1.call-start
  7.3 1.7 %pad_maximum_fusion.1 = bf16[29,16,256]{2,1,0:T(8,128)(2,1)} fusion(bf16[2,16,256]{2,1,0:T(8,128)(2,1)} %bitcast.26, bf16[27,16,256]{2,1,0:T(8,128)(2,1)} %param.18), kind=kLoop, calls=%fused_computation.3 | loop fusion | flops 118784 | bytes 475136 | tf_op jit(solution)/shard_map/concatenate | solution.py:271
  9.0 0.0 all-gather.5.cloned.1.call-update
  9.0 1.0 copy.18
  10.0 4.8 %collective-permute-start = (bf16[2,6,16,512]{3,1,2,0:T(8,128)(2,1)S(1)}, bf16[2,6,16,512]{3,1,2,0:T(8,128)(2,1)S(1)}, u32[]{:S(2)}, u32[]{:S(2)}) collective-permute-start(bf16[2,6,16,512]{3,1,2,0:T(8,128)(2,1)S(1)} %copy.18), channel_id=1, source_target_pairs={{0,16},{16,32},{32,48},{48,64},{64,80},{80,96},{96,112},{112,128},... | collective-permute-start | bytes 589832 | tf_op jit(solution)/shard_map/ppermute | solution.py:19
  14.9 1.7 %shard_map.100 = f32[16,8,128]{2,1,0:T(8,128)} custom-call(bf16[192,512]{1,0:T(8,128)(2,1)} %bitcast.18), custom_call_target="tpu_custom_call" | custom-call | tf_op jit(solution)/shard_map/pallas_call | solution.py:284
  16.6 8.1 %all-to-all-start = ((f32[16,8,128]{2,1,0:T(8,128)}), f32[16,8,128]{2,1,0:T(8,128)S(1)}, u32[]{:S(2)}, u32[]{:S(2)}) async-start(f32[16,8,128]{2,1,0:T(8,128)} %shard_map.100), calls=%async_computation | async-start | bytes 131072 | tf_op jit(solution)/shard_map/all_to_all | solution.py:275
  24.6 5.8 %collective-permute-start.1 = (bf16[2,6,16,512]{3,1,2,0:T(8,128)(2,1)S(1)}, bf16[2,6,16,512]{3,1,2,0:T(8,128)(2,1)S(1)}, u32[]{:S(2)}, u32[]{:S(2)}) collective-permute-start(bf16[2,6,16,512]{3,1,2,0:T(8,128)(2,1)S(1)} %copy.18), channel_id=1, source_target_pairs={{0,32},{16,48},{32,64},{48,80},{64,96},{80,112},{96,128},{112,144}... | collective-permute-start | bytes 589832 | tf_op jit(solution)/shard_map/ppermute | solution.py:19
  30.5 2.0 %all-to-all-done.parts_ref = f32[16,8,128]{2,1,0:T(8,128)S(1)} async-done(((f32[16,8,128]{2,1,0:T(8,128)}), f32[16,8,128]{2,1,0:T(8,128)S(1)}, u32[]{:S(2)}, u32[]{:S(2)}) %all-to-all-start) | async-done | bytes 65568 | tf_op jit(solution)/shard_map/all_to_all | solution.py:275
  32.5 0.0 copy-start.11
  32.5 0.6 copy-done.11
  33.2 1.5 %shard_map.101 = f32[32,8,128]{2,1,0:T(8,128)} custom-call(f32[16,8,128]{2,1,0:T(8,128)} %copy-done.11), custom_call_target="tpu_custom_call" | custom-call | tf_op jit(solution)/shard_map/pallas_call | solution.py:276
  34.7 12.5 %all-to-all-start.1 = ((f32[32,8,128]{2,1,0:T(8,128)}), f32[32,8,128]{2,1,0:T(8,128)S(1)}, u32[]{:S(2)}, u32[]{:S(2)}) async-start(f32[32,8,128]{2,1,0:T(8,128)} %shard_map.101), calls=%async_computation.1 | async-start | bytes 262144 | tf_op jit(solution)/shard_map/all_to_all | solution.py:282
  47.2 0.0 collective-permute-done
  47.2 0.1 maximum_select_fusion
  47.3 0.0 collective-permute-done.1
  47.3 0.1 maximum_select_fusion.1
  47.4 0.2 pad_maximum_fusion
  47.6 0.0 copy-start.7
  47.6 0.3 fusion
  47.9 1.9 %collective-permute-start.2 = (bf16[6,2,16,512]{3,1,2,0:T(2,128)(2,1)S(1)}, bf16[6,2,16,512]{3,1,2,0:T(2,128)(2,1)S(1)}, u32[]{:S(2)}, u32[]{:S(2)}) collective-permute-start(bf16[6,2,16,512]{3,1,2,0:T(2,128)(2,1)S(1)} %get-tuple-element.10), channel_id=1, source_target_pairs={{0,2},{2,4},{4,6},{6,8},{8,10},{10,12},{12,14},{1,3},{3,5},{5,7},{... | collective-permute-start | bytes 589832 | tf_op jit(solution)/shard_map/ppermute | solution.py:19
  49.8 1.3 collective-permute-start.3
  51.2 6.8 %collective-permute-done.2 = bf16[6,2,16,512]{3,1,2,0:T(2,128)(2,1)S(1)} collective-permute-done((bf16[6,2,16,512]{3,1,2,0:T(2,128)(2,1)S(1)}, bf16[6,2,16,512]{3,1,2,0:T(2,128)(2,1)S(1)}, u32[]{:S(2)}, u32[]{:S(2)}) %collective-permute-start.2) | collective-permute-done | bytes 196640 | tf_op jit(solution)/shard_map/ppermute | solution.py:19
  58.1 4.5 %collective-permute-done.3 = bf16[6,2,16,512]{3,1,2,0:T(2,128)(2,1)S(1)} collective-permute-done((bf16[6,2,16,512]{3,1,2,0:T(2,128)(2,1)S(1)}, bf16[6,2,16,512]{3,1,2,0:T(2,128)(2,1)S(1)}, u32[]{:S(2)}, u32[]{:S(2)}) %collective-permute-start.3) | collective-permute-done | bytes 196640 | tf_op jit(solution)/shard_map/ppermute | solution.py:19
  62.6 0.1 maximum_bitcast_fusion
  62.8 3.2 %collective-permute-start.4 = (bf16[6,2,16,512]{3,2,1,0:T(8,128)(2,1)S(1)}, bf16[6,2,16,512]{3,2,1,0:T(8,128)(2,1)S(1)}, u32[]{:S(2)}, u32[]{:S(2)}) collective-permute-start(bf16[6,2,16,512]{3,2,1,0:T(8,128)(2,1)S(1)} %pad.4), channel_id=1, source_target_pairs={{0,1},{1,0},{2,3},{3,2},{4,5},{5,4},{6,7},{7,6},{8,9},{9,8},{10,11... | collective-permute-start | bytes 589832 | tf_op jit(solution)/shard_map/ppermute | solution.py:23
  66.0 0.1 pad_add_fusion.place_ref
  66.1 0.2 copy.22.centre_ref
  66.3 0.0 all-to-all-done.1.parts_ref
  66.3 0.7 collective-permute-done.4.border_ref
  67.0 0.0 copy-done.5
  67.1 0.0 copy-done.6
  67.1 3.5 %shard_map.102.copies_ref = bf16[6,960,512]{2,1,0:T(8,128)(2,1)S(1)} custom-call(s32[3]{0:T(128)S(1)} %pad_add_fusion.place_ref, f32[32,8,128]{2,1,0:T(8,128)S(1)} %all-to-all-done.1.parts_ref, f32[1,512]{1,0:T(1,128)S(1)} %bitcast.20, f32[1,512]{1,0:T(1,128)S(1)} %bitcast.21, bf16[6,6,16,512]{3,2,1,0:T(8,128)(2,1)S(1)} %copy.22.centre_ref, ...), custom_call_target="tpu_custom_call" | custom-call | tf_op jit(solution)/shard_map/pallas_call | solution.py:309
  70.6 0.0 copy-start.1
  70.6 2.6 %copy-done.1 = bf16[6,960,512]{2,1,0:T(8,128)(2,1)} copy-done((bf16[6,960,512]{2,1,0:T(8,128)(2,1)}, bf16[6,960,512]{2,1,0:T(8,128)(2,1)S(1)}, u32[]{:S(2)}) %copy-start.1) | copy-done | bytes 5898264
  73.1 0.0 all-gather.3.cloned.1.call-done.weight_ref
  73.1 0.0 copy-done.7
  73.1 0.0 copy-start.2
  73.1 2.7 %copy-done.2 = bf16[6,960,512]{2,1,0:T(8,128)(2,1)S(1)} copy-done((bf16[6,960,512]{2,1,0:T(8,128)(2,1)S(1)}, bf16[6,960,512]{2,1,0:T(8,128)(2,1)}, u32[]{:S(2)}) %copy-start.2) | copy-done | bytes 5898264
  75.8 0.0 copy-start.3
  75.8 3.0 %copy-done.3 = bf16[27,512,256]{2,1,0:T(8,128)(2,1)S(1)} copy-done((bf16[27,512,256]{2,1,0:T(8,128)(2,1)S(1)}, bf16[27,512,256]{2,1,0:T(8,128)(2,1)}, u32[]{:S(2)}) %copy-start.3) | copy-done | bytes 7077912
  78.8 0.0 copy-start.4
  78.8 0.0 copy-start.8
  78.8 0.0 copy-start.9
  78.8 0.0 copy-start.10
  78.8 6.0 %shard_map.103 = (f32[576,256]{1,0:T(8,128)S(1)}, f32[16,8,128]{2,1,0:T(8,128)S(1)}) custom-call(bf16[6,960,512]{2,1,0:T(8,128)(2,1)S(1)} %copy-done.2, bf16[27,512,256]{2,1,0:T(8,128)(2,1)S(1)} %copy-done.3, f32[1,256]{1,0:T(1,128)S(1)} %bitcast.22), custom_call_target="tpu_custom_call" | custom-call | tf_op jit(solution)/shard_map/pallas_call | solution.py:318
  84.9 13.1 %all_to_all.20.parts_ref = f32[16,8,128]{2,1,0:T(8,128)} all-to-all(f32[16,8,128]{2,1,0:T(8,128)S(1)} %get-tuple-element.7), channel_id=1, replica_groups=mesh['tm'=32,'row'=8,'col'=2] {'row','col'}, dimensions={0} | all-to-all | bytes 131072 | tf_op jit(solution)/shard_map/all_to_all | solution.py:275
  97.9 1.5 %shard_map.104 = f32[32,8,128]{2,1,0:T(8,128)} custom-call(f32[16,8,128]{2,1,0:T(8,128)} %all_to_all.20.parts_ref), custom_call_target="tpu_custom_call" | custom-call | tf_op jit(solution)/shard_map/pallas_call | solution.py:276
  99.5 12.4 %all-to-all-start.3 = ((f32[32,8,128]{2,1,0:T(8,128)}), f32[32,8,128]{2,1,0:T(8,128)S(1)}, u32[]{:S(2)}, u32[]{:S(2)}) async-start(f32[32,8,128]{2,1,0:T(8,128)} %shard_map.104), calls=%async_computation.3 | async-start | bytes 262144 | tf_op jit(solution)/shard_map/all_to_all | solution.py:282
  111.9 5.9 %all-gather.5.cloned.1.call-done.weight_ref.skip_a_ref.skip_b_ref = bf16[29,256,256]{2,1,0:T(8,128)(2,1)} async-done(((bf16[29,16,256]{2,1,0:T(8,128)(2,1)}), bf16[29,256,256]{2,1,0:T(8,128)(2,1)}) %all-gather.5.cloned.1.call-update) | async-done | bytes 3801104 | tf_op jit(solution)/shard_map/all_gather | solution.py:270
  117.8 3.3 %all-to-all-done.3.parts_ref = f32[32,8,128]{2,1,0:T(8,128)S(1)} async-done(((f32[32,8,128]{2,1,0:T(8,128)}), f32[32,8,128]{2,1,0:T(8,128)S(1)}, u32[]{:S(2)}, u32[]{:S(2)}) %all-to-all-start.3) | async-done | bytes 131104 | tf_op jit(solution)/shard_map/all_to_all | solution.py:282
  121.0 0.0 copy-done.4
  121.0 0.0 copy-done.8
  121.0 0.0 copy-done.9
  121.1 0.0 copy-done.10
  121.1 0.0 copy-start
  121.1 2.1 %copy-done = bf16[29,256,256]{2,1,0:T(8,128)(2,1)S(1)} copy-done((bf16[29,256,256]{2,1,0:T(8,128)(2,1)S(1)}, bf16[29,256,256]{2,1,0:T(8,128)(2,1)}, u32[]{:S(2)}) %copy-start) | copy-done | bytes 3801112
  123.1 3.8 %shard_map.105 = bf16[192,256]{1,0:T(8,128)(2,1)} custom-call(s32[3]{0:T(128)S(1)} %pad_add_fusion.place_ref, f32[32,8,128]{2,1,0:T(8,128)S(1)} %all-to-all-done.3.parts_ref, f32[1,256]{1,0:T(1,128)S(1)} %bitcast.23, f32[1,256]{1,0:T(1,128)S(1)} %bitcast.24, f32[1,256]{1,0:T(1,128)S(1)} %bitcast.25, f32[576,256]{1,0:T(8,128)S(1)} %get-tuple-element.8.middle_ref, ...), custom_call_target="tpu_custom_call" | custom-call | tf_op jit(solution)/shard_map/pallas_call | solution.py:339
  (10 shorter events, 0.2 us)
Async XLA Ops:
  6.5 60.5 %copy-start.5 = (f32[512]{0:T(512)S(1)}, f32[512]{0:T(512)}, u32[]{:S(2)}) copy-start(f32[512]{0:T(512)} %param.11) | copy-start | bytes 6148
  6.5 60.5 %copy-start.6 = (f32[512]{0:T(512)S(1)}, f32[512]{0:T(512)}, u32[]{:S(2)}) copy-start(f32[512]{0:T(512)} %param.12) | copy-start | bytes 6148
  6.5 66.6 %all-gather.3.cloned.1.call-start = ((), (), s32[]{:S(2)}) async-start(), calls=%async_computation.4 | async-start | bytes 7520256 | tf_op jit(solution)/shard_map/all_gather | solution.py:267
  7.3 110.5 %all-gather.5.cloned.1.call-start = ((), (), s32[]{:S(2)}) async-start(), calls=%async_computation.5 | async-start | bytes 4038656 | tf_op jit(solution)/shard_map/all_gather | solution.py:270
  10.0 37.2 %collective-permute-start = (bf16[2,6,16,512]{3,1,2,0:T(8,128)(2,1)S(1)}, bf16[2,6,16,512]{3,1,2,0:T(8,128)(2,1)S(1)}, u32[]{:S(2)}, u32[]{:S(2)}) collective-permute-start(bf16[2,6,16,512]{3,1,2,0:T(8,128)(2,1)S(1)} %copy.18), channel_id=1, source_target_pairs={{0,16},{16,32},{32,48},{48,64},{64,80},{80,96},{96,112},{112,128},... | collective-permute-start | bytes 589832 | tf_op jit(solution)/shard_map/ppermute | solution.py:19
  16.6 16.0 %all-to-all-start = ((f32[16,8,128]{2,1,0:T(8,128)}), f32[16,8,128]{2,1,0:T(8,128)S(1)}, u32[]{:S(2)}, u32[]{:S(2)}) async-start(f32[16,8,128]{2,1,0:T(8,128)} %shard_map.100), calls=%async_computation | async-start | bytes 131072 | tf_op jit(solution)/shard_map/all_to_all | solution.py:275
  24.6 22.7 %collective-permute-start.1 = (bf16[2,6,16,512]{3,1,2,0:T(8,128)(2,1)S(1)}, bf16[2,6,16,512]{3,1,2,0:T(8,128)(2,1)S(1)}, u32[]{:S(2)}, u32[]{:S(2)}) collective-permute-start(bf16[2,6,16,512]{3,1,2,0:T(8,128)(2,1)S(1)} %copy.18), channel_id=1, source_target_pairs={{0,32},{16,48},{32,64},{48,80},{64,96},{80,112},{96,128},{112,144}... | collective-permute-start | bytes 589832 | tf_op jit(solution)/shard_map/ppermute | solution.py:19
  32.5 0.6 copy-start.11
  34.7 31.6 %all-to-all-start.1 = ((f32[32,8,128]{2,1,0:T(8,128)}), f32[32,8,128]{2,1,0:T(8,128)S(1)}, u32[]{:S(2)}, u32[]{:S(2)}) async-start(f32[32,8,128]{2,1,0:T(8,128)} %shard_map.101), calls=%async_computation.1 | async-start | bytes 262144 | tf_op jit(solution)/shard_map/all_to_all | solution.py:282
  47.6 25.6 %copy-start.7 = (f32[256]{0:T(256)S(1)}, f32[256]{0:T(256)}, u32[]{:S(2)}) copy-start(f32[256]{0:T(256)} %param.14) | copy-start | bytes 3076
  47.9 10.2 %collective-permute-start.2 = (bf16[6,2,16,512]{3,1,2,0:T(2,128)(2,1)S(1)}, bf16[6,2,16,512]{3,1,2,0:T(2,128)(2,1)S(1)}, u32[]{:S(2)}, u32[]{:S(2)}) collective-permute-start(bf16[6,2,16,512]{3,1,2,0:T(2,128)(2,1)S(1)} %get-tuple-element.10), channel_id=1, source_target_pairs={{0,2},{2,4},{4,6},{6,8},{8,10},{10,12},{12,14},{1,3},{3,5},{5,7},{... | collective-permute-start | bytes 589832 | tf_op jit(solution)/shard_map/ppermute | solution.py:19
  49.8 12.8 %collective-permute-start.3 = (bf16[6,2,16,512]{3,1,2,0:T(2,128)(2,1)S(1)}, bf16[6,2,16,512]{3,1,2,0:T(2,128)(2,1)S(1)}, u32[]{:S(2)}, u32[]{:S(2)}) collective-permute-start(bf16[6,2,16,512]{3,1,2,0:T(2,128)(2,1)S(1)} %get-tuple-element.9), channel_id=1, source_target_pairs={{2,0},{4,2},{6,4},{8,6},{10,8},{12,10},{14,12},{3,1},{5,3},{7,5},{... | collective-permute-start | bytes 589832 | tf_op jit(solution)/shard_map/ppermute | solution.py:19
  62.8 4.3 %collective-permute-start.4 = (bf16[6,2,16,512]{3,2,1,0:T(8,128)(2,1)S(1)}, bf16[6,2,16,512]{3,2,1,0:T(8,128)(2,1)S(1)}, u32[]{:S(2)}, u32[]{:S(2)}) collective-permute-start(bf16[6,2,16,512]{3,2,1,0:T(8,128)(2,1)S(1)} %pad.4), channel_id=1, source_target_pairs={{0,1},{1,0},{2,3},{3,2},{4,5},{5,4},{6,7},{7,6},{8,9},{9,8},{10,11... | collective-permute-start | bytes 589832 | tf_op jit(solution)/shard_map/ppermute | solution.py:23
  70.6 2.6 %copy-start.1 = (bf16[6,960,512]{2,1,0:T(8,128)(2,1)}, bf16[6,960,512]{2,1,0:T(8,128)(2,1)S(1)}, u32[]{:S(2)}) copy-start(bf16[6,960,512]{2,1,0:T(8,128)(2,1)S(1)} %shard_map.102.copies_ref) | copy-start | bytes 17694724
  73.1 2.7 %copy-start.2 = (bf16[6,960,512]{2,1,0:T(8,128)(2,1)S(1)}, bf16[6,960,512]{2,1,0:T(8,128)(2,1)}, u32[]{:S(2)}) copy-start(bf16[6,960,512]{2,1,0:T(8,128)(2,1)} %copy-done.1) | copy-start | bytes 17694724
  75.8 3.0 %copy-start.3 = (bf16[27,512,256]{2,1,0:T(8,128)(2,1)S(1)}, bf16[27,512,256]{2,1,0:T(8,128)(2,1)}, u32[]{:S(2)}) copy-start(bf16[27,512,256]{2,1,0:T(8,128)(2,1)} %all-gather.3.cloned.1.call-done.weight_ref) | copy-start | bytes 21233668
  78.8 42.2 %copy-start.4 = (bf16[2,6,16,512]{3,2,1,0:T(8,128)(2,1)S(1)}, bf16[2,6,16,512]{3,2,1,0:T(8,128)(2,1)}, u32[]{:S(2)}) copy-start(bf16[2,6,16,512]{3,2,1,0:T(8,128)(2,1)} %param.10) | copy-start | bytes 589828
  78.8 42.2 %copy-start.8 = (f32[256]{0:T(256)S(1)}, f32[256]{0:T(256)}, u32[]{:S(2)}) copy-start(f32[256]{0:T(256)} %param.16) | copy-start | bytes 3076
  78.8 42.2 %copy-start.9 = (f32[256]{0:T(256)S(1)}, f32[256]{0:T(256)}, u32[]{:S(2)}) copy-start(f32[256]{0:T(256)} %param.17) | copy-start | bytes 3076
  78.8 42.2 %copy-start.10 = (f32[256]{0:T(256)S(1)}, f32[256]{0:T(256)}, u32[]{:S(2)}) copy-start(f32[256]{0:T(256)} %param.19) | copy-start | bytes 3076
  99.5 21.6 %all-to-all-start.3 = ((f32[32,8,128]{2,1,0:T(8,128)}), f32[32,8,128]{2,1,0:T(8,128)S(1)}, u32[]{:S(2)}, u32[]{:S(2)}) async-start(f32[32,8,128]{2,1,0:T(8,128)} %shard_map.104), calls=%async_computation.3 | async-start | bytes 262144 | tf_op jit(solution)/shard_map/all_to_all | solution.py:282
  121.1 2.1 %copy-start = (bf16[29,256,256]{2,1,0:T(8,128)(2,1)S(1)}, bf16[29,256,256]{2,1,0:T(8,128)(2,1)}, u32[]{:S(2)}) copy-start(bf16[29,256,256]{2,1,0:T(8,128)(2,1)} %all-gather.5.cloned.1.call-done.weight_ref.skip_a_ref.skip_b_ref) | copy-start | bytes 11403268
Sparse Core Ops, SparseCore 0:
  9.5 61.5 all-gather.2
  73.2 44.4 all-gather.4

commit v3 on v2

v3 whole, which is shorter than its diff:
```python
import functools

import jax
import jax.numpy as jnp
from jax import lax
from jax.experimental import pallas as pl
from jax.experimental.pallas import tpu as pltpu
from jax.sharding import Mesh
from jax.sharding import PartitionSpec as P

GROUPS = 32
TM = ("x", "z")
MIB = 1024 * 1024
VMEM = pltpu.VMEM
SMEM = pltpu.SMEM
HBM = pltpu.HBM


def moved(block, axis, distance):
    size = lax.axis_size(axis)
    route = [(i, i + distance) for i in range(size) if 0 <= i + distance < size]
    return lax.ppermute(block, axis, route)


def swapped(block, axis):
    return lax.ppermute(block, axis, [(0, 1), (1, 0)])


def as_rows(row):
    return jnp.concatenate([row[:, 128 * j : 128 * (j + 1)] for j in range(row.shape[1] // 128)], axis=0)


def as_row(rows):
    return jnp.concatenate([rows[j : j + 1] for j in range(rows.shape[0])], axis=1)


def packed(mean, squares):
    half = 4
    mean, squares = as_rows(mean), as_rows(squares)
    if mean.shape[0] < half:
        blank = jnp.zeros((half - mean.shape[0], 128), jnp.float32)
        mean = jnp.concatenate([mean, blank], axis=0)
        squares = jnp.concatenate([squares, blank], axis=0)
    return jnp.concatenate([mean, squares], axis=0)


def merged(parts_ref, count):
    parts = parts_ref[...]
    total = jnp.sum(parts, axis=0)
    mean = total / parts.shape[0]
    off = parts - mean[None]
    between = jnp.sum(off * off, axis=0)
    return jnp.concatenate([mean[:4], total[4:] + count * between[:4]], axis=0)


def group_average(rows, size):
    lane = lax.broadcasted_iota(jnp.int32, rows.shape, 1)
    step = 1
    while step < size:
        up, down = pltpu.roll(rows, 128 - step, 1), pltpu.roll(rows, step, 1)
        rows = rows + jnp.where((lane & step) == 0, up, down)
        step *= 2
    return rows / size


def group_moments(tile, count, size, chans):
    mean, squares = tile[:4], tile[4:]
    centre = group_average(mean, size)
    off = mean - centre
    variance = group_average(squares / count + off * off, size)
    scale = lax.rsqrt(variance + 1e-06)
    k = chans // 128
    return as_row(centre[:k]), as_row(scale[:k])


def silu_of(values, mean, scale, gain, shift):
    return jax.nn.silu((values - mean) * scale * gain + shift)


def channel_stats(values, keep, count):
    if keep is not None:
        mean = jnp.sum(jnp.where(keep, values, 0.0), axis=0, keepdims=True) / count
        off = jnp.where(keep, values - mean, 0.0)
    else:
        mean = jnp.sum(values, axis=0, keepdims=True) / count
        off = values - mean
    return packed(mean, jnp.sum(off * off, axis=0, keepdims=True))


def stats_kernel(x_ref, out_ref):
    values = x_ref[...].astype(jnp.float32)
    tile = channel_stats(values, None, float(values.shape[0]))
    out_ref[...] = jnp.broadcast_to(tile[None], out_ref.shape)


def merge_kernel(count, parts_ref, out_ref):
    out_ref[...] = jnp.broadcast_to(merged(parts_ref, count)[None], out_ref.shape)


def border_kernel(place_ref, centre_ref, above_ref, below_ref, out_ref, plain):
    row, col = place_ref[0], place_ref[1]
    pieces = plain.shape[0]

    def put(y, block):
        block = block.astype(jnp.float32)
        for j in range(pieces):
            plain[j, 16 * y : 16 * y + 16, :] = block[:, 128 * j : 128 * (j + 1)]

    plain[...] = jnp.zeros_like(plain)

    def frame(t, _):
        for y in range(2):
            put(y, jnp.where(row == 0, centre_ref[t, 0], above_ref[t, y]))
            put(y + 8, jnp.where(row == 7, centre_ref[t, 5], below_ref[t, y]))
        for y in range(6):
            put(y + 2, centre_ref[t, y])

        def column(x):
            return jnp.concatenate([plain[j, pl.ds(x, 16, stride=16), :] for j in range(pieces)], axis=1)

        for x in range(2):
            out_ref[t, x] = jnp.where(col == 0, column(14 + x), column(x)).astype(jnp.bfloat16)
        return 0

    lax.fori_loop(0, 6, frame, 0)


def hidden1_kernel(
    count, peers, place_ref, parts_ref, gain_ref, shift_ref, centre_ref, above_ref, below_ref, border_ref, out_ref, plain, side
):
    chans = centre_ref.shape[-1]
    tile = merged(parts_ref, count)
    mean, scale = group_moments(tile, count * peers, chans // GROUPS, chans)
    gain, shift = gain_ref[...], shift_ref[...]
    row, col = place_ref[0], place_ref[1]

    def normed(block):
        return silu_of(block.astype(jnp.float32), mean, scale, gain, shift)

    def put(y, block):
        for j in range(chans // 128):
            plain[j, 16 * y : 16 * y + 16, :] = block[:, 128 * j : 128 * (j + 1)]

    def frame(t, _):
        own = [normed(centre_ref[t, y]) for y in range(6)]
        for y in range(2):
            put(y, jnp.where(row == 0, own[0], normed(above_ref[t, y])))
            put(y + 8, jnp.where(row == 7, own[5], normed(below_ref[t, y])))
        for y in range(6):
            put(y + 2, own[y])
        for x in range(2):
            side[pl.ds(16 * x, 16), :] = normed(border_ref[t, x])
        for dy in range(3):

            def column(x):
                pieces = [plain[j, pl.ds(16 * dy + x, 8, stride=16), :] for j in range(chans // 128)]
                return jnp.concatenate(pieces, axis=1)

            inner = [column(x) for x in range(16)]
            outer = [side[pl.ds(16 * x + dy, 8), :] for x in range(2)]
            left = [jnp.where(col == 0, inner[0], o) for o in outer]
            right = [jnp.where(col == 0, o, inner[15]) for o in outer]
            columns = left + inner + right
            base = pl.multiple_of(t * 160, 16)
            for p in range(2):
                for i in range(10 - p):
                    pair = jnp.concatenate([columns[2 * i + p], columns[2 * i + p + 1]], axis=0)
                    out_ref[2 * dy + p, pl.ds(base + 16 * i, 16), :] = pair.astype(jnp.bfloat16)
            out_ref[2 * dy + 1, pl.ds(base + 144, 16), :] = jnp.zeros((16, chans), jnp.bfloat16)
        return 0

    lax.fori_loop(0, 6, frame, 0)


def conv1_kernel(count, bias_ref, copies_ref, gathered_ref, middle_ref, stats_ref, copies, weights, arrived):
    layouts = [pltpu.make_async_copy(copies_ref.at[i], copies.at[i], arrived.at[i]) for i in range(6)]
    fetches = [
        pltpu.make_async_copy(gathered_ref.at[3 * i : 3 * i + 3], weights.at[3 * i : 3 * i + 3], arrived.at[6 + i])
        for i in range(9)
    ]
    for dy in range(3):
        for copy in [*layouts[2 * dy : 2 * dy + 2], *fetches[dy::3]]:
            copy.start()
    middle_ref[...] = jnp.broadcast_to(bias_ref[...], middle_ref.shape)
    depth = 3 * weights.shape[1]
    for dy in range(3):
        for copy in layouts[2 * dy : 2 * dy + 2]:
            copy.wait()
        for dt in range(3):
            fetches[3 * dt + dy].wait()
            weight = weights[9 * dt + 3 * dy : 9 * dt + 3 * dy + 3].reshape(depth, weights.shape[2])
            for half in range(2):

                def window(dx, dy=dy, first=dt + 2 * half):
                    starts = [(first + t) * 160 + (dx // 2) * 16 for t in range(2)]
                    return jnp.concatenate([copies[2 * dy + dx % 2, at : at + 144, :] for at in starts], axis=0)

                lhs = jnp.concatenate([window(dx) for dx in range(3)], axis=1)
                product = jnp.dot(lhs, weight, preferred_element_type=jnp.float32)
                middle_ref[288 * half : 288 * half + 288, :] += product

    values = middle_ref[288:, :]
    place = lax.broadcasted_iota(jnp.int32, values.shape, 0)
    y, x = place % 8, (place // 8) % 18
    keep = (y >= 1) & (y <= 6) & (x >= 1) & (x <= 16)
    tile = channel_stats(values, keep, count)
    stats_ref[...] = jnp.broadcast_to(tile[None], stats_ref.shape)


def hidden2_kernel(count, peers, place_ref, parts_ref, gain_ref, shift_ref, middle_ref, copies):
    row, col, tm = place_ref[0], place_ref[1], place_ref[2]
    chans = middle_ref.shape[1]
    tile = merged(parts_ref, count)
    mean, scale = group_moments(tile, count * peers, chans // GROUPS, chans)
    gain, shift = gain_ref[...], shift_ref[...]
    y = lax.broadcasted_iota(jnp.int32, (8, chans), 0)
    for t in range(4):
        source = jnp.where(tm == 0, 2, t) if t < 2 else t
        block = middle_ref[pl.ds(pl.multiple_of(source * 144, 16), 144), :]
        block = silu_of(block, mean, scale, gain, shift)
        columns = [block[8 * x : 8 * x + 8] for x in range(18)]
        columns[0] = jnp.where(col == 0, columns[1], columns[0])
        columns[17] = jnp.where(col == 1, columns[16], columns[17])
        for x in range(18):
            column = columns[x]
            column = jnp.where((y == 0) & (row == 0), pltpu.roll(column, 7, 0), column)
            columns[x] = jnp.where((y == 7) & (row == 7), pltpu.roll(column, 1, 0), column)
        for dy in range(3):
            rolled = columns if dy == 0 else [pltpu.roll(c, 8 - dy, 0) for c in columns]
            for p in range(2):
                for i in range(9 - p):
                    pair = jnp.concatenate([rolled[2 * i + p], rolled[2 * i + p + 1]], axis=0)
                    copies[2 * dy + p, 144 * t + 16 * i : 144 * t + 16 * i + 16, :] = pair.astype(jnp.bfloat16)


def conv2_kernel(copies, bias_ref, features_ref, weight_ref, out_ref, total):
    chans = weight_ref.shape[3]

    def tap(k):
        return weight_ref[k // 2, :, 16 * (k % 2) : 16 * (k % 2) + 16, :].reshape(chans, chans)

    rows = [weight_ref[(27 + h) // 2, d, 16 * ((27 + h) % 2) : 16 * ((27 + h) % 2) + 16, :] for d in range(chans // 16) for h in range(2)]
    skip = jnp.concatenate(rows, axis=0)
    shortcut = jnp.dot(features_ref[...], skip, preferred_element_type=jnp.float32) + bias_ref[...]
    for dt in range(3):
        for dy in range(3):
            weight = jnp.concatenate([tap(9 * dt + 3 * dy + dx) for dx in range(3)], axis=0)
            for t in range(2):

                def window(dx, dy=dy, first=dt + t):
                    start = first * 144 + (dx // 2) * 16
                    return copies[2 * dy + dx % 2, start : start + 128, :]

                lhs = jnp.concatenate([window(dx) for dx in range(3)], axis=1)
                product = jnp.dot(lhs, weight, preferred_element_type=jnp.float32)
                for j in range(chans // 128):
                    part = product[:, 128 * j : 128 * (j + 1)]
                    if dt == 0 and dy == 0:
                        total[j, 128 * t : 128 * t + 128, :] = part
                    else:
                        total[j, 128 * t : 128 * t + 128, :] += part

    for t in range(2):
        for y in range(6):
            conv = [total[j, pl.ds(128 * t + y, 16, stride=8), :] for j in range(chans // 128)]
            at = (6 * t + y) * 16
            out_ref[at : at + 16, :] = (jnp.concatenate(conv, axis=1) + shortcut[at : at + 16]).astype(jnp.bfloat16)


def whole(*_):
    return pl.BlockSpec(memory_space=VMEM)


def per_device(
    features,
    gn1_gain,
    gn1_bias,
    conv1_weight,
    conv1_bias,
    skip_weight,
    gn2_gain,
    gn2_bias,
    conv2_weight,
    conv2_bias,
):
    frames, rows, cols, chans_in = features.shape
    chans_out = conv1_weight.shape[2]
    ntm, nrow, ncol = (lax.axis_size(a) for a in (TM, "row", "col"))
    tm, row, col = (lax.axis_index(a) for a in (TM, "row", "col"))
    place = jnp.stack([row, col, tm]).astype(jnp.int32)
    positions = frames * rows * cols
    plane = nrow * ncol
    flat_features = features.reshape(positions, chans_in)
    tile = jax.ShapeDtypeStruct((8, 128), jnp.float32)

    share = conv2_weight.shape[1]
    spare = jnp.zeros((3, share, chans_out), jnp.bfloat16)
    later = jnp.concatenate([conv2_weight, skip_weight.reshape(2, share, chans_out), spare], axis=0)
    later = later.reshape(16, 2 * share, chans_out)
    later = lax.dynamic_slice_in_dim(later, 4 * lax.axis_index("x"), 4, axis=0)
    taps = conv1_weight.shape[0]
    first = lax.all_gather(
        jnp.concatenate([conv1_weight, later], axis=0), ("row", "col"), axis=1, tiled=True
    )
    def shared(stats, count, beside=()):
        stats = lax.all_to_all(stats, ("row", "col"), 0, 0, tiled=True)
        if beside:
            stats, beside = lax.optimization_barrier((stats, beside))
        stats = pl.pallas_call(
            functools.partial(merge_kernel, count),
            out_shape=jax.ShapeDtypeStruct((ntm, *tile.shape), tile.dtype),
            in_specs=[whole()],
            out_specs=whole(),
        )(stats)
        return lax.all_to_all(stats, TM, 0, 0, tiled=True), beside

    stats = pl.pallas_call(
        stats_kernel,
        out_shape=jax.ShapeDtypeStruct((plane, *tile.shape), tile.dtype),
        in_specs=[whole()],
        out_specs=whole(),
    )(flat_features)
    back_one = moved(features, TM, 1)
    back_two = moved(features, TM, 2)
    first_twice = jnp.concatenate([features[:1], features[:1]], axis=0)
    back_one = jnp.where(tm == 0, first_twice, back_one)
    earliest = jnp.concatenate([back_one[:1], back_one[:1]], axis=0)
    back_two = jnp.where(tm <= 1, earliest, back_two)
    volume = jnp.concatenate([back_two, back_one, features], axis=0)

    parts, (last, leading) = shared(stats, float(positions), (volume[:, -2:], volume[:, :2]))
    above = moved(last, "row", 1)
    below = moved(leading, "row", -1)

    border = pl.pallas_call(
        border_kernel,
        out_shape=jax.ShapeDtypeStruct((volume.shape[0], 2, 16, chans_in), jnp.bfloat16),
        in_specs=[pl.BlockSpec(memory_space=SMEM)] + [whole()] * 3,
        out_specs=whole(),
        scratch_shapes=[VMEM((chans_in // 128, 256, 128), jnp.float32)],
        compiler_params=pltpu.CompilerParams(vmem_limit_bytes=16 * MIB),
    )(place, volume, above, below)
    border = swapped(border, "col")

    copies = pl.pallas_call(
        functools.partial(hidden1_kernel, float(positions * plane), ntm),
        out_shape=jax.ShapeDtypeStruct((6, 960, chans_in), jnp.bfloat16),
        in_specs=[pl.BlockSpec(memory_space=SMEM)] + [whole()] * 7,
        out_specs=whole(),
        scratch_shapes=[VMEM((chans_in // 128, 160, 128), jnp.float32), VMEM((32, chans_in), jnp.float32)],
        compiler_params=pltpu.CompilerParams(vmem_limit_bytes=24 * MIB),
    )(place, parts, gn1_gain[None], gn1_bias[None], volume, above, below, border)

    copies, first = lax.optimization_barrier((copies, first))
    half = lax.dynamic_slice_in_dim(first, taps + 2 * col, 2, axis=0)
    second = lax.all_gather(half, ("x", "col"), axis=0, tiled=True)
    second = second.reshape(16, plane, 2 * share, chans_out)

    middle, stats = pl.pallas_call(
        functools.partial(conv1_kernel, float(positions)),
        out_shape=(
            jax.ShapeDtypeStruct((576, chans_out), jnp.float32),
            jax.ShapeDtypeStruct((plane, *tile.shape), tile.dtype),
        ),
        in_specs=[whole()] + [pl.BlockSpec(memory_space=HBM)] * 2,
        out_specs=(whole(), whole()),
        scratch_shapes=[
            VMEM(copies.shape, jnp.bfloat16),
            VMEM((taps, chans_in, chans_out), jnp.bfloat16),
            pltpu.SemaphoreType.DMA((15,)),
        ],
        compiler_params=pltpu.CompilerParams(vmem_limit_bytes=60 * MIB),
    )(conv1_bias[None], copies, first)

    parts, _ = shared(stats, float(positions))

    copies = pl.pallas_call(
        functools.partial(hidden2_kernel, float(positions * plane), ntm),
        out_shape=jax.ShapeDtypeStruct((6, 576, chans_out), jnp.bfloat16),
        in_specs=[pl.BlockSpec(memory_space=SMEM)] + [whole()] * 4,
        out_specs=whole(),
        compiler_params=pltpu.CompilerParams(vmem_limit_bytes=16 * MIB),
    )(place, parts, gn2_gain[None], gn2_bias[None], middle)

    copies, second = lax.optimization_barrier((copies, second))
    out = pl.pallas_call(
        conv2_kernel,
        out_shape=jax.ShapeDtypeStruct((positions, chans_out), jnp.bfloat16),
        in_specs=[whole()] * 4,
        out_specs=whole(),
        scratch_shapes=[VMEM((chans_out // 128, 256, 128), jnp.float32)],
        compiler_params=pltpu.CompilerParams(vmem_limit_bytes=24 * MIB),
    )(copies, conv2_bias[None], flat_features, second)
    return out.reshape(frames, rows, cols, chans_out)


def solution(mesh):
    mesh = Mesh(mesh.devices.reshape(4, -1, *mesh.devices.shape[1:]), (*TM, "row", "col"))
    in_specs = (
        P(TM, "row", "col", None),
        P(),
        P(),
        P(None, ("row", "col"), None),
        P(),
        P(None, ("row", "col"), None),
        P(),
        P(),
        P(None, ("row", "col"), None),
        P(),
    )
    out_specs = P(TM, "row", "col", None)
    return jax.shard_map(
        per_device, mesh=mesh, in_specs=in_specs, out_specs=out_specs, check_vma=False
    )
```

time: 134 us -> 136 us (1.015)
  blocking collectives: 13.1 us -> 32.9 us
  starting transfers between devices: 50.1 us -> 35 us
  waiting for transfers between devices: 24 us -> 20 us
  local copies, waits for them, and re-layouts: 12.7 us -> 8.78 us
  Pallas kernels: 18 us -> 20.5 us
  other arithmetic: 2.24 us -> 4.03 us
    all_to_all x0 -> x1, blocking collectives: none -> 19 us  [shared(): return (lax.all_to_all(stats, TM, 0, 0, tiled=True), beside)]
    all_to_all x2 -> x1, starting transfers between devices: 24.9 us -> 10.2 us  [shared(): return (lax.all_to_all(stats, TM, 0, 0, tiled=True), beside)]
    ppermute x4, waiting for transfers between devices: 11.3 us -> 0.01 us  [moved(): return lax.ppermute(block, axis, route)]
    unnamed x26 -> x20, local copies, waits for them, and re-layouts: 12.1 us -> 5.88 us
    all_to_all x1, waiting for transfers between devices: 2.03 us -> 6.57 us  [shared(): stats = lax.all_to_all(stats, ('row', 'col'), 0, 0, tiled=True)]
    pallas_call x2 -> x4, Pallas kernels: 9.77 us -> 12.2 us  [the longest x1 8.11 us: per_device(): pl.pallas_call(functools.partial(conv1_kernel, float(positions)), out_sha...]
    all_to_all x2 -> x1, waiting for transfers between devices: 3.29 us -> 5.47 us  [shared(): return (lax.all_to_all(stats, TM, 0, 0, tiled=True), beside)]
    all_gather x2, waiting for transfers between devices: 5.87 us -> 7.93 us  [the longest x1 7.91 us: per_device(): lax.all_gather(jnp.concatenate([conv1_weight, later], axis=0), ('row', 'c...]
  transfers between devices with their start and end apart: 10 -> 9, of which waited for: 6 -> 3; matrix products, arithmetic and copies ran while one was open for 3% -> 2% of each run, Pallas kernels for 11% -> 14%
where the time goes in v3:
time: 136 us; the launch traced here: 135 us
  starting transfers between devices  35 us (26%)
  blocking collectives  32.9 us (24%)
  Pallas kernels  20.5 us (15%)
  waiting for transfers between devices  20 us (15%)
  between operations  13.6 us (10%)
  local copies, waits for them, and re-layouts  8.78 us (6%)
  other arithmetic  4.03 us (3%)
    all_to_all x1, blocking collectives, shared(): return (lax.all_to_all(stats, TM, 0, 0, tiled=True), beside)  19 us
    all_to_all x1, blocking collectives, shared(): stats = lax.all_to_all(stats, ('row', 'col'), 0, 0, tiled=True)  13.9 us
    ppermute x4, starting transfers between devices, moved(): return lax.ppermute(block, axis, route)  13.9 us
    all_to_all x1, starting transfers between devices, shared(): return (lax.all_to_all(stats, TM, 0, 0, tiled=True), beside)  10.2 us
    all_to_all x1, starting transfers between devices, shared(): stats = lax.all_to_all(stats, ('row', 'col'), 0, 0, tiled=True)  8.35 us
    pallas_call x1, Pallas kernels, per_device(): pl.pallas_call(functools.partial(conv1_kernel, float(positions)), out_sha...  8.11 us
    all_gather x1, waiting for transfers between devices, per_device(): lax.all_gather(jnp.concatenate([conv1_weight, later], axis=0), ('row', 'c...  7.91 us
    all_to_all x1, waiting for transfers between devices, shared(): stats = lax.all_to_all(stats, ('row', 'col'), 0, 0, tiled=True)  6.57 us
  transfers between devices with their start and end apart: 9, of which 3 were waited for; matrix products, arithmetic and copies ran while one was open for 2% of the time, Pallas kernels for 14%

profile of v3, /device:TPU:1, one launch (start us, length us, event | category | flops | bytes accessed | tf_op | source)
XLA Modules:
  0.0 134.9 jit_solution(18390608557617576024)
XLA Ops:
  6.5 0.0 copy-start.4
  6.5 0.0 copy-start.5
  6.5 0.0 all-gather.3.cloned.1.call-start
  6.5 0.1 pad.4.clone
  6.6 1.1 maximum_maximum_fusion
  7.7 1.9 %pad_maximum_fusion.1 = bf16[31,32,256]{2,1,0:T(8,128)(2,1)} fusion(bf16[4,32,256]{2,1,0:T(8,128)(2,1)S(1)} %constant_dynamic-slice_fusion.1, bf16[27,32,256]{2,1,0:T(8,128)(2,1)} %param.13), kind=kLoop, calls=%fused_computation.1 | loop fusion | flops 253952 | bytes 1015808 | tf_op jit(solution)/shard_map/concatenate | solution.py:303
  9.6 0.0 all-gather.3.cloned.1.call-update
  9.6 4.9 %collective-permute-start = (bf16[2,6,16,512]{3,2,1,0:T(8,128)(2,1)}, bf16[2,6,16,512]{3,2,1,0:T(8,128)(2,1)S(1)}, u32[]{:S(2)}, u32[]{:S(2)}) collective-permute-start(bf16[2,6,16,512]{3,2,1,0:T(8,128)(2,1)} %param.10), channel_id=1, source_target_pairs={{0,16},{16,32},{32,48},{48,64},{64,80},{80,96},{96,112},{112,128},... | collective-permute-start | bytes 589832 | tf_op jit(solution)/shard_map/ppermute | solution.py:22
  14.5 5.8 %collective-permute-start.1 = (bf16[2,6,16,512]{3,2,1,0:T(8,128)(2,1)}, bf16[2,6,16,512]{3,2,1,0:T(8,128)(2,1)S(1)}, u32[]{:S(2)}, u32[]{:S(2)}) collective-permute-start(bf16[2,6,16,512]{3,2,1,0:T(8,128)(2,1)} %param.10), channel_id=1, source_target_pairs={{0,32},{16,48},{32,64},{48,80},{64,96},{80,112},{96,128},{112,144}... | collective-permute-start | bytes 589832 | tf_op jit(solution)/shard_map/ppermute | solution.py:22
  20.3 1.7 %shard_map.100 = f32[16,8,128]{2,1,0:T(8,128)} custom-call(bf16[192,512]{1,0:T(8,128)(2,1)} %bitcast.15), custom_call_target="tpu_custom_call" | custom-call | tf_op jit(solution)/shard_map/pallas_call | solution.py:317
  21.9 8.3 %all-to-all-start = ((f32[16,8,128]{2,1,0:T(8,128)}), f32[16,8,128]{2,1,0:T(8,128)S(1)}, u32[]{:S(2)}, u32[]{:S(2)}) async-start(f32[16,8,128]{2,1,0:T(8,128)} %shard_map.100), calls=%async_computation | async-start | bytes 131072 | tf_op jit(solution)/shard_map/all_to_all | solution.py:306
  30.3 0.9 slice.14
  31.2 0.0 collective-permute-done
  31.2 0.0 collective-permute-done.1
  31.3 1.0 pad_maximum_fusion.centre_ref
  32.3 6.6 %all-to-all-done.parts_ref = f32[16,8,128]{2,1,0:T(8,128)S(1)} async-done(((f32[16,8,128]{2,1,0:T(8,128)}), f32[16,8,128]{2,1,0:T(8,128)S(1)}, u32[]{:S(2)}, u32[]{:S(2)}) %all-to-all-start) | async-done | bytes 65568 | tf_op jit(solution)/shard_map/all_to_all | solution.py:306
  38.9 0.0 copy-start.9
  38.9 1.9 %collective-permute-start.2 = (bf16[6,2,16,512]{3,2,1,0:T(8,128)(2,1)S(1)}, bf16[6,2,16,512]{3,2,1,0:T(8,128)(2,1)S(1)}, u32[]{:S(2)}, u32[]{:S(2)}) collective-permute-start(bf16[6,2,16,512]{3,2,1,0:T(8,128)(2,1)S(1)} %get-tuple-element.15), channel_id=1, source_target_pairs={{0,2},{2,4},{4,6},{6,8},{8,10},{10,12},{12,14},{1,3},{3,5},{5,7},{... | collective-permute-start | bytes 589832 | tf_op jit(solution)/shard_map/ppermute | solution.py:22
  40.8 1.3 collective-permute-start.3
  42.1 0.0 copy-done.9
  42.1 1.5 %shard_map.101 = f32[32,8,128]{2,1,0:T(8,128)} custom-call(f32[16,8,128]{2,1,0:T(8,128)} %copy-done.9), custom_call_target="tpu_custom_call" | custom-call | tf_op jit(solution)/shard_map/pallas_call | solution.py:309
  43.7 10.2 %all-to-all-start.1 = ((f32[32,8,128]{2,1,0:T(8,128)}), f32[32,8,128]{2,1,0:T(8,128)S(1)}, u32[]{:S(2)}, u32[]{:S(2)}) async-start(f32[32,8,128]{2,1,0:T(8,128)} %shard_map.101), calls=%async_computation.1 | async-start | bytes 262144 | tf_op jit(solution)/shard_map/all_to_all | solution.py:315
  53.8 0.0 all-gather.5.cloned.1.call-start
  53.9 0.1 pad_add_fusion.place_ref
  54.0 0.0 collective-permute-done.2.above_ref
  54.0 0.0 collective-permute-done.3.below_ref
  54.0 1.0 shard_map.102
  55.0 2.5 %collective-permute-start.4 = (bf16[6,2,16,512]{3,2,1,0:T(8,128)(2,1)S(1)}, bf16[6,2,16,512]{3,2,1,0:T(8,128)(2,1)S(1)}, u32[]{:S(2)}, u32[]{:S(2)}) collective-permute-start(bf16[6,2,16,512]{3,2,1,0:T(8,128)(2,1)S(1)} %shard_map.102), channel_id=1, source_target_pairs={{0,1},{1,0},{2,3},{3,2},{4,5},{5,4},{6,7},{7,6},{8,9},{9,8},{10,11... | collective-permute-start | bytes 589832 | tf_op jit(solution)/shard_map/ppermute | solution.py:26
  57.5 5.5 %all-to-all-done.1.parts_ref = f32[32,8,128]{2,1,0:T(8,128)S(1)} async-done(((f32[32,8,128]{2,1,0:T(8,128)}), f32[32,8,128]{2,1,0:T(8,128)S(1)}, u32[]{:S(2)}, u32[]{:S(2)}) %all-to-all-start.1) | async-done | bytes 131104 | tf_op jit(solution)/shard_map/all_to_all | solution.py:315
  63.0 0.0 collective-permute-done.4.border_ref
  63.0 0.0 copy-done.4
  63.0 0.0 copy-done.5
  63.0 3.5 %shard_map.103.copies_ref = bf16[6,960,512]{2,1,0:T(8,128)(2,1)S(1)} custom-call(s32[3]{0:T(128)S(1)} %pad_add_fusion.place_ref, f32[32,8,128]{2,1,0:T(8,128)S(1)} %all-to-all-done.1.parts_ref, f32[1,512]{1,0:T(1,128)S(1)} %bitcast.17, f32[1,512]{1,0:T(1,128)S(1)} %bitcast.18, bf16[6,6,16,512]{3,2,1,0:T(8,128)(2,1)S(1)} %pad_maximum_fusion.centre_ref, ...), custom_call_target="tpu_custom_call" | custom-call | tf_op jit(solution)/shard_map/pallas_call | solution.py:345
  66.5 0.0 copy-start
  66.5 2.6 %copy-done = bf16[6,960,512]{2,1,0:T(8,128)(2,1)} copy-done((bf16[6,960,512]{2,1,0:T(8,128)(2,1)}, bf16[6,960,512]{2,1,0:T(8,128)(2,1)S(1)}, u32[]{:S(2)}) %copy-start) | copy-done | bytes 5898264
  69.1 7.9 %all-gather.3.cloned.1.call-done.gathered_ref = bf16[31,512,256]{2,1,0:T(8,128)(2,1)} async-done(((bf16[31,32,256]{2,1,0:T(8,128)(2,1)}), bf16[31,512,256]{2,1,0:T(8,128)(2,1)}) %all-gather.3.cloned.1.call-update) | async-done | bytes 8126480 | tf_op jit(solution)/shard_map/all_gather | solution.py:302
  77.0 1.9 %constant_dynamic-slice_fusion = bf16[2,512,256]{2,1,0:T(8,128)(2,1)} fusion(bf16[31,512,256]{2,1,0:T(8,128)(2,1)} %all-gather.3.cloned.1.call-done.gathered_ref, s32[]{:T(128)S(6)} %select_n.25), kind=kLoop, calls=%fused_computation.6 | loop fusion | bytes 1048580 | tf_op jit(solution)/shard_map/dynamic_slice | solution.py:355
  78.9 0.0 all-gather.5.cloned.1.call-update
  78.9 0.0 copy-start.6
  78.9 0.0 copy-start.7
  78.9 0.0 copy-start.2
  79.0 0.0 copy-start.8
  79.0 8.1 %shard_map.104 = (f32[576,256]{1,0:T(8,128)}, f32[16,8,128]{2,1,0:T(8,128)}) custom-call(f32[1,256]{1,0:T(1,128)} %bitcast.24, bf16[6,960,512]{2,1,0:T(8,128)(2,1)} %copy-done, bf16[31,512,256]{2,1,0:T(8,128)(2,1)} %all-gather.3.cloned.1.call-done.gathered_ref), custom_call_target="tpu_custom_call" | custom-call | tf_op jit(solution)/shard_map/pallas_call | solution.py:359
  87.1 13.9 %all_to_all.20.parts_ref = f32[16,8,128]{2,1,0:T(8,128)} all-to-all(f32[16,8,128]{2,1,0:T(8,128)} %get-tuple-element.19), channel_id=1, replica_groups=mesh['x'=4,'z'=8,'row'=8,'col'=2] {'row','col'}, dimensions={0} | all-to-all | bytes 131072 | tf_op jit(solution)/shard_map/all_to_all | solution.py:306
  101.0 1.5 %shard_map.105 = f32[32,8,128]{2,1,0:T(8,128)} custom-call(f32[16,8,128]{2,1,0:T(8,128)} %all_to_all.20.parts_ref), custom_call_target="tpu_custom_call" | custom-call | tf_op jit(solution)/shard_map/pallas_call | solution.py:309
  102.5 19.0 %all_to_all.21.parts_ref = f32[32,8,128]{2,1,0:T(8,128)S(1)} all-to-all(f32[32,8,128]{2,1,0:T(8,128)} %shard_map.105), channel_id=1, replica_groups=mesh['x'=4,'z'=8,'row'=8,'col'=2] {'x','z'}, dimensions={0} | all-to-all | bytes 262144 | tf_op jit(solution)/shard_map/all_to_all | solution.py:315
  121.6 0.0 copy-done.6
  121.6 0.0 copy-done.7
  121.6 0.0 copy-start.3
  121.6 1.1 copy-done.3
  122.6 1.3 shard_map.106.copies
  124.0 0.0 all-gather.5.cloned.1.call-done
  124.0 0.0 copy-done.2
  124.0 0.0 copy-done.8
  124.0 0.0 copy-start.1
  124.0 2.2 %copy-done.1 = bf16[16,512,256]{2,1,0:T(8,128)(2,1)S(1)} copy-done((bf16[16,512,256]{2,1,0:T(8,128)(2,1)S(1)}, bf16[16,512,256]{2,1,0:T(8,128)(2,1)}, u32[]{:S(2)}) %copy-start.1) | copy-done | bytes 4194328
  126.2 1.8 %shard_map.107 = bf16[192,256]{1,0:T(8,128)(2,1)} custom-call(bf16[6,576,256]{2,1,0:T(8,128)(2,1)S(1)} %shard_map.106.copies, f32[1,256]{1,0:T(1,128)S(1)} %bitcast.21, bf16[192,512]{1,0:T(8,128)(2,1)S(1)} %bitcast.16, bf16[16,16,32,256]{3,2,1,0:T(8,128)(2,1)S(1)} %bitcast.14), custom_call_target="tpu_custom_call" | custom-call | tf_op jit(solution)/shard_map/pallas_call | solution.py:386
  (6 shorter events, 0.1 us)
Async XLA Ops:
  6.5 56.5 %copy-start.4 = (f32[512]{0:T(512)S(1)}, f32[512]{0:T(512)}, u32[]{:S(2)}) copy-start(f32[512]{0:T(512)} %param.11) | copy-start | bytes 6148
  6.5 56.5 %copy-start.5 = (f32[512]{0:T(512)S(1)}, f32[512]{0:T(512)}, u32[]{:S(2)}) copy-start(f32[512]{0:T(512)} %param.12) | copy-start | bytes 6148
  6.5 70.5 %all-gather.3.cloned.1.call-start = ((), (), s32[]{:S(2)}) async-start(), calls=%async_computation.4 | async-start | bytes 8634368 | tf_op jit(solution)/shard_map/all_gather | solution.py:302
  9.6 21.6 %collective-permute-start = (bf16[2,6,16,512]{3,2,1,0:T(8,128)(2,1)}, bf16[2,6,16,512]{3,2,1,0:T(8,128)(2,1)S(1)}, u32[]{:S(2)}, u32[]{:S(2)}) collective-permute-start(bf16[2,6,16,512]{3,2,1,0:T(8,128)(2,1)} %param.10), channel_id=1, source_target_pairs={{0,16},{16,32},{32,48},{48,64},{64,80},{80,96},{96,112},{112,128},... | collective-permute-start | bytes 589832 | tf_op jit(solution)/shard_map/ppermute | solution.py:22
  14.5 16.8 %collective-permute-start.1 = (bf16[2,6,16,512]{3,2,1,0:T(8,128)(2,1)}, bf16[2,6,16,512]{3,2,1,0:T(8,128)(2,1)S(1)}, u32[]{:S(2)}, u32[]{:S(2)}) collective-permute-start(bf16[2,6,16,512]{3,2,1,0:T(8,128)(2,1)} %param.10), channel_id=1, source_target_pairs={{0,32},{16,48},{32,64},{48,80},{64,96},{80,112},{96,128},{112,144}... | collective-permute-start | bytes 589832 | tf_op jit(solution)/shard_map/ppermute | solution.py:22
  21.9 16.9 %all-to-all-start = ((f32[16,8,128]{2,1,0:T(8,128)}), f32[16,8,128]{2,1,0:T(8,128)S(1)}, u32[]{:S(2)}, u32[]{:S(2)}) async-start(f32[16,8,128]{2,1,0:T(8,128)} %shard_map.100), calls=%async_computation | async-start | bytes 131072 | tf_op jit(solution)/shard_map/all_to_all | solution.py:306
  38.9 3.2 %copy-start.9 = (f32[16,8,128]{2,1,0:T(8,128)}, f32[16,8,128]{2,1,0:T(8,128)S(1)}, u32[]{:S(2)}) copy-start(f32[16,8,128]{2,1,0:T(8,128)S(1)} %all-to-all-done.parts_ref) | copy-start | bytes 196612
  38.9 15.1 %collective-permute-start.2 = (bf16[6,2,16,512]{3,2,1,0:T(8,128)(2,1)S(1)}, bf16[6,2,16,512]{3,2,1,0:T(8,128)(2,1)S(1)}, u32[]{:S(2)}, u32[]{:S(2)}) collective-permute-start(bf16[6,2,16,512]{3,2,1,0:T(8,128)(2,1)S(1)} %get-tuple-element.15), channel_id=1, source_target_pairs={{0,2},{2,4},{4,6},{6,8},{8,10},{10,12},{12,14},{1,3},{3,5},{5,7},{... | collective-permute-start | bytes 589832 | tf_op jit(solution)/shard_map/ppermute | solution.py:22
  40.8 13.2 %collective-permute-start.3 = (bf16[6,2,16,512]{3,2,1,0:T(8,128)(2,1)S(1)}, bf16[6,2,16,512]{3,2,1,0:T(8,128)(2,1)S(1)}, u32[]{:S(2)}, u32[]{:S(2)}) collective-permute-start(bf16[6,2,16,512]{3,2,1,0:T(8,128)(2,1)S(1)} %get-tuple-element.16), channel_id=1, source_target_pairs={{2,0},{4,2},{6,4},{8,6},{10,8},{12,10},{14,12},{3,1},{5,3},{7,5},{... | collective-permute-start | bytes 589832 | tf_op jit(solution)/shard_map/ppermute | solution.py:22
  43.7 19.3 %all-to-all-start.1 = ((f32[32,8,128]{2,1,0:T(8,128)}), f32[32,8,128]{2,1,0:T(8,128)S(1)}, u32[]{:S(2)}, u32[]{:S(2)}) async-start(f32[32,8,128]{2,1,0:T(8,128)} %shard_map.101), calls=%async_computation.1 | async-start | bytes 262144 | tf_op jit(solution)/shard_map/all_to_all | solution.py:315
  53.8 70.2 %all-gather.5.cloned.1.call-start = ((), (), s32[]{:S(2)}) async-start(), calls=%async_computation.5 | async-start | bytes 4718592 | tf_op jit(solution)/shard_map/all_gather | solution.py:356
  55.0 8.0 %collective-permute-start.4 = (bf16[6,2,16,512]{3,2,1,0:T(8,128)(2,1)S(1)}, bf16[6,2,16,512]{3,2,1,0:T(8,128)(2,1)S(1)}, u32[]{:S(2)}, u32[]{:S(2)}) collective-permute-start(bf16[6,2,16,512]{3,2,1,0:T(8,128)(2,1)S(1)} %shard_map.102), channel_id=1, source_target_pairs={{0,1},{1,0},{2,3},{3,2},{4,5},{5,4},{6,7},{7,6},{8,9},{9,8},{10,11... | collective-permute-start | bytes 589832 | tf_op jit(solution)/shard_map/ppermute | solution.py:26
  66.5 2.6 %copy-start = (bf16[6,960,512]{2,1,0:T(8,128)(2,1)}, bf16[6,960,512]{2,1,0:T(8,128)(2,1)S(1)}, u32[]{:S(2)}) copy-start(bf16[6,960,512]{2,1,0:T(8,128)(2,1)S(1)} %shard_map.103.copies_ref) | copy-start | bytes 17694724
  78.9 42.6 %copy-start.6 = (f32[256]{0:T(256)S(1)}, f32[256]{0:T(256)}, u32[]{:S(2)}) copy-start(f32[256]{0:T(256)} %param.16) | copy-start | bytes 3076
  78.9 42.6 %copy-start.7 = (f32[256]{0:T(256)S(1)}, f32[256]{0:T(256)}, u32[]{:S(2)}) copy-start(f32[256]{0:T(256)} %param.17) | copy-start | bytes 3076
  78.9 45.1 %copy-start.2 = (bf16[2,6,16,512]{3,2,1,0:T(8,128)(2,1)S(1)}, bf16[2,6,16,512]{3,2,1,0:T(8,128)(2,1)}, u32[]{:S(2)}) copy-start(bf16[2,6,16,512]{3,2,1,0:T(8,128)(2,1)} %param.10) | copy-start | bytes 589828
  79.0 45.1 %copy-start.8 = (f32[256]{0:T(256)S(1)}, f32[256]{0:T(256)}, u32[]{:S(2)}) copy-start(f32[256]{0:T(256)} %param.19) | copy-start | bytes 3076
  121.6 1.1 copy-start.3
  124.0 2.2 %copy-start.1 = (bf16[16,512,256]{2,1,0:T(8,128)(2,1)S(1)}, bf16[16,512,256]{2,1,0:T(8,128)(2,1)}, u32[]{:S(2)}) copy-start(bf16[16,512,256]{2,1,0:T(8,128)(2,1)} %all-gather.5.cloned.1.call-done) | copy-start | bytes 12582916
Sparse Core Ops, SparseCore 0:
  9.7 67.2 all-gather.2
  79.2 37.6 all-gather.4

commit v4 on v3

--- a/solution.py
+++ b/solution.py
@@ -122,7 +122,7 @@
             out_ref[t, x] = jnp.where(col == 0, column(14 + x), column(x)).astype(jnp.bfloat16)
         return 0
 
-    lax.fori_loop(0, 6, frame, 0)
+    lax.fori_loop(0, 4, frame, 0)
 
 
 def hidden1_kernel(
@@ -169,7 +169,7 @@
             out_ref[2 * dy + 1, pl.ds(base + 144, 16), :] = jnp.zeros((16, chans), jnp.bfloat16)
         return 0
 
-    lax.fori_loop(0, 6, frame, 0)
+    lax.fori_loop(0, 4, frame, 0)
 
 
 def conv1_kernel(count, bias_ref, copies_ref, gathered_ref, middle_ref, stats_ref, copies, weights, arrived):
@@ -189,17 +189,15 @@
         for dt in range(3):
             fetches[3 * dt + dy].wait()
             weight = weights[9 * dt + 3 * dy : 9 * dt + 3 * dy + 3].reshape(depth, weights.shape[2])
-            for half in range(2):
-
-                def window(dx, dy=dy, first=dt + 2 * half):
-                    starts = [(first + t) * 160 + (dx // 2) * 16 for t in range(2)]
-                    return jnp.concatenate([copies[2 * dy + dx % 2, at : at + 144, :] for at in starts], axis=0)
-
-                lhs = jnp.concatenate([window(dx) for dx in range(3)], axis=1)
-                product = jnp.dot(lhs, weight, preferred_element_type=jnp.float32)
-                middle_ref[288 * half : 288 * half + 288, :] += product
-
-    values = middle_ref[288:, :]
+
+            def window(dx, dy=dy, dt=dt):
+                starts = [(dt + t) * 160 + (dx // 2) * 16 for t in range(2)]
+                return jnp.concatenate([copies[2 * dy + dx % 2, at : at + 144, :] for at in starts], axis=0)
+
+            lhs = jnp.concatenate([window(dx) for dx in range(3)], axis=1)
+            middle_ref[...] += jnp.dot(lhs, weight, preferred_element_type=jnp.float32)
+
+    values = middle_ref[...]
     place = lax.broadcasted_iota(jnp.int32, values.shape, 0)
     y, x = place % 8, (place // 8) % 18
     keep = (y >= 1) & (y <= 6) & (x >= 1) & (x <= 16)
@@ -207,7 +205,7 @@
     stats_ref[...] = jnp.broadcast_to(tile[None], stats_ref.shape)
 
 
-def hidden2_kernel(count, peers, place_ref, parts_ref, gain_ref, shift_ref, middle_ref, copies):
+def hidden2_kernel(count, peers, place_ref, parts_ref, gain_ref, shift_ref, earlier_ref, middle_ref, copies):
     row, col, tm = place_ref[0], place_ref[1], place_ref[2]
     chans = middle_ref.shape[1]
     tile = merged(parts_ref, count)
@@ -215,8 +213,10 @@
     gain, shift = gain_ref[...], shift_ref[...]
     y = lax.broadcasted_iota(jnp.int32, (8, chans), 0)
     for t in range(4):
-        source = jnp.where(tm == 0, 2, t) if t < 2 else t
-        block = middle_ref[pl.ds(pl.multiple_of(source * 144, 16), 144), :]
+        if t < 2:
+            block = jnp.where(tm == 0, middle_ref[:144, :], earlier_ref[144 * t : 144 * t + 144, :])
+        else:
+            block = middle_ref[144 * (t - 2) : 144 * (t - 1), :]
         block = silu_of(block, mean, scale, gain, shift)
         columns = [block[8 * x : 8 * x + 8] for x in range(18)]
         columns[0] = jnp.where(col == 0, columns[1], columns[0])
@@ -234,17 +234,13 @@
 
 
 def conv2_kernel(copies, bias_ref, features_ref, weight_ref, out_ref, total):
-    chans = weight_ref.shape[3]
-
-    def tap(k):
-        return weight_ref[k // 2, :, 16 * (k % 2) : 16 * (k % 2) + 16, :].reshape(chans, chans)
-
-    rows = [weight_ref[(27 + h) // 2, d, 16 * ((27 + h) % 2) : 16 * ((27 + h) % 2) + 16, :] for d in range(chans // 16) for h in range(2)]
+    chans = weight_ref.shape[2]
+    rows = [weight_ref[27 + h, 16 * d : 16 * d + 16, :] for d in range(chans // 16) for h in range(2)]
     skip = jnp.concatenate(rows, axis=0)
     shortcut = jnp.dot(features_ref[...], skip, preferred_element_type=jnp.float32) + bias_ref[...]
     for dt in range(3):
         for dy in range(3):
-            weight = jnp.concatenate([tap(9 * dt + 3 * dy + dx) for dx in range(3)], axis=0)
+            weight = weight_ref[9 * dt + 3 * dy : 9 * dt + 3 * dy + 3].reshape(3 * chans, chans)
             for t in range(2):
 
                 def window(dx, dy=dy, first=dt + t):
@@ -293,15 +289,11 @@
     flat_features = features.reshape(positions, chans_in)
     tile = jax.ShapeDtypeStruct((8, 128), jnp.float32)
 
+    first = lax.all_gather(conv1_weight, ("row", "col"), axis=1, tiled=True)
     share = conv2_weight.shape[1]
-    spare = jnp.zeros((3, share, chans_out), jnp.bfloat16)
-    later = jnp.concatenate([conv2_weight, skip_weight.reshape(2, share, chans_out), spare], axis=0)
-    later = later.reshape(16, 2 * share, chans_out)
-    later = lax.dynamic_slice_in_dim(later, 4 * lax.axis_index("x"), 4, axis=0)
-    taps = conv1_weight.shape[0]
-    first = lax.all_gather(
-        jnp.concatenate([conv1_weight, later], axis=0), ("row", "col"), axis=1, tiled=True
-    )
+    halves = skip_weight.reshape(2, share, chans_out)
+    second = lax.all_gather(jnp.concatenate([conv2_weight, halves], axis=0), ("row", "col"), axis=1, tiled=True)
+
     def shared(stats, count, beside=()):
         stats = lax.all_to_all(stats, ("row", "col"), 0, 0, tiled=True)
         if beside:
@@ -320,13 +312,10 @@
         in_specs=[whole()],
         out_specs=whole(),
     )(flat_features)
-    back_one = moved(features, TM, 1)
-    back_two = moved(features, TM, 2)
+    earlier = moved(features, TM, 1)
     first_twice = jnp.concatenate([features[:1], features[:1]], axis=0)
-    back_one = jnp.where(tm == 0, first_twice, back_one)
-    earliest = jnp.concatenate([back_one[:1], back_one[:1]], axis=0)
-    back_two = jnp.where(tm <= 1, earliest, back_two)
-    volume = jnp.concatenate([back_two, back_one, features], axis=0)
+    earlier = jnp.where(tm == 0, first_twice, earlier)
+    volume = jnp.concatenate([earlier, features], axis=0)
 
     parts, (last, leading) = shared(stats, float(positions), (volume[:, -2:], volume[:, :2]))
     above = moved(last, "row", 1)
@@ -344,43 +333,39 @@
 
     copies = pl.pallas_call(
         functools.partial(hidden1_kernel, float(positions * plane), ntm),
-        out_shape=jax.ShapeDtypeStruct((6, 960, chans_in), jnp.bfloat16),
+        out_shape=jax.ShapeDtypeStruct((6, 640, chans_in), jnp.bfloat16),
         in_specs=[pl.BlockSpec(memory_space=SMEM)] + [whole()] * 7,
         out_specs=whole(),
         scratch_shapes=[VMEM((chans_in // 128, 160, 128), jnp.float32), VMEM((32, chans_in), jnp.float32)],
         compiler_params=pltpu.CompilerParams(vmem_limit_bytes=24 * MIB),
     )(place, parts, gn1_gain[None], gn1_bias[None], volume, above, below, border)
 
-    copies, first = lax.optimization_barrier((copies, first))
-    half = lax.dynamic_slice_in_dim(first, taps + 2 * col, 2, axis=0)
-    second = lax.all_gather(half, ("x", "col"), axis=0, tiled=True)
-    second = second.reshape(16, plane, 2 * share, chans_out)
-
     middle, stats = pl.pallas_call(
         functools.partial(conv1_kernel, float(positions)),
         out_shape=(
-            jax.ShapeDtypeStruct((576, chans_out), jnp.float32),
+            jax.ShapeDtypeStruct((288, chans_out), jnp.float32),
             jax.ShapeDtypeStruct((plane, *tile.shape), tile.dtype),
         ),
         in_specs=[whole()] + [pl.BlockSpec(memory_space=HBM)] * 2,
         out_specs=(whole(), whole()),
         scratch_shapes=[
             VMEM(copies.shape, jnp.bfloat16),
-            VMEM((taps, chans_in, chans_out), jnp.bfloat16),
+            VMEM(first.shape, jnp.bfloat16),
             pltpu.SemaphoreType.DMA((15,)),
         ],
         compiler_params=pltpu.CompilerParams(vmem_limit_bytes=60 * MIB),
     )(conv1_bias[None], copies, first)
 
+    earlier = moved(middle, TM, 1)
     parts, _ = shared(stats, float(positions))
 
     copies = pl.pallas_call(
         functools.partial(hidden2_kernel, float(positions * plane), ntm),
         out_shape=jax.ShapeDtypeStruct((6, 576, chans_out), jnp.bfloat16),
-        in_specs=[pl.BlockSpec(memory_space=SMEM)] + [whole()] * 4,
+        in_specs=[pl.BlockSpec(memory_space=SMEM)] + [whole()] * 5,
         out_specs=whole(),
         compiler_params=pltpu.CompilerParams(vmem_limit_bytes=16 * MIB),
-    )(place, parts, gn2_gain[None], gn2_bias[None], middle)
+    )(place, parts, gn2_gain[None], gn2_bias[None], earlier, middle)
 
     copies, second = lax.optimization_barrier((copies, second))
     out = pl.pallas_call(

time: 136 us -> 127 us (0.934)
  blocking collectives: 32.9 us -> 0 us
  starting transfers between devices: 35 us -> 49.6 us
  waiting for transfers between devices: 20 us -> 34.2 us
  local copies, waits for them, and re-layouts: 8.78 us -> 6.59 us
  Pallas kernels: 20.5 us -> 19 us
    all_to_all x2 -> x0, blocking collectives: 32.9 us -> none  [the longest x1 19 us: shared(): return (lax.all_to_all(stats, TM, 0, 0, tiled=True), beside)]
    all_to_all x1 -> x2, starting transfers between devices: 10.2 us -> 21.9 us  [shared(): return (lax.all_to_all(stats, TM, 0, 0, tiled=True), beside)]
    all_to_all x1 -> x2, waiting for transfers between devices: 5.47 us -> 13.7 us  [shared(): return (lax.all_to_all(stats, TM, 0, 0, tiled=True), beside)]
    all_to_all x1 -> x2, starting transfers between devices: 8.35 us -> 13.4 us  [shared(): stats = lax.all_to_all(stats, ('row', 'col'), 0, 0, tiled=True)]
    all_to_all x1 -> x2, waiting for transfers between devices: 6.57 us -> 10.5 us  [shared(): stats = lax.all_to_all(stats, ('row', 'col'), 0, 0, tiled=True)]
    ppermute x4, starting transfers between devices: 13.9 us -> 11.5 us  [moved(): return lax.ppermute(block, axis, route)]
    dynamic_slice x2 -> x0, local copies, waits for them, and re-layouts: 1.88 us -> none  [the longest x1 1.87 us: per_device(): half = lax.dynamic_slice_in_dim(first, taps + 2 * col, 2, axis=0)]
    unnamed x20 -> x22, local copies, waits for them, and re-layouts: 5.88 us -> 5.69 us
  transfers between devices with their start and end apart: 9 -> 11, of which waited for: 3 -> 6; matrix products, arithmetic and copies ran while one was open for 2% -> 4% of each run, Pallas kernels for 14% -> 14%
where the time goes in v4:
time: 127 us
  starting transfers between devices  49.6 us (39%)
  waiting for transfers between devices  34.2 us (27%)
  Pallas kernels  19 us (15%)
  between operations  13.6 us (11%)
  local copies, waits for them, and re-layouts  6.59 us (5%)
  other arithmetic  3.64 us (3%)
    all_to_all x2, starting transfers between devices, shared(): return (lax.all_to_all(stats, TM, 0, 0, tiled=True), beside)  21.9 us
    all_to_all x2, waiting for transfers between devices, shared(): return (lax.all_to_all(stats, TM, 0, 0, tiled=True), beside)  13.7 us
    all_to_all x2, starting transfers between devices, shared(): stats = lax.all_to_all(stats, ('row', 'col'), 0, 0, tiled=True)  13.4 us
    ppermute x4, starting transfers between devices, moved(): return lax.ppermute(block, axis, route)  11.5 us
    all_to_all x2, waiting for transfers between devices, shared(): stats = lax.all_to_all(stats, ('row', 'col'), 0, 0, tiled=True)  10.5 us
    pallas_call x1, Pallas kernels, per_device(): pl.pallas_call(functools.partial(conv1_kernel, float(positions)), out_sha...  7.55 us
    all_gather x1, waiting for transfers between devices, per_device(): first = lax.all_gather(conv1_weight, ('row', 'col'), axis=1, tiled=True)  7.42 us
    unnamed x22, local copies, waits for them, and re-layouts  5.69 us
  transfers between devices with their start and end apart: 11, of which 6 were waited for; matrix products, arithmetic and copies ran while one was open for 4% of the time, Pallas kernels for 14%

profile of v4, /device:TPU:1, one launch (start us, length us, event | category | flops | bytes accessed | tf_op | source)
XLA Modules:
  0.0 126.6 jit_solution(7697920049541750115)
XLA Ops:
  6.5 0.0 copy-start.4
  6.5 0.0 copy-start.5
  6.5 0.0 all-gather.3.cloned.1.call-start
  6.5 0.7 all-gather.3.cloned.1.call-update
  7.3 0.0 all-gather.5.cloned.1.call-start
  7.3 1.7 %pad_maximum_fusion.1 = bf16[29,16,256]{2,1,0:T(8,128)(2,1)} fusion(bf16[2,16,256]{2,1,0:T(8,128)(2,1)} %bitcast.19, bf16[27,16,256]{2,1,0:T(8,128)(2,1)} %param.18), kind=kLoop, calls=%fused_computation.5 | loop fusion | flops 118784 | bytes 475136 | tf_op jit(solution)/shard_map/concatenate | solution.py:295
  9.0 0.0 all-gather.5.cloned.1.call-update
  9.0 4.8 %collective-permute-start = (bf16[2,6,16,512]{3,2,1,0:T(8,128)(2,1)}, bf16[2,6,16,512]{3,2,1,0:T(8,128)(2,1)S(1)}, u32[]{:S(2)}, u32[]{:S(2)}) collective-permute-start(bf16[2,6,16,512]{3,2,1,0:T(8,128)(2,1)} %param.10), channel_id=1, source_target_pairs={{0,16},{16,32},{32,48},{48,64},{64,80},{80,96},{96,112},{112,128},... | collective-permute-start | bytes 589832 | tf_op jit(solution)/shard_map/ppermute | solution.py:22
  13.8 1.7 %shard_map.100 = f32[16,8,128]{2,1,0:T(8,128)} custom-call(bf16[192,512]{1,0:T(8,128)(2,1)} %bitcast.12), custom_call_target="tpu_custom_call" | custom-call | tf_op jit(solution)/shard_map/pallas_call | solution.py:309
  15.5 8.1 %all-to-all-start = ((f32[16,8,128]{2,1,0:T(8,128)}), f32[16,8,128]{2,1,0:T(8,128)S(1)}, u32[]{:S(2)}, u32[]{:S(2)}) async-start(f32[16,8,128]{2,1,0:T(8,128)} %shard_map.100), calls=%async_computation | async-start | bytes 131072 | tf_op jit(solution)/shard_map/all_to_all | solution.py:298
  23.6 0.9 slice.10
  24.5 0.0 collective-permute-done
  24.5 0.9 fusion.1
  25.4 6.0 %all-to-all-done.parts_ref = f32[16,8,128]{2,1,0:T(8,128)S(1)} async-done(((f32[16,8,128]{2,1,0:T(8,128)}), f32[16,8,128]{2,1,0:T(8,128)S(1)}, u32[]{:S(2)}, u32[]{:S(2)}) %all-to-all-start) | async-done | bytes 65568 | tf_op jit(solution)/shard_map/all_to_all | solution.py:298
  31.4 0.0 copy-start.9
  31.4 2.1 %collective-permute-start.1 = (bf16[4,2,16,512]{3,2,1,0:T(8,128)(2,1)S(1)}, bf16[4,2,16,512]{3,2,1,0:T(8,128)(2,1)S(1)}, u32[]{:S(2)}, u32[]{:S(2)}) collective-permute-start(bf16[4,2,16,512]{3,2,1,0:T(8,128)(2,1)S(1)} %get-tuple-element.13), channel_id=1, source_target_pairs={{0,2},{2,4},{4,6},{6,8},{8,10},{10,12},{12,14},{1,3},{3,5},{5,7},{... | collective-permute-start | bytes 393224 | tf_op jit(solution)/shard_map/ppermute | solution.py:22
  33.5 1.3 %collective-permute-start.2 = (bf16[4,2,16,512]{3,2,1,0:T(8,128)(2,1)S(1)}, bf16[4,2,16,512]{3,2,1,0:T(8,128)(2,1)S(1)}, u32[]{:S(2)}, u32[]{:S(2)}) collective-permute-start(bf16[4,2,16,512]{3,2,1,0:T(8,128)(2,1)S(1)} %get-tuple-element.14), channel_id=1, source_target_pairs={{2,0},{4,2},{6,4},{8,6},{10,8},{12,10},{14,12},{3,1},{5,3},{7,5},{... | collective-permute-start | bytes 393224 | tf_op jit(solution)/shard_map/ppermute | solution.py:22
  34.8 0.0 copy-done.9
  34.8 1.5 %shard_map.101 = f32[32,8,128]{2,1,0:T(8,128)} custom-call(f32[16,8,128]{2,1,0:T(8,128)} %copy-done.9), custom_call_target="tpu_custom_call" | custom-call | tf_op jit(solution)/shard_map/pallas_call | solution.py:301
  36.4 12.0 %all-to-all-start.1 = ((f32[32,8,128]{2,1,0:T(8,128)}), f32[32,8,128]{2,1,0:T(8,128)S(1)}, u32[]{:S(2)}, u32[]{:S(2)}) async-start(f32[32,8,128]{2,1,0:T(8,128)} %shard_map.101), calls=%async_computation.1 | async-start | bytes 262144 | tf_op jit(solution)/shard_map/all_to_all | solution.py:307
  48.4 0.1 pad_add_fusion.place_ref
  48.4 1.0 pad_maximum_fusion.centre_ref
  49.4 0.0 collective-permute-done.1.above_ref
  49.4 0.0 collective-permute-done.2.below_ref
  49.4 0.8 shard_map.102
  50.3 2.7 %collective-permute-start.3 = (bf16[4,2,16,512]{3,2,1,0:T(8,128)(2,1)S(1)}, bf16[4,2,16,512]{3,2,1,0:T(8,128)(2,1)S(1)}, u32[]{:S(2)}, u32[]{:S(2)}) collective-permute-start(bf16[4,2,16,512]{3,2,1,0:T(8,128)(2,1)S(1)} %shard_map.102), channel_id=1, source_target_pairs={{0,1},{1,0},{2,3},{3,2},{4,5},{5,4},{6,7},{7,6},{8,9},{9,8},{10,11... | collective-permute-start | bytes 393224 | tf_op jit(solution)/shard_map/ppermute | solution.py:26
  53.0 4.5 %all-to-all-done.1.parts_ref = f32[32,8,128]{2,1,0:T(8,128)S(1)} async-done(((f32[32,8,128]{2,1,0:T(8,128)}), f32[32,8,128]{2,1,0:T(8,128)S(1)}, u32[]{:S(2)}, u32[]{:S(2)}) %all-to-all-start.1) | async-done | bytes 131104 | tf_op jit(solution)/shard_map/all_to_all | solution.py:307
  57.5 0.0 collective-permute-done.3.border_ref
  57.5 0.0 copy-done.4
  57.5 0.0 copy-done.5
  57.5 2.7 %shard_map.103.copies_ref = bf16[6,640,512]{2,1,0:T(8,128)(2,1)S(1)} custom-call(s32[3]{0:T(128)S(1)} %pad_add_fusion.place_ref, f32[32,8,128]{2,1,0:T(8,128)S(1)} %all-to-all-done.1.parts_ref, f32[1,512]{1,0:T(1,128)S(1)} %bitcast.14, f32[1,512]{1,0:T(1,128)S(1)} %bitcast.15, bf16[4,6,16,512]{3,2,1,0:T(8,128)(2,1)S(1)} %pad_maximum_fusion.centre_ref, ...), custom_call_target="tpu_custom_call" | custom-call | tf_op jit(solution)/shard_map/pallas_call | solution.py:334
  60.3 0.0 copy-start
  60.3 2.0 %copy-done = bf16[6,640,512]{2,1,0:T(8,128)(2,1)} copy-done((bf16[6,640,512]{2,1,0:T(8,128)(2,1)}, bf16[6,640,512]{2,1,0:T(8,128)(2,1)S(1)}, u32[]{:S(2)}) %copy-start) | copy-done | bytes 3932184
  62.3 7.4 %all-gather.3.cloned.1.call-done.gathered_ref = bf16[27,512,256]{2,1,0:T(8,128)(2,1)} async-done(((bf16[27,32,256]{2,1,0:T(8,128)(2,1)}), bf16[27,512,256]{2,1,0:T(8,128)(2,1)}) %all-gather.3.cloned.1.call-update) | async-done | bytes 7077904 | tf_op jit(solution)/shard_map/all_gather | solution.py:292
  69.7 0.0 copy-start.6
  69.7 0.0 copy-start.7
  69.7 0.0 copy-start.1
  69.7 0.0 copy-start.8
  69.7 7.5 %shard_map.104 = (f32[288,256]{1,0:T(8,128)}, f32[16,8,128]{2,1,0:T(8,128)}) custom-call(f32[1,256]{1,0:T(1,128)} %bitcast.20, bf16[6,640,512]{2,1,0:T(8,128)(2,1)} %copy-done, bf16[27,512,256]{2,1,0:T(8,128)(2,1)} %all-gather.3.cloned.1.call-done.gathered_ref), custom_call_target="tpu_custom_call" | custom-call | tf_op jit(solution)/shard_map/pallas_call | solution.py:343
  77.3 5.3 %all-to-all-start.2 = ((f32[16,8,128]{2,1,0:T(8,128)}), f32[16,8,128]{2,1,0:T(8,128)S(1)}, u32[]{:S(2)}, u32[]{:S(2)}) async-start(f32[16,8,128]{2,1,0:T(8,128)} %get-tuple-element.15), calls=%async_computation.2 | async-start | bytes 131072 | tf_op jit(solution)/shard_map/all_to_all | solution.py:298
  82.6 3.3 %collective-permute-start.4 = (f32[288,256]{1,0:T(8,128)}, f32[288,256]{1,0:T(8,128)S(1)}, u32[]{:S(2)}, u32[]{:S(2)}) collective-permute-start(f32[288,256]{1,0:T(8,128)} %get-tuple-element.16.middle_ref), channel_id=1, source_target_pairs={{0,16},{16,32},{32,48},{48,64},{64,80},{80,96},{96,112},{112,128},... | collective-permute-start | bytes 884744 | tf_op jit(solution)/shard_map/ppermute | solution.py:22
  85.9 4.5 %all-to-all-done.2.parts_ref = f32[16,8,128]{2,1,0:T(8,128)S(1)} async-done(((f32[16,8,128]{2,1,0:T(8,128)}), f32[16,8,128]{2,1,0:T(8,128)S(1)}, u32[]{:S(2)}, u32[]{:S(2)}) %all-to-all-start.2) | async-done | bytes 65568 | tf_op jit(solution)/shard_map/all_to_all | solution.py:298
  90.5 0.0 copy-start.10
  90.5 0.6 copy-done.10
  91.1 1.5 %shard_map.105 = f32[32,8,128]{2,1,0:T(8,128)} custom-call(f32[16,8,128]{2,1,0:T(8,128)} %copy-done.10), custom_call_target="tpu_custom_call" | custom-call | tf_op jit(solution)/shard_map/pallas_call | solution.py:301
  92.6 9.9 %all-to-all-start.3 = ((f32[32,8,128]{2,1,0:T(8,128)}), f32[32,8,128]{2,1,0:T(8,128)S(1)}, u32[]{:S(2)}, u32[]{:S(2)}) async-start(f32[32,8,128]{2,1,0:T(8,128)} %shard_map.105), calls=%async_computation.3 | async-start | bytes 262144 | tf_op jit(solution)/shard_map/all_to_all | solution.py:307
  102.5 0.0 collective-permute-done.4.earlier_ref
  102.5 9.1 %all-to-all-done.3.parts_ref = f32[32,8,128]{2,1,0:T(8,128)S(1)} async-done(((f32[32,8,128]{2,1,0:T(8,128)}), f32[32,8,128]{2,1,0:T(8,128)S(1)}, u32[]{:S(2)}, u32[]{:S(2)}) %all-to-all-start.3) | async-done | bytes 131104 | tf_op jit(solution)/shard_map/all_to_all | solution.py:307
  111.7 0.0 copy-done.6
  111.7 0.0 copy-done.7
  111.7 0.0 copy-start.3
  111.7 1.0 copy-done.3
  112.7 1.4 %shard_map.106.copies = bf16[6,576,256]{2,1,0:T(8,128)(2,1)S(1)} custom-call(s32[3]{0:T(128)S(1)} %pad_add_fusion.place_ref, f32[32,8,128]{2,1,0:T(8,128)S(1)} %all-to-all-done.3.parts_ref, f32[1,256]{1,0:T(1,128)S(1)} %bitcast.16, f32[1,256]{1,0:T(1,128)S(1)} %bitcast.17, f32[288,256]{1,0:T(8,128)S(1)} %collective-permute-done.4.earlier_ref, ...), custom_call_target="tpu_custom_call" | custom-call | tf_op jit(solution)/shard_map/pallas_call | solution.py:362
  114.0 1.9 %all-gather.5.cloned.1.call-done.weight_ref = bf16[29,256,256]{2,1,0:T(8,128)(2,1)} async-done(((bf16[29,16,256]{2,1,0:T(8,128)(2,1)}), bf16[29,256,256]{2,1,0:T(8,128)(2,1)}) %all-gather.5.cloned.1.call-update) | async-done | bytes 3801104 | tf_op jit(solution)/shard_map/all_gather | solution.py:295
  115.9 0.0 copy-done.1
  115.9 0.0 copy-done.8
  115.9 0.0 copy-start.2
  115.9 2.1 %copy-done.2 = bf16[29,256,256]{2,1,0:T(8,128)(2,1)S(1)} copy-done((bf16[29,256,256]{2,1,0:T(8,128)(2,1)S(1)}, bf16[29,256,256]{2,1,0:T(8,128)(2,1)}, u32[]{:S(2)}) %copy-start.2) | copy-done | bytes 3801112
  118.0 1.8 %shard_map.107 = bf16[192,256]{1,0:T(8,128)(2,1)} custom-call(bf16[6,576,256]{2,1,0:T(8,128)(2,1)S(1)} %shard_map.106.copies, f32[1,256]{1,0:T(1,128)S(1)} %bitcast.18, bf16[192,512]{1,0:T(8,128)(2,1)S(1)} %bitcast.13, bf16[29,256,256]{2,1,0:T(8,128)(2,1)S(1)} %copy-done.2), custom_call_target="tpu_custom_call" | custom-call | tf_op jit(solution)/shard_map/pallas_call | solution.py:371
  (1 shorter events, 0.0 us)
Async XLA Ops:
  6.5 51.0 %copy-start.4 = (f32[512]{0:T(512)S(1)}, f32[512]{0:T(512)}, u32[]{:S(2)}) copy-start(f32[512]{0:T(512)} %param.11) | copy-start | bytes 6148
  6.5 51.0 %copy-start.5 = (f32[512]{0:T(512)S(1)}, f32[512]{0:T(512)}, u32[]{:S(2)}) copy-start(f32[512]{0:T(512)} %param.12) | copy-start | bytes 6148
  6.5 63.2 %all-gather.3.cloned.1.call-start = ((), (), s32[]{:S(2)}) async-start(), calls=%async_computation.4 | async-start | bytes 7520256 | tf_op jit(solution)/shard_map/all_gather | solution.py:292
  7.3 108.6 %all-gather.5.cloned.1.call-start = ((), (), s32[]{:S(2)}) async-start(), calls=%async_computation.5 | async-start | bytes 4038656 | tf_op jit(solution)/shard_map/all_gather | solution.py:295
  9.0 15.5 %collective-permute-start = (bf16[2,6,16,512]{3,2,1,0:T(8,128)(2,1)}, bf16[2,6,16,512]{3,2,1,0:T(8,128)(2,1)S(1)}, u32[]{:S(2)}, u32[]{:S(2)}) collective-permute-start(bf16[2,6,16,512]{3,2,1,0:T(8,128)(2,1)} %param.10), channel_id=1, source_target_pairs={{0,16},{16,32},{32,48},{48,64},{64,80},{80,96},{96,112},{112,128},... | collective-permute-start | bytes 589832 | tf_op jit(solution)/shard_map/ppermute | solution.py:22
  15.5 15.9 %all-to-all-start = ((f32[16,8,128]{2,1,0:T(8,128)}), f32[16,8,128]{2,1,0:T(8,128)S(1)}, u32[]{:S(2)}, u32[]{:S(2)}) async-start(f32[16,8,128]{2,1,0:T(8,128)} %shard_map.100), calls=%async_computation | async-start | bytes 131072 | tf_op jit(solution)/shard_map/all_to_all | solution.py:298
  31.4 3.4 %copy-start.9 = (f32[16,8,128]{2,1,0:T(8,128)}, f32[16,8,128]{2,1,0:T(8,128)S(1)}, u32[]{:S(2)}) copy-start(f32[16,8,128]{2,1,0:T(8,128)S(1)} %all-to-all-done.parts_ref) | copy-start | bytes 196612
  31.4 18.0 %collective-permute-start.1 = (bf16[4,2,16,512]{3,2,1,0:T(8,128)(2,1)S(1)}, bf16[4,2,16,512]{3,2,1,0:T(8,128)(2,1)S(1)}, u32[]{:S(2)}, u32[]{:S(2)}) collective-permute-start(bf16[4,2,16,512]{3,2,1,0:T(8,128)(2,1)S(1)} %get-tuple-element.13), channel_id=1, source_target_pairs={{0,2},{2,4},{4,6},{6,8},{8,10},{10,12},{12,14},{1,3},{3,5},{5,7},{... | collective-permute-start | bytes 393224 | tf_op jit(solution)/shard_map/ppermute | solution.py:22
  33.5 15.9 %collective-permute-start.2 = (bf16[4,2,16,512]{3,2,1,0:T(8,128)(2,1)S(1)}, bf16[4,2,16,512]{3,2,1,0:T(8,128)(2,1)S(1)}, u32[]{:S(2)}, u32[]{:S(2)}) collective-permute-start(bf16[4,2,16,512]{3,2,1,0:T(8,128)(2,1)S(1)} %get-tuple-element.14), channel_id=1, source_target_pairs={{2,0},{4,2},{6,4},{8,6},{10,8},{12,10},{14,12},{3,1},{5,3},{7,5},{... | collective-permute-start | bytes 393224 | tf_op jit(solution)/shard_map/ppermute | solution.py:22
  36.4 21.2 %all-to-all-start.1 = ((f32[32,8,128]{2,1,0:T(8,128)}), f32[32,8,128]{2,1,0:T(8,128)S(1)}, u32[]{:S(2)}, u32[]{:S(2)}) async-start(f32[32,8,128]{2,1,0:T(8,128)} %shard_map.101), calls=%async_computation.1 | async-start | bytes 262144 | tf_op jit(solution)/shard_map/all_to_all | solution.py:307
  50.3 7.3 %collective-permute-start.3 = (bf16[4,2,16,512]{3,2,1,0:T(8,128)(2,1)S(1)}, bf16[4,2,16,512]{3,2,1,0:T(8,128)(2,1)S(1)}, u32[]{:S(2)}, u32[]{:S(2)}) collective-permute-start(bf16[4,2,16,512]{3,2,1,0:T(8,128)(2,1)S(1)} %shard_map.102), channel_id=1, source_target_pairs={{0,1},{1,0},{2,3},{3,2},{4,5},{5,4},{6,7},{7,6},{8,9},{9,8},{10,11... | collective-permute-start | bytes 393224 | tf_op jit(solution)/shard_map/ppermute | solution.py:26
  60.3 2.0 %copy-start = (bf16[6,640,512]{2,1,0:T(8,128)(2,1)}, bf16[6,640,512]{2,1,0:T(8,128)(2,1)S(1)}, u32[]{:S(2)}) copy-start(bf16[6,640,512]{2,1,0:T(8,128)(2,1)S(1)} %shard_map.103.copies_ref) | copy-start | bytes 11796484
  69.7 42.0 %copy-start.6 = (f32[256]{0:T(256)S(1)}, f32[256]{0:T(256)}, u32[]{:S(2)}) copy-start(f32[256]{0:T(256)} %param.16) | copy-start | bytes 3076
  69.7 42.0 %copy-start.7 = (f32[256]{0:T(256)S(1)}, f32[256]{0:T(256)}, u32[]{:S(2)}) copy-start(f32[256]{0:T(256)} %param.17) | copy-start | bytes 3076
  69.7 46.2 %copy-start.1 = (bf16[2,6,16,512]{3,2,1,0:T(8,128)(2,1)S(1)}, bf16[2,6,16,512]{3,2,1,0:T(8,128)(2,1)}, u32[]{:S(2)}) copy-start(bf16[2,6,16,512]{3,2,1,0:T(8,128)(2,1)} %param.10) | copy-start | bytes 589828
  69.7 46.2 %copy-start.8 = (f32[256]{0:T(256)S(1)}, f32[256]{0:T(256)}, u32[]{:S(2)}) copy-start(f32[256]{0:T(256)} %param.19) | copy-start | bytes 3076
  77.3 13.2 %all-to-all-start.2 = ((f32[16,8,128]{2,1,0:T(8,128)}), f32[16,8,128]{2,1,0:T(8,128)S(1)}, u32[]{:S(2)}, u32[]{:S(2)}) async-start(f32[16,8,128]{2,1,0:T(8,128)} %get-tuple-element.15), calls=%async_computation.2 | async-start | bytes 131072 | tf_op jit(solution)/shard_map/all_to_all | solution.py:298
  82.6 19.9 %collective-permute-start.4 = (f32[288,256]{1,0:T(8,128)}, f32[288,256]{1,0:T(8,128)S(1)}, u32[]{:S(2)}, u32[]{:S(2)}) collective-permute-start(f32[288,256]{1,0:T(8,128)} %get-tuple-element.16.middle_ref), channel_id=1, source_target_pairs={{0,16},{16,32},{32,48},{48,64},{64,80},{80,96},{96,112},{112,128},... | collective-permute-start | bytes 884744 | tf_op jit(solution)/shard_map/ppermute | solution.py:22
  90.5 0.6 copy-start.10
  92.6 19.1 %all-to-all-start.3 = ((f32[32,8,128]{2,1,0:T(8,128)}), f32[32,8,128]{2,1,0:T(8,128)S(1)}, u32[]{:S(2)}, u32[]{:S(2)}) async-start(f32[32,8,128]{2,1,0:T(8,128)} %shard_map.105), calls=%async_computation.3 | async-start | bytes 262144 | tf_op jit(solution)/shard_map/all_to_all | solution.py:307
  111.7 1.0 copy-start.3
  115.9 2.1 %copy-start.2 = (bf16[29,256,256]{2,1,0:T(8,128)(2,1)S(1)}, bf16[29,256,256]{2,1,0:T(8,128)(2,1)}, u32[]{:S(2)}) copy-start(bf16[29,256,256]{2,1,0:T(8,128)(2,1)} %all-gather.5.cloned.1.call-done.weight_ref) | copy-start | bytes 11403268
Sparse Core Ops, SparseCore 0:
  9.5 60.1 all-gather.2
  71.9 43.9 all-gather.4

commit v5 on v4

--- a/solution.py
+++ b/solution.py
@@ -326,7 +326,7 @@
         out_shape=jax.ShapeDtypeStruct((volume.shape[0], 2, 16, chans_in), jnp.bfloat16),
         in_specs=[pl.BlockSpec(memory_space=SMEM)] + [whole()] * 3,
         out_specs=whole(),
-        scratch_shapes=[VMEM((chans_in // 128, 256, 128), jnp.float32)],
+        scratch_shapes=[VMEM((chans_in // 128, 288, 128), jnp.float32)],
         compiler_params=pltpu.CompilerParams(vmem_limit_bytes=16 * MIB),
     )(place, volume, above, below)
     border = swapped(border, "col")
@@ -336,7 +336,7 @@
         out_shape=jax.ShapeDtypeStruct((6, 640, chans_in), jnp.bfloat16),
         in_specs=[pl.BlockSpec(memory_space=SMEM)] + [whole()] * 7,
         out_specs=whole(),
-        scratch_shapes=[VMEM((chans_in // 128, 160, 128), jnp.float32), VMEM((32, chans_in), jnp.float32)],
+        scratch_shapes=[VMEM((chans_in // 128, 192, 128), jnp.float32), VMEM((32, chans_in), jnp.float32)],
         compiler_params=pltpu.CompilerParams(vmem_limit_bytes=24 * MIB),
     )(place, parts, gn1_gain[None], gn1_bias[None], volume, above, below, border)
 
@@ -373,7 +373,7 @@
         out_shape=jax.ShapeDtypeStruct((positions, chans_out), jnp.bfloat16),
         in_specs=[whole()] * 4,
         out_specs=whole(),
-        scratch_shapes=[VMEM((chans_out // 128, 256, 128), jnp.float32)],
+        scratch_shapes=[VMEM((chans_out // 128, 272, 128), jnp.float32)],
         compiler_params=pltpu.CompilerParams(vmem_limit_bytes=24 * MIB),
     )(copies, conv2_bias[None], flat_features, second)
     return out.reshape(frames, rows, cols, chans_out)

time: 127 us -> 127 us (level)
  no operation moved by 1% of the time
where the time goes in v5:
time: 127 us
  starting transfers between devices  49.6 us (39%)
  waiting for transfers between devices  34.2 us (27%)
  Pallas kernels  19 us (15%)
  between operations  13.6 us (11%)
  local copies, waits for them, and re-layouts  6.59 us (5%)
  other arithmetic  3.64 us (3%)
    all_to_all x2, starting transfers between devices, shared(): return (lax.all_to_all(stats, TM, 0, 0, tiled=True), beside)  21.9 us
    all_to_all x2, waiting for transfers between devices, shared(): return (lax.all_to_all(stats, TM, 0, 0, tiled=True), beside)  13.7 us
    all_to_all x2, starting transfers between devices, shared(): stats = lax.all_to_all(stats, ('row', 'col'), 0, 0, tiled=True)  13.4 us
    ppermute x4, starting transfers between devices, moved(): return lax.ppermute(block, axis, route)  11.5 us
    all_to_all x2, waiting for transfers between devices, shared(): stats = lax.all_to_all(stats, ('row', 'col'), 0, 0, tiled=True)  10.5 us
    pallas_call x1, Pallas kernels, per_device(): pl.pallas_call(functools.partial(conv1_kernel, float(positions)), out_sha...  7.55 us
    all_gather x1, waiting for transfers between devices, per_device(): first = lax.all_gather(conv1_weight, ('row', 'col'), axis=1, tiled=True)  7.42 us
    unnamed x22, local copies, waits for them, and re-layouts  5.69 us
  transfers between devices with their start and end apart: 11, of which 6 were waited for; matrix products, arithmetic and copies ran while one was open for 4% of the time, Pallas kernels for 14%

profile of v5, /device:TPU:1, one launch (start us, length us, event | category | flops | bytes accessed | tf_op | source)
XLA Modules:
  0.0 126.6 jit_solution(11860666085881967763)
XLA Ops:
  6.5 0.0 copy-start.4
  6.5 0.0 copy-start.5
  6.5 0.0 all-gather.3.cloned.1.call-start
  6.5 0.7 all-gather.3.cloned.1.call-update
  7.3 0.0 all-gather.5.cloned.1.call-start
  7.3 1.7 %pad_maximum_fusion.1 = bf16[29,16,256]{2,1,0:T(8,128)(2,1)} fusion(bf16[2,16,256]{2,1,0:T(8,128)(2,1)} %bitcast.19, bf16[27,16,256]{2,1,0:T(8,128)(2,1)} %param.18), kind=kLoop, calls=%fused_computation.5 | loop fusion | flops 118784 | bytes 475136 | tf_op jit(solution)/shard_map/concatenate | solution.py:295
  9.0 0.0 all-gather.5.cloned.1.call-update
  9.0 4.8 %collective-permute-start = (bf16[2,6,16,512]{3,2,1,0:T(8,128)(2,1)}, bf16[2,6,16,512]{3,2,1,0:T(8,128)(2,1)S(1)}, u32[]{:S(2)}, u32[]{:S(2)}) collective-permute-start(bf16[2,6,16,512]{3,2,1,0:T(8,128)(2,1)} %param.10), channel_id=1, source_target_pairs={{0,16},{16,32},{32,48},{48,64},{64,80},{80,96},{96,112},{112,128},... | collective-permute-start | bytes 589832 | tf_op jit(solution)/shard_map/ppermute | solution.py:22
  13.8 1.7 %shard_map.100 = f32[16,8,128]{2,1,0:T(8,128)} custom-call(bf16[192,512]{1,0:T(8,128)(2,1)} %bitcast.12), custom_call_target="tpu_custom_call" | custom-call | tf_op jit(solution)/shard_map/pallas_call | solution.py:309
  15.5 8.1 %all-to-all-start = ((f32[16,8,128]{2,1,0:T(8,128)}), f32[16,8,128]{2,1,0:T(8,128)S(1)}, u32[]{:S(2)}, u32[]{:S(2)}) async-start(f32[16,8,128]{2,1,0:T(8,128)} %shard_map.100), calls=%async_computation | async-start | bytes 131072 | tf_op jit(solution)/shard_map/all_to_all | solution.py:298
  23.6 0.9 slice.10
  24.5 0.0 collective-permute-done
  24.5 0.9 fusion.1
  25.4 6.0 %all-to-all-done.parts_ref = f32[16,8,128]{2,1,0:T(8,128)S(1)} async-done(((f32[16,8,128]{2,1,0:T(8,128)}), f32[16,8,128]{2,1,0:T(8,128)S(1)}, u32[]{:S(2)}, u32[]{:S(2)}) %all-to-all-start) | async-done | bytes 65568 | tf_op jit(solution)/shard_map/all_to_all | solution.py:298
  31.4 0.0 copy-start.9
  31.4 2.1 %collective-permute-start.1 = (bf16[4,2,16,512]{3,2,1,0:T(8,128)(2,1)S(1)}, bf16[4,2,16,512]{3,2,1,0:T(8,128)(2,1)S(1)}, u32[]{:S(2)}, u32[]{:S(2)}) collective-permute-start(bf16[4,2,16,512]{3,2,1,0:T(8,128)(2,1)S(1)} %get-tuple-element.13), channel_id=1, source_target_pairs={{0,2},{2,4},{4,6},{6,8},{8,10},{10,12},{12,14},{1,3},{3,5},{5,7},{... | collective-permute-start | bytes 393224 | tf_op jit(solution)/shard_map/ppermute | solution.py:22
  33.5 1.3 %collective-permute-start.2 = (bf16[4,2,16,512]{3,2,1,0:T(8,128)(2,1)S(1)}, bf16[4,2,16,512]{3,2,1,0:T(8,128)(2,1)S(1)}, u32[]{:S(2)}, u32[]{:S(2)}) collective-permute-start(bf16[4,2,16,512]{3,2,1,0:T(8,128)(2,1)S(1)} %get-tuple-element.14), channel_id=1, source_target_pairs={{2,0},{4,2},{6,4},{8,6},{10,8},{12,10},{14,12},{3,1},{5,3},{7,5},{... | collective-permute-start | bytes 393224 | tf_op jit(solution)/shard_map/ppermute | solution.py:22
  34.8 0.0 copy-done.9
  34.8 1.5 %shard_map.101 = f32[32,8,128]{2,1,0:T(8,128)} custom-call(f32[16,8,128]{2,1,0:T(8,128)} %copy-done.9), custom_call_target="tpu_custom_call" | custom-call | tf_op jit(solution)/shard_map/pallas_call | solution.py:301
  36.4 12.0 %all-to-all-start.1 = ((f32[32,8,128]{2,1,0:T(8,128)}), f32[32,8,128]{2,1,0:T(8,128)S(1)}, u32[]{:S(2)}, u32[]{:S(2)}) async-start(f32[32,8,128]{2,1,0:T(8,128)} %shard_map.101), calls=%async_computation.1 | async-start | bytes 262144 | tf_op jit(solution)/shard_map/all_to_all | solution.py:307
  48.4 0.1 pad_add_fusion.place_ref
  48.4 1.0 pad_maximum_fusion.centre_ref
  49.4 0.0 collective-permute-done.1.above_ref
  49.4 0.0 collective-permute-done.2.below_ref
  49.4 0.8 shard_map.102
  50.3 2.7 %collective-permute-start.3 = (bf16[4,2,16,512]{3,2,1,0:T(8,128)(2,1)S(1)}, bf16[4,2,16,512]{3,2,1,0:T(8,128)(2,1)S(1)}, u32[]{:S(2)}, u32[]{:S(2)}) collective-permute-start(bf16[4,2,16,512]{3,2,1,0:T(8,128)(2,1)S(1)} %shard_map.102), channel_id=1, source_target_pairs={{0,1},{1,0},{2,3},{3,2},{4,5},{5,4},{6,7},{7,6},{8,9},{9,8},{10,11... | collective-permute-start | bytes 393224 | tf_op jit(solution)/shard_map/ppermute | solution.py:26
  53.0 4.5 %all-to-all-done.1.parts_ref = f32[32,8,128]{2,1,0:T(8,128)S(1)} async-done(((f32[32,8,128]{2,1,0:T(8,128)}), f32[32,8,128]{2,1,0:T(8,128)S(1)}, u32[]{:S(2)}, u32[]{:S(2)}) %all-to-all-start.1) | async-done | bytes 131104 | tf_op jit(solution)/shard_map/all_to_all | solution.py:307
  57.5 0.0 collective-permute-done.3.border_ref
  57.5 0.0 copy-done.4
  57.5 0.0 copy-done.5
  57.5 2.7 %shard_map.103.copies_ref = bf16[6,640,512]{2,1,0:T(8,128)(2,1)S(1)} custom-call(s32[3]{0:T(128)S(1)} %pad_add_fusion.place_ref, f32[32,8,128]{2,1,0:T(8,128)S(1)} %all-to-all-done.1.parts_ref, f32[1,512]{1,0:T(1,128)S(1)} %bitcast.14, f32[1,512]{1,0:T(1,128)S(1)} %bitcast.15, bf16[4,6,16,512]{3,2,1,0:T(8,128)(2,1)S(1)} %pad_maximum_fusion.centre_ref, ...), custom_call_target="tpu_custom_call" | custom-call | tf_op jit(solution)/shard_map/pallas_call | solution.py:334
  60.3 0.0 copy-start
  60.3 2.0 %copy-done = bf16[6,640,512]{2,1,0:T(8,128)(2,1)} copy-done((bf16[6,640,512]{2,1,0:T(8,128)(2,1)}, bf16[6,640,512]{2,1,0:T(8,128)(2,1)S(1)}, u32[]{:S(2)}) %copy-start) | copy-done | bytes 3932184
  62.3 7.4 %all-gather.3.cloned.1.call-done.gathered_ref = bf16[27,512,256]{2,1,0:T(8,128)(2,1)} async-done(((bf16[27,32,256]{2,1,0:T(8,128)(2,1)}), bf16[27,512,256]{2,1,0:T(8,128)(2,1)}) %all-gather.3.cloned.1.call-update) | async-done | bytes 7077904 | tf_op jit(solution)/shard_map/all_gather | solution.py:292
  69.7 0.0 copy-start.6
  69.7 0.0 copy-start.7
  69.7 0.0 copy-start.1
  69.7 0.0 copy-start.8
  69.7 7.5 %shard_map.104 = (f32[288,256]{1,0:T(8,128)}, f32[16,8,128]{2,1,0:T(8,128)}) custom-call(f32[1,256]{1,0:T(1,128)} %bitcast.20, bf16[6,640,512]{2,1,0:T(8,128)(2,1)} %copy-done, bf16[27,512,256]{2,1,0:T(8,128)(2,1)} %all-gather.3.cloned.1.call-done.gathered_ref), custom_call_target="tpu_custom_call" | custom-call | tf_op jit(solution)/shard_map/pallas_call | solution.py:343
  77.3 5.3 %all-to-all-start.2 = ((f32[16,8,128]{2,1,0:T(8,128)}), f32[16,8,128]{2,1,0:T(8,128)S(1)}, u32[]{:S(2)}, u32[]{:S(2)}) async-start(f32[16,8,128]{2,1,0:T(8,128)} %get-tuple-element.15), calls=%async_computation.2 | async-start | bytes 131072 | tf_op jit(solution)/shard_map/all_to_all | solution.py:298
  82.6 3.3 %collective-permute-start.4 = (f32[288,256]{1,0:T(8,128)}, f32[288,256]{1,0:T(8,128)S(1)}, u32[]{:S(2)}, u32[]{:S(2)}) collective-permute-start(f32[288,256]{1,0:T(8,128)} %get-tuple-element.16.middle_ref), channel_id=1, source_target_pairs={{0,16},{16,32},{32,48},{48,64},{64,80},{80,96},{96,112},{112,128},... | collective-permute-start | bytes 884744 | tf_op jit(solution)/shard_map/ppermute | solution.py:22
  85.9 4.5 %all-to-all-done.2.parts_ref = f32[16,8,128]{2,1,0:T(8,128)S(1)} async-done(((f32[16,8,128]{2,1,0:T(8,128)}), f32[16,8,128]{2,1,0:T(8,128)S(1)}, u32[]{:S(2)}, u32[]{:S(2)}) %all-to-all-start.2) | async-done | bytes 65568 | tf_op jit(solution)/shard_map/all_to_all | solution.py:298
  90.5 0.0 copy-start.10
  90.5 0.6 copy-done.10
  91.1 1.5 %shard_map.105 = f32[32,8,128]{2,1,0:T(8,128)} custom-call(f32[16,8,128]{2,1,0:T(8,128)} %copy-done.10), custom_call_target="tpu_custom_call" | custom-call | tf_op jit(solution)/shard_map/pallas_call | solution.py:301
  92.6 9.9 %all-to-all-start.3 = ((f32[32,8,128]{2,1,0:T(8,128)}), f32[32,8,128]{2,1,0:T(8,128)S(1)}, u32[]{:S(2)}, u32[]{:S(2)}) async-start(f32[32,8,128]{2,1,0:T(8,128)} %shard_map.105), calls=%async_computation.3 | async-start | bytes 262144 | tf_op jit(solution)/shard_map/all_to_all | solution.py:307
  102.5 0.0 collective-permute-done.4.earlier_ref
  102.5 9.1 %all-to-all-done.3.parts_ref = f32[32,8,128]{2,1,0:T(8,128)S(1)} async-done(((f32[32,8,128]{2,1,0:T(8,128)}), f32[32,8,128]{2,1,0:T(8,128)S(1)}, u32[]{:S(2)}, u32[]{:S(2)}) %all-to-all-start.3) | async-done | bytes 131104 | tf_op jit(solution)/shard_map/all_to_all | solution.py:307
  111.7 0.0 copy-done.6
  111.7 0.0 copy-done.7
  111.7 0.0 copy-start.3
  111.7 1.0 copy-done.3
  112.7 1.4 %shard_map.106.copies = bf16[6,576,256]{2,1,0:T(8,128)(2,1)S(1)} custom-call(s32[3]{0:T(128)S(1)} %pad_add_fusion.place_ref, f32[32,8,128]{2,1,0:T(8,128)S(1)} %all-to-all-done.3.parts_ref, f32[1,256]{1,0:T(1,128)S(1)} %bitcast.16, f32[1,256]{1,0:T(1,128)S(1)} %bitcast.17, f32[288,256]{1,0:T(8,128)S(1)} %collective-permute-done.4.earlier_ref, ...), custom_call_target="tpu_custom_call" | custom-call | tf_op jit(solution)/shard_map/pallas_call | solution.py:362
  114.0 1.9 %all-gather.5.cloned.1.call-done.weight_ref = bf16[29,256,256]{2,1,0:T(8,128)(2,1)} async-done(((bf16[29,16,256]{2,1,0:T(8,128)(2,1)}), bf16[29,256,256]{2,1,0:T(8,128)(2,1)}) %all-gather.5.cloned.1.call-update) | async-done | bytes 3801104 | tf_op jit(solution)/shard_map/all_gather | solution.py:295
  115.9 0.0 copy-done.1
  115.9 0.0 copy-done.8
  115.9 0.0 copy-start.2
  115.9 2.1 %copy-done.2 = bf16[29,256,256]{2,1,0:T(8,128)(2,1)S(1)} copy-done((bf16[29,256,256]{2,1,0:T(8,128)(2,1)S(1)}, bf16[29,256,256]{2,1,0:T(8,128)(2,1)}, u32[]{:S(2)}) %copy-start.2) | copy-done | bytes 3801112
  118.0 1.8 %shard_map.107 = bf16[192,256]{1,0:T(8,128)(2,1)} custom-call(bf16[6,576,256]{2,1,0:T(8,128)(2,1)S(1)} %shard_map.106.copies, f32[1,256]{1,0:T(1,128)S(1)} %bitcast.18, bf16[192,512]{1,0:T(8,128)(2,1)S(1)} %bitcast.13, bf16[29,256,256]{2,1,0:T(8,128)(2,1)S(1)} %copy-done.2), custom_call_target="tpu_custom_call" | custom-call | tf_op jit(solution)/shard_map/pallas_call | solution.py:371
  (1 shorter events, 0.0 us)
Async XLA Ops:
  6.5 51.0 %copy-start.4 = (f32[512]{0:T(512)S(1)}, f32[512]{0:T(512)}, u32[]{:S(2)}) copy-start(f32[512]{0:T(512)} %param.11) | copy-start | bytes 6148
  6.5 51.0 %copy-start.5 = (f32[512]{0:T(512)S(1)}, f32[512]{0:T(512)}, u32[]{:S(2)}) copy-start(f32[512]{0:T(512)} %param.12) | copy-start | bytes 6148
  6.5 63.2 %all-gather.3.cloned.1.call-start = ((), (), s32[]{:S(2)}) async-start(), calls=%async_computation.4 | async-start | bytes 7520256 | tf_op jit(solution)/shard_map/all_gather | solution.py:292
  7.3 108.6 %all-gather.5.cloned.1.call-start = ((), (), s32[]{:S(2)}) async-start(), calls=%async_computation.5 | async-start | bytes 4038656 | tf_op jit(solution)/shard_map/all_gather | solution.py:295
  9.0 15.5 %collective-permute-start = (bf16[2,6,16,512]{3,2,1,0:T(8,128)(2,1)}, bf16[2,6,16,512]{3,2,1,0:T(8,128)(2,1)S(1)}, u32[]{:S(2)}, u32[]{:S(2)}) collective-permute-start(bf16[2,6,16,512]{3,2,1,0:T(8,128)(2,1)} %param.10), channel_id=1, source_target_pairs={{0,16},{16,32},{32,48},{48,64},{64,80},{80,96},{96,112},{112,128},... | collective-permute-start | bytes 589832 | tf_op jit(solution)/shard_map/ppermute | solution.py:22
  15.5 15.9 %all-to-all-start = ((f32[16,8,128]{2,1,0:T(8,128)}), f32[16,8,128]{2,1,0:T(8,128)S(1)}, u32[]{:S(2)}, u32[]{:S(2)}) async-start(f32[16,8,128]{2,1,0:T(8,128)} %shard_map.100), calls=%async_computation | async-start | bytes 131072 | tf_op jit(solution)/shard_map/all_to_all | solution.py:298
  31.4 3.4 %copy-start.9 = (f32[16,8,128]{2,1,0:T(8,128)}, f32[16,8,128]{2,1,0:T(8,128)S(1)}, u32[]{:S(2)}) copy-start(f32[16,8,128]{2,1,0:T(8,128)S(1)} %all-to-all-done.parts_ref) | copy-start | bytes 196612
  31.4 18.0 %collective-permute-start.1 = (bf16[4,2,16,512]{3,2,1,0:T(8,128)(2,1)S(1)}, bf16[4,2,16,512]{3,2,1,0:T(8,128)(2,1)S(1)}, u32[]{:S(2)}, u32[]{:S(2)}) collective-permute-start(bf16[4,2,16,512]{3,2,1,0:T(8,128)(2,1)S(1)} %get-tuple-element.13), channel_id=1, source_target_pairs={{0,2},{2,4},{4,6},{6,8},{8,10},{10,12},{12,14},{1,3},{3,5},{5,7},{... | collective-permute-start | bytes 393224 | tf_op jit(solution)/shard_map/ppermute | solution.py:22
  33.5 15.9 %collective-permute-start.2 = (bf16[4,2,16,512]{3,2,1,0:T(8,128)(2,1)S(1)}, bf16[4,2,16,512]{3,2,1,0:T(8,128)(2,1)S(1)}, u32[]{:S(2)}, u32[]{:S(2)}) collective-permute-start(bf16[4,2,16,512]{3,2,1,0:T(8,128)(2,1)S(1)} %get-tuple-element.14), channel_id=1, source_target_pairs={{2,0},{4,2},{6,4},{8,6},{10,8},{12,10},{14,12},{3,1},{5,3},{7,5},{... | collective-permute-start | bytes 393224 | tf_op jit(solution)/shard_map/ppermute | solution.py:22
  36.4 21.2 %all-to-all-start.1 = ((f32[32,8,128]{2,1,0:T(8,128)}), f32[32,8,128]{2,1,0:T(8,128)S(1)}, u32[]{:S(2)}, u32[]{:S(2)}) async-start(f32[32,8,128]{2,1,0:T(8,128)} %shard_map.101), calls=%async_computation.1 | async-start | bytes 262144 | tf_op jit(solution)/shard_map/all_to_all | solution.py:307
  50.3 7.3 %collective-permute-start.3 = (bf16[4,2,16,512]{3,2,1,0:T(8,128)(2,1)S(1)}, bf16[4,2,16,512]{3,2,1,0:T(8,128)(2,1)S(1)}, u32[]{:S(2)}, u32[]{:S(2)}) collective-permute-start(bf16[4,2,16,512]{3,2,1,0:T(8,128)(2,1)S(1)} %shard_map.102), channel_id=1, source_target_pairs={{0,1},{1,0},{2,3},{3,2},{4,5},{5,4},{6,7},{7,6},{8,9},{9,8},{10,11... | collective-permute-start | bytes 393224 | tf_op jit(solution)/shard_map/ppermute | solution.py:26
  60.3 2.0 %copy-start = (bf16[6,640,512]{2,1,0:T(8,128)(2,1)}, bf16[6,640,512]{2,1,0:T(8,128)(2,1)S(1)}, u32[]{:S(2)}) copy-start(bf16[6,640,512]{2,1,0:T(8,128)(2,1)S(1)} %shard_map.103.copies_ref) | copy-start | bytes 11796484
  69.7 42.0 %copy-start.6 = (f32[256]{0:T(256)S(1)}, f32[256]{0:T(256)}, u32[]{:S(2)}) copy-start(f32[256]{0:T(256)} %param.16) | copy-start | bytes 3076
  69.7 42.0 %copy-start.7 = (f32[256]{0:T(256)S(1)}, f32[256]{0:T(256)}, u32[]{:S(2)}) copy-start(f32[256]{0:T(256)} %param.17) | copy-start | bytes 3076
  69.7 46.2 %copy-start.1 = (bf16[2,6,16,512]{3,2,1,0:T(8,128)(2,1)S(1)}, bf16[2,6,16,512]{3,2,1,0:T(8,128)(2,1)}, u32[]{:S(2)}) copy-start(bf16[2,6,16,512]{3,2,1,0:T(8,128)(2,1)} %param.10) | copy-start | bytes 589828
  69.7 46.2 %copy-start.8 = (f32[256]{0:T(256)S(1)}, f32[256]{0:T(256)}, u32[]{:S(2)}) copy-start(f32[256]{0:T(256)} %param.19) | copy-start | bytes 3076
  77.3 13.2 %all-to-all-start.2 = ((f32[16,8,128]{2,1,0:T(8,128)}), f32[16,8,128]{2,1,0:T(8,128)S(1)}, u32[]{:S(2)}, u32[]{:S(2)}) async-start(f32[16,8,128]{2,1,0:T(8,128)} %get-tuple-element.15), calls=%async_computation.2 | async-start | bytes 131072 | tf_op jit(solution)/shard_map/all_to_all | solution.py:298
  82.6 19.9 %collective-permute-start.4 = (f32[288,256]{1,0:T(8,128)}, f32[288,256]{1,0:T(8,128)S(1)}, u32[]{:S(2)}, u32[]{:S(2)}) collective-permute-start(f32[288,256]{1,0:T(8,128)} %get-tuple-element.16.middle_ref), channel_id=1, source_target_pairs={{0,16},{16,32},{32,48},{48,64},{64,80},{80,96},{96,112},{112,128},... | collective-permute-start | bytes 884744 | tf_op jit(solution)/shard_map/ppermute | solution.py:22
  90.5 0.6 copy-start.10
  92.6 19.1 %all-to-all-start.3 = ((f32[32,8,128]{2,1,0:T(8,128)}), f32[32,8,128]{2,1,0:T(8,128)S(1)}, u32[]{:S(2)}, u32[]{:S(2)}) async-start(f32[32,8,128]{2,1,0:T(8,128)} %shard_map.105), calls=%async_computation.3 | async-start | bytes 262144 | tf_op jit(solution)/shard_map/all_to_all | solution.py:307
  111.7 1.0 copy-start.3
  115.9 2.1 %copy-start.2 = (bf16[29,256,256]{2,1,0:T(8,128)(2,1)S(1)}, bf16[29,256,256]{2,1,0:T(8,128)(2,1)}, u32[]{:S(2)}) copy-start(bf16[29,256,256]{2,1,0:T(8,128)(2,1)} %all-gather.5.cloned.1.call-done.weight_ref) | copy-start | bytes 11403268
Sparse Core Ops, SparseCore 0:
  9.5 60.1 all-gather.2
  71.9 43.9 all-gather.4

commit v6 on v5

--- a/solution.py
+++ b/solution.py
@@ -87,6 +87,12 @@
     return packed(mean, jnp.sum(off * off, axis=0, keepdims=True))
 
 
+def frame_row(earlier_ref, own_ref, tm, t, y):
+    if t < 2:
+        return jnp.where(tm == 0, own_ref[0, y], earlier_ref[t, y])
+    return own_ref[t - 2, y]
+
+
 def stats_kernel(x_ref, out_ref):
     values = x_ref[...].astype(jnp.float32)
     tile = channel_stats(values, None, float(values.shape[0]))
@@ -97,42 +103,31 @@
     out_ref[...] = jnp.broadcast_to(merged(parts_ref, count)[None], out_ref.shape)
 
 
-def border_kernel(place_ref, centre_ref, above_ref, below_ref, out_ref, plain):
-    row, col = place_ref[0], place_ref[1]
+def border_kernel(place_ref, earlier_ref, own_ref, out_ref, plain):
+    col, tm = place_ref[1], place_ref[2]
     pieces = plain.shape[0]
-
-    def put(y, block):
-        block = block.astype(jnp.float32)
-        for j in range(pieces):
-            plain[j, 16 * y : 16 * y + 16, :] = block[:, 128 * j : 128 * (j + 1)]
-
     plain[...] = jnp.zeros_like(plain)
-
-    def frame(t, _):
-        for y in range(2):
-            put(y, jnp.where(row == 0, centre_ref[t, 0], above_ref[t, y]))
-            put(y + 8, jnp.where(row == 7, centre_ref[t, 5], below_ref[t, y]))
-        for y in range(6):
-            put(y + 2, centre_ref[t, y])
+    for t in range(4):
+        for y in range(10):
+            block = frame_row(earlier_ref, own_ref, tm, t, y).astype(jnp.float32)
+            for j in range(pieces):
+                plain[j, 16 * y : 16 * y + 16, :] = block[:, 128 * j : 128 * (j + 1)]
 
         def column(x):
             return jnp.concatenate([plain[j, pl.ds(x, 16, stride=16), :] for j in range(pieces)], axis=1)
 
         for x in range(2):
             out_ref[t, x] = jnp.where(col == 0, column(14 + x), column(x)).astype(jnp.bfloat16)
-        return 0
-
-    lax.fori_loop(0, 4, frame, 0)
 
 
 def hidden1_kernel(
-    count, peers, place_ref, parts_ref, gain_ref, shift_ref, centre_ref, above_ref, below_ref, border_ref, out_ref, plain, side
+    count, peers, place_ref, parts_ref, gain_ref, shift_ref, earlier_ref, own_ref, border_ref, out_ref, plain, side
 ):
-    chans = centre_ref.shape[-1]
+    chans = own_ref.shape[-1]
     tile = merged(parts_ref, count)
     mean, scale = group_moments(tile, count * peers, chans // GROUPS, chans)
     gain, shift = gain_ref[...], shift_ref[...]
-    row, col = place_ref[0], place_ref[1]
+    col, tm = place_ref[1], place_ref[2]
 
     def normed(block):
         return silu_of(block.astype(jnp.float32), mean, scale, gain, shift)
@@ -141,13 +136,9 @@
         for j in range(chans // 128):
             plain[j, 16 * y : 16 * y + 16, :] = block[:, 128 * j : 128 * (j + 1)]
 
-    def frame(t, _):
-        own = [normed(centre_ref[t, y]) for y in range(6)]
-        for y in range(2):
-            put(y, jnp.where(row == 0, own[0], normed(above_ref[t, y])))
-            put(y + 8, jnp.where(row == 7, own[5], normed(below_ref[t, y])))
-        for y in range(6):
-            put(y + 2, own[y])
+    for t in range(4):
+        for y in range(10):
+            put(y, normed(frame_row(earlier_ref, own_ref, tm, t, y)))
         for x in range(2):
             side[pl.ds(16 * x, 16), :] = normed(border_ref[t, x])
         for dy in range(3):
@@ -161,15 +152,12 @@
             left = [jnp.where(col == 0, inner[0], o) for o in outer]
             right = [jnp.where(col == 0, o, inner[15]) for o in outer]
             columns = left + inner + right
-            base = pl.multiple_of(t * 160, 16)
+            base = t * 160
             for p in range(2):
                 for i in range(10 - p):
                     pair = jnp.concatenate([columns[2 * i + p], columns[2 * i + p + 1]], axis=0)
                     out_ref[2 * dy + p, pl.ds(base + 16 * i, 16), :] = pair.astype(jnp.bfloat16)
             out_ref[2 * dy + 1, pl.ds(base + 144, 16), :] = jnp.zeros((16, chans), jnp.bfloat16)
-        return 0
-
-    lax.fori_loop(0, 4, frame, 0)
 
 
 def conv1_kernel(count, bias_ref, copies_ref, gathered_ref, middle_ref, stats_ref, copies, weights, arrived):
@@ -312,33 +300,31 @@
         in_specs=[whole()],
         out_specs=whole(),
     )(flat_features)
-    earlier = moved(features, TM, 1)
-    first_twice = jnp.concatenate([features[:1], features[:1]], axis=0)
-    earlier = jnp.where(tm == 0, first_twice, earlier)
-    volume = jnp.concatenate([earlier, features], axis=0)
-
-    parts, (last, leading) = shared(stats, float(positions), (volume[:, -2:], volume[:, :2]))
-    above = moved(last, "row", 1)
-    below = moved(leading, "row", -1)
-
+    above = moved(features[:, -2:], "row", 1)
+    below = moved(features[:, :2], "row", -1)
+    parts, (above, below) = shared(stats, float(positions), (above, below))
+    above = jnp.where(row == 0, features[:, :1], above)
+    below = jnp.where(row == nrow - 1, features[:, -1:], below)
+    own = jnp.concatenate([above, features, below], axis=1)
+    earlier = moved(own, TM, 1)
     border = pl.pallas_call(
         border_kernel,
-        out_shape=jax.ShapeDtypeStruct((volume.shape[0], 2, 16, chans_in), jnp.bfloat16),
-        in_specs=[pl.BlockSpec(memory_space=SMEM)] + [whole()] * 3,
+        out_shape=jax.ShapeDtypeStruct((4, 2, 16, chans_in), jnp.bfloat16),
+        in_specs=[pl.BlockSpec(memory_space=SMEM)] + [whole()] * 2,
         out_specs=whole(),
         scratch_shapes=[VMEM((chans_in // 128, 288, 128), jnp.float32)],
         compiler_params=pltpu.CompilerParams(vmem_limit_bytes=16 * MIB),
-    )(place, volume, above, below)
+    )(place, earlier, own)
     border = swapped(border, "col")
 
     copies = pl.pallas_call(
         functools.partial(hidden1_kernel, float(positions * plane), ntm),
         out_shape=jax.ShapeDtypeStruct((6, 640, chans_in), jnp.bfloat16),
-        in_specs=[pl.BlockSpec(memory_space=SMEM)] + [whole()] * 7,
+        in_specs=[pl.BlockSpec(memory_space=SMEM)] + [whole()] * 6,
         out_specs=whole(),
         scratch_shapes=[VMEM((chans_in // 128, 192, 128), jnp.float32), VMEM((32, chans_in), jnp.float32)],
         compiler_params=pltpu.CompilerParams(vmem_limit_bytes=24 * MIB),
-    )(place, parts, gn1_gain[None], gn1_bias[None], volume, above, below, border)
+    )(place, parts, gn1_gain[None], gn1_bias[None], earlier, own, border)
 
     middle, stats = pl.pallas_call(
         functools.partial(conv1_kernel, float(positions)),

time: 127 us -> 126 us (level)
  waiting for transfers between devices: 34.2 us -> 29.6 us
  starting transfers between devices: 49.6 us -> 53.1 us
    all_gather x1, waiting for transfers between devices: 7.42 us -> 0.01 us  [per_device(): first = lax.all_gather(conv1_weight, ('row', 'col'), axis=1, tiled=True)]
    all_to_all x2, starting transfers between devices: 13.4 us -> 15.8 us  [shared(): stats = lax.all_to_all(stats, ('row', 'col'), 0, 0, tiled=True)]
    all_to_all x2, waiting for transfers between devices: 10.5 us -> 12.1 us  [shared(): stats = lax.all_to_all(stats, ('row', 'col'), 0, 0, tiled=True)]
  transfers between devices with their start and end apart: 11 -> 11, of which waited for: 6 -> 5; matrix products, arithmetic and copies ran while one was open for 4% -> 4% of each run, Pallas kernels for 14% -> 14%
where the time goes in v6:
time: 126 us; the launch traced here: 125 us
  starting transfers between devices  53.1 us (42%)
  waiting for transfers between devices  29.6 us (23%)
  Pallas kernels  18.9 us (15%)
  between operations  13.6 us (11%)
  local copies, waits for them, and re-layouts  7.37 us (6%)
  other arithmetic  2.75 us (2%)
    all_to_all x2, starting transfers between devices, shared(): return (lax.all_to_all(stats, TM, 0, 0, tiled=True), beside)  22 us
    all_to_all x2, starting transfers between devices, shared(): stats = lax.all_to_all(stats, ('row', 'col'), 0, 0, tiled=True)  15.8 us
    all_to_all x2, waiting for transfers between devices, shared(): return (lax.all_to_all(stats, TM, 0, 0, tiled=True), beside)  14.9 us
    ppermute x4, starting transfers between devices, moved(): return lax.ppermute(block, axis, route)  12.7 us
    all_to_all x2, waiting for transfers between devices, shared(): stats = lax.all_to_all(stats, ('row', 'col'), 0, 0, tiled=True)  12.1 us
    pallas_call x1, Pallas kernels, per_device(): pl.pallas_call(functools.partial(conv1_kernel, float(positions)), out_sha...  7.57 us
    unnamed x22, local copies, waits for them, and re-layouts  5.71 us
    pallas_call x2, Pallas kernels, shared(): pl.pallas_call(functools.partial(merge_kernel, count), out_shape=jax.Shap...  3.08 us
  transfers between devices with their start and end apart: 11, of which 5 were waited for; matrix products, arithmetic and copies ran while one was open for 4% of the time, Pallas kernels for 14%

profile of v6, /device:TPU:1, one launch (start us, length us, event | category | flops | bytes accessed | tf_op | source)
XLA Modules:
  0.0 125.2 jit_solution(13941343953785909626)
XLA Ops:
  6.5 0.0 copy-start.4
  6.5 0.0 copy-start.5
  6.5 0.0 all-gather.3.cloned.1.call-start
  6.5 0.7 all-gather.3.cloned.1.call-update
  7.3 0.0 all-gather.5.cloned.1.call-start
  7.3 1.7 %pad_maximum_fusion.1 = bf16[29,16,256]{2,1,0:T(8,128)(2,1)} fusion(bf16[2,16,256]{2,1,0:T(8,128)(2,1)} %bitcast.23, bf16[27,16,256]{2,1,0:T(8,128)(2,1)} %param.18), kind=kLoop, calls=%fused_computation.1 | loop fusion | flops 118784 | bytes 475136 | tf_op jit(solution)/shard_map/concatenate | solution.py:283
  9.0 0.0 all-gather.5.cloned.1.call-update
  9.0 0.9 fusion
  9.9 4.0 %collective-permute-start = (bf16[2,2,16,512]{3,2,1,0:T(8,128)(2,1)S(1)}, bf16[2,2,16,512]{3,2,1,0:T(8,128)(2,1)S(1)}, u32[]{:S(2)}, u32[]{:S(2)}) collective-permute-start(bf16[2,2,16,512]{3,2,1,0:T(8,128)(2,1)S(1)} %get-tuple-element.22), channel_id=1, source_target_pairs={{0,2},{2,4},{4,6},{6,8},{8,10},{10,12},{12,14},{1,3},{3,5},{5,7},{... | collective-permute-start | bytes 196616 | tf_op jit(solution)/shard_map/ppermute | solution.py:22
  13.9 1.3 %collective-permute-start.1 = (bf16[2,2,16,512]{3,2,1,0:T(8,128)(2,1)S(1)}, bf16[2,2,16,512]{3,2,1,0:T(8,128)(2,1)S(1)}, u32[]{:S(2)}, u32[]{:S(2)}) collective-permute-start(bf16[2,2,16,512]{3,2,1,0:T(8,128)(2,1)S(1)} %get-tuple-element.21), channel_id=1, source_target_pairs={{2,0},{4,2},{6,4},{8,6},{10,8},{12,10},{14,12},{3,1},{5,3},{7,5},{... | collective-permute-start | bytes 196616 | tf_op jit(solution)/shard_map/ppermute | solution.py:22
  15.2 1.7 %shard_map.100 = f32[16,8,128]{2,1,0:T(8,128)} custom-call(bf16[192,512]{1,0:T(8,128)(2,1)} %bitcast.16), custom_call_target="tpu_custom_call" | custom-call | tf_op jit(solution)/shard_map/pallas_call | solution.py:297
  16.9 10.3 %all-to-all-start = ((f32[16,8,128]{2,1,0:T(8,128)}), f32[16,8,128]{2,1,0:T(8,128)S(1)}, u32[]{:S(2)}, u32[]{:S(2)}) async-start(f32[16,8,128]{2,1,0:T(8,128)} %shard_map.100), calls=%async_computation | async-start | bytes 131072 | tf_op jit(solution)/shard_map/all_to_all | solution.py:286
  27.2 0.8 slice_bitcast_fusion.1
  28.0 0.0 collective-permute-done
  28.0 0.0 collective-permute-done.1
  28.0 7.1 %all-to-all-done.parts_ref = f32[16,8,128]{2,1,0:T(8,128)S(1)} async-done(((f32[16,8,128]{2,1,0:T(8,128)}), f32[16,8,128]{2,1,0:T(8,128)S(1)}, u32[]{:S(2)}, u32[]{:S(2)}) %all-to-all-start) | async-done | bytes 65568 | tf_op jit(solution)/shard_map/all_to_all | solution.py:286
  35.1 0.0 copy-start.9
  35.1 1.0 pad_maximum_fusion.own_ref
  36.1 4.6 %collective-permute-start.2 = (bf16[2,10,16,512]{3,2,1,0:T(8,128)(2,1)S(1)}, bf16[2,10,16,512]{3,2,1,0:T(8,128)(2,1)S(1)}, u32[]{:S(2)}, u32[]{:S(2)}) collective-permute-start(bf16[2,10,16,512]{3,2,1,0:T(8,128)(2,1)S(1)} %pad_maximum_fusion.own_ref), channel_id=1, source_target_pairs={{0,16},{16,32},{32,48},{48,64},{64,80},{80,96},{96,112},{112,128},... | collective-permute-start | bytes 983048 | tf_op jit(solution)/shard_map/ppermute | solution.py:22
  40.7 0.0 copy-done.9
  40.7 1.5 %shard_map.101 = f32[32,8,128]{2,1,0:T(8,128)} custom-call(f32[16,8,128]{2,1,0:T(8,128)} %copy-done.9), custom_call_target="tpu_custom_call" | custom-call | tf_op jit(solution)/shard_map/pallas_call | solution.py:289
  42.3 12.2 %all-to-all-start.1 = ((f32[32,8,128]{2,1,0:T(8,128)}), f32[32,8,128]{2,1,0:T(8,128)S(1)}, u32[]{:S(2)}, u32[]{:S(2)}) async-start(f32[32,8,128]{2,1,0:T(8,128)} %shard_map.101), calls=%async_computation.1 | async-start | bytes 262144 | tf_op jit(solution)/shard_map/all_to_all | solution.py:295
  54.4 0.1 pad_add_fusion.place_ref
  54.5 0.0 collective-permute-done.2.earlier_ref
  54.5 0.8 shard_map.102
  55.3 2.5 %collective-permute-start.3 = (bf16[4,2,16,512]{3,2,1,0:T(8,128)(2,1)S(1)}, bf16[4,2,16,512]{3,2,1,0:T(8,128)(2,1)S(1)}, u32[]{:S(2)}, u32[]{:S(2)}) collective-permute-start(bf16[4,2,16,512]{3,2,1,0:T(8,128)(2,1)S(1)} %shard_map.102), channel_id=1, source_target_pairs={{0,1},{1,0},{2,3},{3,2},{4,5},{5,4},{6,7},{7,6},{8,9},{9,8},{10,11... | collective-permute-start | bytes 393224 | tf_op jit(solution)/shard_map/ppermute | solution.py:26
  57.8 5.7 %all-to-all-done.1.parts_ref = f32[32,8,128]{2,1,0:T(8,128)S(1)} async-done(((f32[32,8,128]{2,1,0:T(8,128)}), f32[32,8,128]{2,1,0:T(8,128)S(1)}, u32[]{:S(2)}, u32[]{:S(2)}) %all-to-all-start.1) | async-done | bytes 131104 | tf_op jit(solution)/shard_map/all_to_all | solution.py:295
  63.6 0.0 collective-permute-done.3.border_ref
  63.6 0.0 copy-done.4
  63.6 0.0 copy-done.5
  63.6 2.6 %shard_map.103.copies_ref = bf16[6,640,512]{2,1,0:T(8,128)(2,1)S(1)} custom-call(s32[3]{0:T(128)S(1)} %pad_add_fusion.place_ref, f32[32,8,128]{2,1,0:T(8,128)S(1)} %all-to-all-done.1.parts_ref, f32[1,512]{1,0:T(1,128)S(1)} %bitcast.18, f32[1,512]{1,0:T(1,128)S(1)} %bitcast.19, bf16[2,10,16,512]{3,2,1,0:T(8,128)(2,1)S(1)} %collective-permute-done.2.earlier_ref, ...), custom_call_target="tpu_custom_call" | custom-call | tf_op jit(solution)/shard_map/pallas_call | solution.py:320
  66.2 0.0 copy-start
  66.2 2.0 %copy-done = bf16[6,640,512]{2,1,0:T(8,128)(2,1)} copy-done((bf16[6,640,512]{2,1,0:T(8,128)(2,1)}, bf16[6,640,512]{2,1,0:T(8,128)(2,1)S(1)}, u32[]{:S(2)}) %copy-start) | copy-done | bytes 3932184
  68.2 0.0 all-gather.3.cloned.1.call-done.gathered_ref
  68.2 0.0 copy-start.6
  68.2 0.0 copy-start.7
  68.2 0.0 copy-start.2
  68.2 0.0 copy-start.8
  68.2 7.6 %shard_map.104 = (f32[288,256]{1,0:T(8,128)}, f32[16,8,128]{2,1,0:T(8,128)}) custom-call(f32[1,256]{1,0:T(1,128)} %bitcast.24, bf16[6,640,512]{2,1,0:T(8,128)(2,1)} %copy-done, bf16[27,512,256]{2,1,0:T(8,128)(2,1)} %all-gather.3.cloned.1.call-done.gathered_ref), custom_call_target="tpu_custom_call" | custom-call | tf_op jit(solution)/shard_map/pallas_call | solution.py:329
  75.8 5.4 %all-to-all-start.2 = ((f32[16,8,128]{2,1,0:T(8,128)}), f32[16,8,128]{2,1,0:T(8,128)S(1)}, u32[]{:S(2)}, u32[]{:S(2)}) async-start(f32[16,8,128]{2,1,0:T(8,128)} %get-tuple-element.15), calls=%async_computation.2 | async-start | bytes 131072 | tf_op jit(solution)/shard_map/all_to_all | solution.py:286
  81.2 2.9 %collective-permute-start.4 = (f32[288,256]{1,0:T(8,128)}, f32[288,256]{1,0:T(8,128)S(1)}, u32[]{:S(2)}, u32[]{:S(2)}) collective-permute-start(f32[288,256]{1,0:T(8,128)} %get-tuple-element.16.middle_ref), channel_id=1, source_target_pairs={{0,16},{16,32},{32,48},{48,64},{64,80},{80,96},{96,112},{112,128},... | collective-permute-start | bytes 884744 | tf_op jit(solution)/shard_map/ppermute | solution.py:22
  84.1 5.0 %all-to-all-done.2.parts_ref = f32[16,8,128]{2,1,0:T(8,128)S(1)} async-done(((f32[16,8,128]{2,1,0:T(8,128)}), f32[16,8,128]{2,1,0:T(8,128)S(1)}, u32[]{:S(2)}, u32[]{:S(2)}) %all-to-all-start.2) | async-done | bytes 65568 | tf_op jit(solution)/shard_map/all_to_all | solution.py:286
  89.1 0.0 copy-start.10
  89.1 0.6 copy-done.10
  89.7 1.5 %shard_map.105 = f32[32,8,128]{2,1,0:T(8,128)} custom-call(f32[16,8,128]{2,1,0:T(8,128)} %copy-done.10), custom_call_target="tpu_custom_call" | custom-call | tf_op jit(solution)/shard_map/pallas_call | solution.py:289
  91.3 9.9 %all-to-all-start.3 = ((f32[32,8,128]{2,1,0:T(8,128)}), f32[32,8,128]{2,1,0:T(8,128)S(1)}, u32[]{:S(2)}, u32[]{:S(2)}) async-start(f32[32,8,128]{2,1,0:T(8,128)} %shard_map.105), calls=%async_computation.3 | async-start | bytes 262144 | tf_op jit(solution)/shard_map/all_to_all | solution.py:295
  101.1 0.0 collective-permute-done.4.earlier_ref
  101.1 9.1 %all-to-all-done.3.parts_ref = f32[32,8,128]{2,1,0:T(8,128)S(1)} async-done(((f32[32,8,128]{2,1,0:T(8,128)}), f32[32,8,128]{2,1,0:T(8,128)S(1)}, u32[]{:S(2)}, u32[]{:S(2)}) %all-to-all-start.3) | async-done | bytes 131104 | tf_op jit(solution)/shard_map/all_to_all | solution.py:295
  110.3 0.0 copy-done.6
  110.3 0.0 copy-done.7
  110.3 0.0 copy-start.3
  110.3 1.0 copy-done.3
  111.3 1.4 %shard_map.106.copies = bf16[6,576,256]{2,1,0:T(8,128)(2,1)S(1)} custom-call(s32[3]{0:T(128)S(1)} %pad_add_fusion.place_ref, f32[32,8,128]{2,1,0:T(8,128)S(1)} %all-to-all-done.3.parts_ref, f32[1,256]{1,0:T(1,128)S(1)} %bitcast.20, f32[1,256]{1,0:T(1,128)S(1)} %bitcast.21, f32[288,256]{1,0:T(8,128)S(1)} %collective-permute-done.4.earlier_ref, ...), custom_call_target="tpu_custom_call" | custom-call | tf_op jit(solution)/shard_map/pallas_call | solution.py:348
  112.6 1.9 %all-gather.5.cloned.1.call-done.weight_ref = bf16[29,256,256]{2,1,0:T(8,128)(2,1)} async-done(((bf16[29,16,256]{2,1,0:T(8,128)(2,1)}), bf16[29,256,256]{2,1,0:T(8,128)(2,1)}) %all-gather.5.cloned.1.call-update) | async-done | bytes 3801104 | tf_op jit(solution)/shard_map/all_gather | solution.py:283
  114.5 0.0 copy-done.2
  114.5 0.0 copy-done.8
  114.5 0.0 copy-start.1
  114.5 2.1 %copy-done.1 = bf16[29,256,256]{2,1,0:T(8,128)(2,1)S(1)} copy-done((bf16[29,256,256]{2,1,0:T(8,128)(2,1)S(1)}, bf16[29,256,256]{2,1,0:T(8,128)(2,1)}, u32[]{:S(2)}) %copy-start.1) | copy-done | bytes 3801112
  116.6 1.8 %shard_map.107 = bf16[192,256]{1,0:T(8,128)(2,1)} custom-call(bf16[6,576,256]{2,1,0:T(8,128)(2,1)S(1)} %shard_map.106.copies, f32[1,256]{1,0:T(1,128)S(1)} %bitcast.22, bf16[192,512]{1,0:T(8,128)(2,1)S(1)} %bitcast.17, bf16[29,256,256]{2,1,0:T(8,128)(2,1)S(1)} %copy-done.1), custom_call_target="tpu_custom_call" | custom-call | tf_op jit(solution)/shard_map/pallas_call | solution.py:357
  (1 shorter events, 0.0 us)
Async XLA Ops:
  6.5 57.1 %copy-start.4 = (f32[512]{0:T(512)S(1)}, f32[512]{0:T(512)}, u32[]{:S(2)}) copy-start(f32[512]{0:T(512)} %param.11) | copy-start | bytes 6148
  6.5 57.1 %copy-start.5 = (f32[512]{0:T(512)S(1)}, f32[512]{0:T(512)}, u32[]{:S(2)}) copy-start(f32[512]{0:T(512)} %param.12) | copy-start | bytes 6148
  6.5 61.7 %all-gather.3.cloned.1.call-start = ((), (), s32[]{:S(2)}) async-start(), calls=%async_computation.4 | async-start | bytes 7520256 | tf_op jit(solution)/shard_map/all_gather | solution.py:280
  7.3 107.3 %all-gather.5.cloned.1.call-start = ((), (), s32[]{:S(2)}) async-start(), calls=%async_computation.5 | async-start | bytes 4038656 | tf_op jit(solution)/shard_map/all_gather | solution.py:283
  9.9 18.1 %collective-permute-start = (bf16[2,2,16,512]{3,2,1,0:T(8,128)(2,1)S(1)}, bf16[2,2,16,512]{3,2,1,0:T(8,128)(2,1)S(1)}, u32[]{:S(2)}, u32[]{:S(2)}) collective-permute-start(bf16[2,2,16,512]{3,2,1,0:T(8,128)(2,1)S(1)} %get-tuple-element.22), channel_id=1, source_target_pairs={{0,2},{2,4},{4,6},{6,8},{8,10},{10,12},{12,14},{1,3},{3,5},{5,7},{... | collective-permute-start | bytes 196616 | tf_op jit(solution)/shard_map/ppermute | solution.py:22
  13.9 14.1 %collective-permute-start.1 = (bf16[2,2,16,512]{3,2,1,0:T(8,128)(2,1)S(1)}, bf16[2,2,16,512]{3,2,1,0:T(8,128)(2,1)S(1)}, u32[]{:S(2)}, u32[]{:S(2)}) collective-permute-start(bf16[2,2,16,512]{3,2,1,0:T(8,128)(2,1)S(1)} %get-tuple-element.21), channel_id=1, source_target_pairs={{2,0},{4,2},{6,4},{8,6},{10,8},{12,10},{14,12},{3,1},{5,3},{7,5},{... | collective-permute-start | bytes 196616 | tf_op jit(solution)/shard_map/ppermute | solution.py:22
  16.9 18.2 %all-to-all-start = ((f32[16,8,128]{2,1,0:T(8,128)}), f32[16,8,128]{2,1,0:T(8,128)S(1)}, u32[]{:S(2)}, u32[]{:S(2)}) async-start(f32[16,8,128]{2,1,0:T(8,128)} %shard_map.100), calls=%async_computation | async-start | bytes 131072 | tf_op jit(solution)/shard_map/all_to_all | solution.py:286
  35.1 5.6 %copy-start.9 = (f32[16,8,128]{2,1,0:T(8,128)}, f32[16,8,128]{2,1,0:T(8,128)S(1)}, u32[]{:S(2)}) copy-start(f32[16,8,128]{2,1,0:T(8,128)S(1)} %all-to-all-done.parts_ref) | copy-start | bytes 196612
  36.1 18.4 %collective-permute-start.2 = (bf16[2,10,16,512]{3,2,1,0:T(8,128)(2,1)S(1)}, bf16[2,10,16,512]{3,2,1,0:T(8,128)(2,1)S(1)}, u32[]{:S(2)}, u32[]{:S(2)}) collective-permute-start(bf16[2,10,16,512]{3,2,1,0:T(8,128)(2,1)S(1)} %pad_maximum_fusion.own_ref), channel_id=1, source_target_pairs={{0,16},{16,32},{32,48},{48,64},{64,80},{80,96},{96,112},{112,128},... | collective-permute-start | bytes 983048 | tf_op jit(solution)/shard_map/ppermute | solution.py:22
  42.3 21.3 %all-to-all-start.1 = ((f32[32,8,128]{2,1,0:T(8,128)}), f32[32,8,128]{2,1,0:T(8,128)S(1)}, u32[]{:S(2)}, u32[]{:S(2)}) async-start(f32[32,8,128]{2,1,0:T(8,128)} %shard_map.101), calls=%async_computation.1 | async-start | bytes 262144 | tf_op jit(solution)/shard_map/all_to_all | solution.py:295
  55.3 8.3 %collective-permute-start.3 = (bf16[4,2,16,512]{3,2,1,0:T(8,128)(2,1)S(1)}, bf16[4,2,16,512]{3,2,1,0:T(8,128)(2,1)S(1)}, u32[]{:S(2)}, u32[]{:S(2)}) collective-permute-start(bf16[4,2,16,512]{3,2,1,0:T(8,128)(2,1)S(1)} %shard_map.102), channel_id=1, source_target_pairs={{0,1},{1,0},{2,3},{3,2},{4,5},{5,4},{6,7},{7,6},{8,9},{9,8},{10,11... | collective-permute-start | bytes 393224 | tf_op jit(solution)/shard_map/ppermute | solution.py:26
  66.2 2.0 %copy-start = (bf16[6,640,512]{2,1,0:T(8,128)(2,1)}, bf16[6,640,512]{2,1,0:T(8,128)(2,1)S(1)}, u32[]{:S(2)}) copy-start(bf16[6,640,512]{2,1,0:T(8,128)(2,1)S(1)} %shard_map.103.copies_ref) | copy-start | bytes 11796484
  68.2 42.1 %copy-start.6 = (f32[256]{0:T(256)S(1)}, f32[256]{0:T(256)}, u32[]{:S(2)}) copy-start(f32[256]{0:T(256)} %param.16) | copy-start | bytes 3076
  68.2 42.1 %copy-start.7 = (f32[256]{0:T(256)S(1)}, f32[256]{0:T(256)}, u32[]{:S(2)}) copy-start(f32[256]{0:T(256)} %param.17) | copy-start | bytes 3076
  68.2 46.3 %copy-start.2 = (bf16[2,6,16,512]{3,2,1,0:T(8,128)(2,1)S(1)}, bf16[2,6,16,512]{3,2,1,0:T(8,128)(2,1)}, u32[]{:S(2)}) copy-start(bf16[2,6,16,512]{3,2,1,0:T(8,128)(2,1)} %param.10) | copy-start | bytes 589828
  68.2 46.3 %copy-start.8 = (f32[256]{0:T(256)S(1)}, f32[256]{0:T(256)}, u32[]{:S(2)}) copy-start(f32[256]{0:T(256)} %param.19) | copy-start | bytes 3076
  75.8 13.3 %all-to-all-start.2 = ((f32[16,8,128]{2,1,0:T(8,128)}), f32[16,8,128]{2,1,0:T(8,128)S(1)}, u32[]{:S(2)}, u32[]{:S(2)}) async-start(f32[16,8,128]{2,1,0:T(8,128)} %get-tuple-element.15), calls=%async_computation.2 | async-start | bytes 131072 | tf_op jit(solution)/shard_map/all_to_all | solution.py:286
  81.2 19.9 %collective-permute-start.4 = (f32[288,256]{1,0:T(8,128)}, f32[288,256]{1,0:T(8,128)S(1)}, u32[]{:S(2)}, u32[]{:S(2)}) collective-permute-start(f32[288,256]{1,0:T(8,128)} %get-tuple-element.16.middle_ref), channel_id=1, source_target_pairs={{0,16},{16,32},{32,48},{48,64},{64,80},{80,96},{96,112},{112,128},... | collective-permute-start | bytes 884744 | tf_op jit(solution)/shard_map/ppermute | solution.py:22
  89.1 0.6 copy-start.10
  91.3 19.0 %all-to-all-start.3 = ((f32[32,8,128]{2,1,0:T(8,128)}), f32[32,8,128]{2,1,0:T(8,128)S(1)}, u32[]{:S(2)}, u32[]{:S(2)}) async-start(f32[32,8,128]{2,1,0:T(8,128)} %shard_map.105), calls=%async_computation.3 | async-start | bytes 262144 | tf_op jit(solution)/shard_map/all_to_all | solution.py:295
  110.3 1.0 copy-start.3
  114.5 2.1 %copy-start.1 = (bf16[29,256,256]{2,1,0:T(8,128)(2,1)S(1)}, bf16[29,256,256]{2,1,0:T(8,128)(2,1)}, u32[]{:S(2)}) copy-start(bf16[29,256,256]{2,1,0:T(8,128)(2,1)} %all-gather.5.cloned.1.call-done.weight_ref) | copy-start | bytes 11403268
Sparse Core Ops, SparseCore 0:
  9.5 58.5 all-gather.2
  70.3 44.2 all-gather.4

commit v7 on v6

--- a/solution.py
+++ b/solution.py
@@ -153,39 +153,38 @@
             right = [jnp.where(col == 0, o, inner[15]) for o in outer]
             columns = left + inner + right
             base = t * 160
-            for p in range(2):
-                for i in range(10 - p):
-                    pair = jnp.concatenate([columns[2 * i + p], columns[2 * i + p + 1]], axis=0)
-                    out_ref[2 * dy + p, pl.ds(base + 16 * i, 16), :] = pair.astype(jnp.bfloat16)
-            out_ref[2 * dy + 1, pl.ds(base + 144, 16), :] = jnp.zeros((16, chans), jnp.bfloat16)
-
-
-def conv1_kernel(count, bias_ref, copies_ref, gathered_ref, middle_ref, stats_ref, copies, weights, arrived):
-    layouts = [pltpu.make_async_copy(copies_ref.at[i], copies.at[i], arrived.at[i]) for i in range(6)]
+            for i in range(10):
+                pair = jnp.concatenate([columns[2 * i], columns[2 * i + 1]], axis=0)
+                out_ref[dy, pl.ds(base + 16 * i, 16), :] = pair.astype(jnp.bfloat16)
+
+
+def conv1_kernel(count, bias_ref, copies_ref, gathered_ref, middle_ref, stats_ref, total, copies, weights, arrived):
+    layouts = [pltpu.make_async_copy(copies_ref.at[dy], copies.at[dy], arrived.at[dy]) for dy in range(3)]
     fetches = [
-        pltpu.make_async_copy(gathered_ref.at[3 * i : 3 * i + 3], weights.at[3 * i : 3 * i + 3], arrived.at[6 + i])
+        pltpu.make_async_copy(gathered_ref.at[3 * i : 3 * i + 3], weights.at[3 * i : 3 * i + 3], arrived.at[3 + i])
         for i in range(9)
     ]
     for dy in range(3):
-        for copy in [*layouts[2 * dy : 2 * dy + 2], *fetches[dy::3]]:
+        for copy in [layouts[dy], *fetches[dy::3]]:
             copy.start()
-    middle_ref[...] = jnp.broadcast_to(bias_ref[...], middle_ref.shape)
-    depth = 3 * weights.shape[1]
     for dy in range(3):
-        for copy in layouts[2 * dy : 2 * dy + 2]:
+        for copy in [layouts[dy], *fetches[dy::3]]:
             copy.wait()
-        for dt in range(3):
-            fetches[3 * dt + dy].wait()
-            weight = weights[9 * dt + 3 * dy : 9 * dt + 3 * dy + 3].reshape(depth, weights.shape[2])
-
-            def window(dx, dy=dy, dt=dt):
-                starts = [(dt + t) * 160 + (dx // 2) * 16 for t in range(2)]
-                return jnp.concatenate([copies[2 * dy + dx % 2, at : at + 144, :] for at in starts], axis=0)
-
-            lhs = jnp.concatenate([window(dx) for dx in range(3)], axis=1)
-            middle_ref[...] += jnp.dot(lhs, weight, preferred_element_type=jnp.float32)
-
-    values = middle_ref[...]
+        lhs = jnp.concatenate([copies[dy, 160 * dt : 160 * dt + 320, :] for dt in range(3)], axis=1)
+        for dx in range(3):
+            weight = jnp.concatenate([weights[9 * dt + 3 * dy + dx] for dt in range(3)], axis=0)
+            product = jnp.dot(lhs, weight, preferred_element_type=jnp.float32)
+            if dy == 0:
+                total[dx] = product
+            else:
+                total[dx] += product
+
+    frames = []
+    for t in range(2):
+        parts = [total[dx, 160 * t + 8 * dx : 160 * t + 8 * dx + 144, :] for dx in range(3)]
+        frames.append(parts[0] + parts[1] + parts[2] + bias_ref[...])
+    values = jnp.concatenate(frames, axis=0)
+    middle_ref[...] = values
     place = lax.broadcasted_iota(jnp.int32, values.shape, 0)
     y, x = place % 8, (place // 8) % 18
     keep = (y >= 1) & (y <= 6) & (x >= 1) & (x <= 16)
@@ -319,7 +318,7 @@
 
     copies = pl.pallas_call(
         functools.partial(hidden1_kernel, float(positions * plane), ntm),
-        out_shape=jax.ShapeDtypeStruct((6, 640, chans_in), jnp.bfloat16),
+        out_shape=jax.ShapeDtypeStruct((3, 640, chans_in), jnp.bfloat16),
         in_specs=[pl.BlockSpec(memory_space=SMEM)] + [whole()] * 6,
         out_specs=whole(),
         scratch_shapes=[VMEM((chans_in // 128, 192, 128), jnp.float32), VMEM((32, chans_in), jnp.float32)],
@@ -335,6 +334,7 @@
         in_specs=[whole()] + [pl.BlockSpec(memory_space=HBM)] * 2,
         out_specs=(whole(), whole()),
         scratch_shapes=[
+            VMEM((3, 320, chans_out), jnp.float32),
             VMEM(copies.shape, jnp.bfloat16),
             VMEM(first.shape, jnp.bfloat16),
             pltpu.SemaphoreType.DMA((15,)),

time: 126 us -> 126 us (level)
  transfers between devices with their start and end apart: 11 -> 11, of which waited for: 5 -> 6; matrix products, arithmetic and copies ran while one was open for 4% -> 4% of each run, Pallas kernels for 14% -> 13%
where the time goes in v7:
time: 126 us; the launch traced here: 125 us
  starting transfers between devices  54 us (43%)
  waiting for transfers between devices  29.7 us (24%)
  Pallas kernels  18.4 us (15%)
  between operations  13.5 us (11%)
  local copies, waits for them, and re-layouts  6.72 us (5%)
  other arithmetic  2.76 us (2%)
    all_to_all x2, starting transfers between devices, shared(): return (lax.all_to_all(stats, TM, 0, 0, tiled=True), beside)  22.7 us
    all_to_all x2, starting transfers between devices, shared(): stats = lax.all_to_all(stats, ('row', 'col'), 0, 0, tiled=True)  15.2 us
    all_to_all x2, waiting for transfers between devices, shared(): return (lax.all_to_all(stats, TM, 0, 0, tiled=True), beside)  14.9 us
    ppermute x4, starting transfers between devices, moved(): return lax.ppermute(block, axis, route)  13.5 us
    all_to_all x2, waiting for transfers between devices, shared(): stats = lax.all_to_all(stats, ('row', 'col'), 0, 0, tiled=True)  11.3 us
    pallas_call x1, Pallas kernels, per_device(): pl.pallas_call(functools.partial(conv1_kernel, float(positions)), out_sha...  7.17 us
    unnamed x22, local copies, waits for them, and re-layouts  5.05 us
    pallas_call x2, Pallas kernels, shared(): pl.pallas_call(functools.partial(merge_kernel, count), out_shape=jax.Shap...  3.06 us
  transfers between devices with their start and end apart: 11, of which 6 were waited for; matrix products, arithmetic and copies ran while one was open for 4% of the time, Pallas kernels for 13%

profile of v7, /device:TPU:1, one launch (start us, length us, event | category | flops | bytes accessed | tf_op | source)
XLA Modules:
  0.0 125.1 jit_solution(14086217789142264262)
XLA Ops:
  6.5 0.0 copy-start.4
  6.5 0.0 copy-start.5
  6.5 0.0 all-gather.3.cloned.1.call-start
  6.5 0.7 all-gather.3.cloned.1.call-update
  7.3 0.0 all-gather.5.cloned.1.call-start
  7.3 1.7 %pad_maximum_fusion.1 = bf16[29,16,256]{2,1,0:T(8,128)(2,1)} fusion(bf16[2,16,256]{2,1,0:T(8,128)(2,1)} %bitcast.23, bf16[27,16,256]{2,1,0:T(8,128)(2,1)} %param.18), kind=kLoop, calls=%fused_computation.1 | loop fusion | flops 118784 | bytes 475136 | tf_op jit(solution)/shard_map/concatenate | solution.py:282
  9.0 0.0 all-gather.5.cloned.1.call-update
  9.0 0.9 fusion
  9.9 4.0 %collective-permute-start = (bf16[2,2,16,512]{3,2,1,0:T(8,128)(2,1)S(1)}, bf16[2,2,16,512]{3,2,1,0:T(8,128)(2,1)S(1)}, u32[]{:S(2)}, u32[]{:S(2)}) collective-permute-start(bf16[2,2,16,512]{3,2,1,0:T(8,128)(2,1)S(1)} %get-tuple-element.22), channel_id=1, source_target_pairs={{0,2},{2,4},{4,6},{6,8},{8,10},{10,12},{12,14},{1,3},{3,5},{5,7},{... | collective-permute-start | bytes 196616 | tf_op jit(solution)/shard_map/ppermute | solution.py:22
  13.9 1.3 %collective-permute-start.1 = (bf16[2,2,16,512]{3,2,1,0:T(8,128)(2,1)S(1)}, bf16[2,2,16,512]{3,2,1,0:T(8,128)(2,1)S(1)}, u32[]{:S(2)}, u32[]{:S(2)}) collective-permute-start(bf16[2,2,16,512]{3,2,1,0:T(8,128)(2,1)S(1)} %get-tuple-element.21), channel_id=1, source_target_pairs={{2,0},{4,2},{6,4},{8,6},{10,8},{12,10},{14,12},{3,1},{5,3},{7,5},{... | collective-permute-start | bytes 196616 | tf_op jit(solution)/shard_map/ppermute | solution.py:22
  15.2 1.7 %shard_map.100 = f32[16,8,128]{2,1,0:T(8,128)} custom-call(bf16[192,512]{1,0:T(8,128)(2,1)} %bitcast.16), custom_call_target="tpu_custom_call" | custom-call | tf_op jit(solution)/shard_map/pallas_call | solution.py:296
  16.9 10.3 %all-to-all-start = ((f32[16,8,128]{2,1,0:T(8,128)}), f32[16,8,128]{2,1,0:T(8,128)S(1)}, u32[]{:S(2)}, u32[]{:S(2)}) async-start(f32[16,8,128]{2,1,0:T(8,128)} %shard_map.100), calls=%async_computation | async-start | bytes 131072 | tf_op jit(solution)/shard_map/all_to_all | solution.py:285
  27.2 0.8 slice_bitcast_fusion.1
  28.0 0.0 collective-permute-done
  28.0 0.0 collective-permute-done.1
  28.0 7.1 %all-to-all-done.parts_ref = f32[16,8,128]{2,1,0:T(8,128)S(1)} async-done(((f32[16,8,128]{2,1,0:T(8,128)}), f32[16,8,128]{2,1,0:T(8,128)S(1)}, u32[]{:S(2)}, u32[]{:S(2)}) %all-to-all-start) | async-done | bytes 65568 | tf_op jit(solution)/shard_map/all_to_all | solution.py:285
  35.1 0.0 copy-start.9
  35.2 1.0 pad_maximum_fusion.own_ref
  36.1 4.6 %collective-permute-start.2 = (bf16[2,10,16,512]{3,2,1,0:T(8,128)(2,1)S(1)}, bf16[2,10,16,512]{3,2,1,0:T(8,128)(2,1)S(1)}, u32[]{:S(2)}, u32[]{:S(2)}) collective-permute-start(bf16[2,10,16,512]{3,2,1,0:T(8,128)(2,1)S(1)} %pad_maximum_fusion.own_ref), channel_id=1, source_target_pairs={{0,16},{16,32},{32,48},{48,64},{64,80},{80,96},{96,112},{112,128},... | collective-permute-start | bytes 983048 | tf_op jit(solution)/shard_map/ppermute | solution.py:22
  40.7 0.0 copy-done.9
  40.7 1.5 %shard_map.101 = f32[32,8,128]{2,1,0:T(8,128)} custom-call(f32[16,8,128]{2,1,0:T(8,128)} %copy-done.9), custom_call_target="tpu_custom_call" | custom-call | tf_op jit(solution)/shard_map/pallas_call | solution.py:288
  42.3 12.2 %all-to-all-start.1 = ((f32[32,8,128]{2,1,0:T(8,128)}), f32[32,8,128]{2,1,0:T(8,128)S(1)}, u32[]{:S(2)}, u32[]{:S(2)}) async-start(f32[32,8,128]{2,1,0:T(8,128)} %shard_map.101), calls=%async_computation.1 | async-start | bytes 262144 | tf_op jit(solution)/shard_map/all_to_all | solution.py:294
  54.5 0.1 pad_add_fusion.place_ref
  54.5 0.0 collective-permute-done.2.earlier_ref
  54.5 0.8 shard_map.102
  55.3 2.5 %collective-permute-start.3 = (bf16[4,2,16,512]{3,2,1,0:T(8,128)(2,1)S(1)}, bf16[4,2,16,512]{3,2,1,0:T(8,128)(2,1)S(1)}, u32[]{:S(2)}, u32[]{:S(2)}) collective-permute-start(bf16[4,2,16,512]{3,2,1,0:T(8,128)(2,1)S(1)} %shard_map.102), channel_id=1, source_target_pairs={{0,1},{1,0},{2,3},{3,2},{4,5},{5,4},{6,7},{7,6},{8,9},{9,8},{10,11... | collective-permute-start | bytes 393224 | tf_op jit(solution)/shard_map/ppermute | solution.py:26
  57.8 5.8 %all-to-all-done.1.parts_ref = f32[32,8,128]{2,1,0:T(8,128)S(1)} async-done(((f32[32,8,128]{2,1,0:T(8,128)}), f32[32,8,128]{2,1,0:T(8,128)S(1)}, u32[]{:S(2)}, u32[]{:S(2)}) %all-to-all-start.1) | async-done | bytes 131104 | tf_op jit(solution)/shard_map/all_to_all | solution.py:294
  63.6 0.0 collective-permute-done.3.border_ref
  63.6 0.0 copy-done.4
  63.6 0.0 copy-done.5
  63.6 2.5 %shard_map.103.copies_ref = bf16[3,640,512]{2,1,0:T(8,128)(2,1)S(1)} custom-call(s32[3]{0:T(128)S(1)} %pad_add_fusion.place_ref, f32[32,8,128]{2,1,0:T(8,128)S(1)} %all-to-all-done.1.parts_ref, f32[1,512]{1,0:T(1,128)S(1)} %bitcast.18, f32[1,512]{1,0:T(1,128)S(1)} %bitcast.19, bf16[2,10,16,512]{3,2,1,0:T(8,128)(2,1)S(1)} %collective-permute-done.2.earlier_ref, ...), custom_call_target="tpu_custom_call" | custom-call | tf_op jit(solution)/shard_map/pallas_call | solution.py:319
  66.2 0.0 copy-start
  66.2 1.4 %copy-done = bf16[3,640,512]{2,1,0:T(8,128)(2,1)} copy-done((bf16[3,640,512]{2,1,0:T(8,128)(2,1)}, bf16[3,640,512]{2,1,0:T(8,128)(2,1)S(1)}, u32[]{:S(2)}) %copy-start) | copy-done | bytes 1966104
  67.5 0.6 all-gather.3.cloned.1.call-done.gathered_ref
  68.1 0.0 copy-start.6
  68.1 0.0 copy-start.7
  68.1 0.0 copy-start.2
  68.1 0.0 copy-start.8
  68.1 7.2 %shard_map.104 = (f32[288,256]{1,0:T(8,128)}, f32[16,8,128]{2,1,0:T(8,128)}) custom-call(f32[1,256]{1,0:T(1,128)} %bitcast.24, bf16[3,640,512]{2,1,0:T(8,128)(2,1)} %copy-done, bf16[27,512,256]{2,1,0:T(8,128)(2,1)} %all-gather.3.cloned.1.call-done.gathered_ref), custom_call_target="tpu_custom_call" | custom-call | tf_op jit(solution)/shard_map/pallas_call | solution.py:328
  75.3 4.9 %all-to-all-start.2 = ((f32[16,8,128]{2,1,0:T(8,128)}), f32[16,8,128]{2,1,0:T(8,128)S(1)}, u32[]{:S(2)}, u32[]{:S(2)}) async-start(f32[16,8,128]{2,1,0:T(8,128)} %get-tuple-element.15), calls=%async_computation.2 | async-start | bytes 131072 | tf_op jit(solution)/shard_map/all_to_all | solution.py:285
  80.2 3.6 %collective-permute-start.4 = (f32[288,256]{1,0:T(8,128)}, f32[288,256]{1,0:T(8,128)S(1)}, u32[]{:S(2)}, u32[]{:S(2)}) collective-permute-start(f32[288,256]{1,0:T(8,128)} %get-tuple-element.16.middle_ref), channel_id=1, source_target_pairs={{0,16},{16,32},{32,48},{48,64},{64,80},{80,96},{96,112},{112,128},... | collective-permute-start | bytes 884744 | tf_op jit(solution)/shard_map/ppermute | solution.py:22
  83.7 4.3 %all-to-all-done.2.parts_ref = f32[16,8,128]{2,1,0:T(8,128)S(1)} async-done(((f32[16,8,128]{2,1,0:T(8,128)}), f32[16,8,128]{2,1,0:T(8,128)S(1)}, u32[]{:S(2)}, u32[]{:S(2)}) %all-to-all-start.2) | async-done | bytes 65568 | tf_op jit(solution)/shard_map/all_to_all | solution.py:285
  88.0 0.0 copy-start.10
  88.0 0.6 copy-done.10
  88.6 1.5 %shard_map.105 = f32[32,8,128]{2,1,0:T(8,128)} custom-call(f32[16,8,128]{2,1,0:T(8,128)} %copy-done.10), custom_call_target="tpu_custom_call" | custom-call | tf_op jit(solution)/shard_map/pallas_call | solution.py:288
  90.2 10.6 %all-to-all-start.3 = ((f32[32,8,128]{2,1,0:T(8,128)}), f32[32,8,128]{2,1,0:T(8,128)S(1)}, u32[]{:S(2)}, u32[]{:S(2)}) async-start(f32[32,8,128]{2,1,0:T(8,128)} %shard_map.105), calls=%async_computation.3 | async-start | bytes 262144 | tf_op jit(solution)/shard_map/all_to_all | solution.py:294
  100.7 0.0 collective-permute-done.4.earlier_ref
  100.7 9.1 %all-to-all-done.3.parts_ref = f32[32,8,128]{2,1,0:T(8,128)S(1)} async-done(((f32[32,8,128]{2,1,0:T(8,128)}), f32[32,8,128]{2,1,0:T(8,128)S(1)}, u32[]{:S(2)}, u32[]{:S(2)}) %all-to-all-start.3) | async-done | bytes 131104 | tf_op jit(solution)/shard_map/all_to_all | solution.py:294
  109.9 0.0 copy-done.6
  109.9 0.0 copy-done.7
  109.9 0.0 copy-start.3
  109.9 1.0 copy-done.3
  110.8 1.4 %shard_map.106.copies = bf16[6,576,256]{2,1,0:T(8,128)(2,1)S(1)} custom-call(s32[3]{0:T(128)S(1)} %pad_add_fusion.place_ref, f32[32,8,128]{2,1,0:T(8,128)S(1)} %all-to-all-done.3.parts_ref, f32[1,256]{1,0:T(1,128)S(1)} %bitcast.20, f32[1,256]{1,0:T(1,128)S(1)} %bitcast.21, f32[288,256]{1,0:T(8,128)S(1)} %collective-permute-done.4.earlier_ref, ...), custom_call_target="tpu_custom_call" | custom-call | tf_op jit(solution)/shard_map/pallas_call | solution.py:348
  112.2 2.2 %all-gather.5.cloned.1.call-done.weight_ref = bf16[29,256,256]{2,1,0:T(8,128)(2,1)} async-done(((bf16[29,16,256]{2,1,0:T(8,128)(2,1)}), bf16[29,256,256]{2,1,0:T(8,128)(2,1)}) %all-gather.5.cloned.1.call-update) | async-done | bytes 3801104 | tf_op jit(solution)/shard_map/all_gather | solution.py:282
  114.4 0.0 copy-done.2
  114.4 0.0 copy-done.8
  114.4 0.0 copy-start.1
  114.4 2.1 %copy-done.1 = bf16[29,256,256]{2,1,0:T(8,128)(2,1)S(1)} copy-done((bf16[29,256,256]{2,1,0:T(8,128)(2,1)S(1)}, bf16[29,256,256]{2,1,0:T(8,128)(2,1)}, u32[]{:S(2)}) %copy-start.1) | copy-done | bytes 3801112
  116.5 1.8 %shard_map.107 = bf16[192,256]{1,0:T(8,128)(2,1)} custom-call(bf16[6,576,256]{2,1,0:T(8,128)(2,1)S(1)} %shard_map.106.copies, f32[1,256]{1,0:T(1,128)S(1)} %bitcast.22, bf16[192,512]{1,0:T(8,128)(2,1)S(1)} %bitcast.17, bf16[29,256,256]{2,1,0:T(8,128)(2,1)S(1)} %copy-done.1), custom_call_target="tpu_custom_call" | custom-call | tf_op jit(solution)/shard_map/pallas_call | solution.py:357
  (1 shorter events, 0.0 us)
Async XLA Ops:
  6.5 57.1 %copy-start.4 = (f32[512]{0:T(512)S(1)}, f32[512]{0:T(512)}, u32[]{:S(2)}) copy-start(f32[512]{0:T(512)} %param.11) | copy-start | bytes 6148
  6.5 57.1 %copy-start.5 = (f32[512]{0:T(512)S(1)}, f32[512]{0:T(512)}, u32[]{:S(2)}) copy-start(f32[512]{0:T(512)} %param.12) | copy-start | bytes 6148
  6.5 61.6 %all-gather.3.cloned.1.call-start = ((), (), s32[]{:S(2)}) async-start(), calls=%async_computation.4 | async-start | bytes 7520256 | tf_op jit(solution)/shard_map/all_gather | solution.py:279
  7.3 107.1 %all-gather.5.cloned.1.call-start = ((), (), s32[]{:S(2)}) async-start(), calls=%async_computation.5 | async-start | bytes 4038656 | tf_op jit(solution)/shard_map/all_gather | solution.py:282
  9.9 18.1 %collective-permute-start = (bf16[2,2,16,512]{3,2,1,0:T(8,128)(2,1)S(1)}, bf16[2,2,16,512]{3,2,1,0:T(8,128)(2,1)S(1)}, u32[]{:S(2)}, u32[]{:S(2)}) collective-permute-start(bf16[2,2,16,512]{3,2,1,0:T(8,128)(2,1)S(1)} %get-tuple-element.22), channel_id=1, source_target_pairs={{0,2},{2,4},{4,6},{6,8},{8,10},{10,12},{12,14},{1,3},{3,5},{5,7},{... | collective-permute-start | bytes 196616 | tf_op jit(solution)/shard_map/ppermute | solution.py:22
  13.9 14.1 %collective-permute-start.1 = (bf16[2,2,16,512]{3,2,1,0:T(8,128)(2,1)S(1)}, bf16[2,2,16,512]{3,2,1,0:T(8,128)(2,1)S(1)}, u32[]{:S(2)}, u32[]{:S(2)}) collective-permute-start(bf16[2,2,16,512]{3,2,1,0:T(8,128)(2,1)S(1)} %get-tuple-element.21), channel_id=1, source_target_pairs={{2,0},{4,2},{6,4},{8,6},{10,8},{12,10},{14,12},{3,1},{5,3},{7,5},{... | collective-permute-start | bytes 196616 | tf_op jit(solution)/shard_map/ppermute | solution.py:22
  16.9 18.2 %all-to-all-start = ((f32[16,8,128]{2,1,0:T(8,128)}), f32[16,8,128]{2,1,0:T(8,128)S(1)}, u32[]{:S(2)}, u32[]{:S(2)}) async-start(f32[16,8,128]{2,1,0:T(8,128)} %shard_map.100), calls=%async_computation | async-start | bytes 131072 | tf_op jit(solution)/shard_map/all_to_all | solution.py:285
  35.1 5.6 %copy-start.9 = (f32[16,8,128]{2,1,0:T(8,128)}, f32[16,8,128]{2,1,0:T(8,128)S(1)}, u32[]{:S(2)}) copy-start(f32[16,8,128]{2,1,0:T(8,128)S(1)} %all-to-all-done.parts_ref) | copy-start | bytes 196612
  36.1 18.4 %collective-permute-start.2 = (bf16[2,10,16,512]{3,2,1,0:T(8,128)(2,1)S(1)}, bf16[2,10,16,512]{3,2,1,0:T(8,128)(2,1)S(1)}, u32[]{:S(2)}, u32[]{:S(2)}) collective-permute-start(bf16[2,10,16,512]{3,2,1,0:T(8,128)(2,1)S(1)} %pad_maximum_fusion.own_ref), channel_id=1, source_target_pairs={{0,16},{16,32},{32,48},{48,64},{64,80},{80,96},{96,112},{112,128},... | collective-permute-start | bytes 983048 | tf_op jit(solution)/shard_map/ppermute | solution.py:22
  42.3 21.3 %all-to-all-start.1 = ((f32[32,8,128]{2,1,0:T(8,128)}), f32[32,8,128]{2,1,0:T(8,128)S(1)}, u32[]{:S(2)}, u32[]{:S(2)}) async-start(f32[32,8,128]{2,1,0:T(8,128)} %shard_map.101), calls=%async_computation.1 | async-start | bytes 262144 | tf_op jit(solution)/shard_map/all_to_all | solution.py:294
  55.3 8.3 %collective-permute-start.3 = (bf16[4,2,16,512]{3,2,1,0:T(8,128)(2,1)S(1)}, bf16[4,2,16,512]{3,2,1,0:T(8,128)(2,1)S(1)}, u32[]{:S(2)}, u32[]{:S(2)}) collective-permute-start(bf16[4,2,16,512]{3,2,1,0:T(8,128)(2,1)S(1)} %shard_map.102), channel_id=1, source_target_pairs={{0,1},{1,0},{2,3},{3,2},{4,5},{5,4},{6,7},{7,6},{8,9},{9,8},{10,11... | collective-permute-start | bytes 393224 | tf_op jit(solution)/shard_map/ppermute | solution.py:26
  66.2 1.4 %copy-start = (bf16[3,640,512]{2,1,0:T(8,128)(2,1)}, bf16[3,640,512]{2,1,0:T(8,128)(2,1)S(1)}, u32[]{:S(2)}) copy-start(bf16[3,640,512]{2,1,0:T(8,128)(2,1)S(1)} %shard_map.103.copies_ref) | copy-start | bytes 5898244
  68.1 41.7 %copy-start.6 = (f32[256]{0:T(256)S(1)}, f32[256]{0:T(256)}, u32[]{:S(2)}) copy-start(f32[256]{0:T(256)} %param.16) | copy-start | bytes 3076
  68.1 41.7 %copy-start.7 = (f32[256]{0:T(256)S(1)}, f32[256]{0:T(256)}, u32[]{:S(2)}) copy-start(f32[256]{0:T(256)} %param.17) | copy-start | bytes 3076
  68.1 46.2 %copy-start.2 = (bf16[2,6,16,512]{3,2,1,0:T(8,128)(2,1)S(1)}, bf16[2,6,16,512]{3,2,1,0:T(8,128)(2,1)}, u32[]{:S(2)}) copy-start(bf16[2,6,16,512]{3,2,1,0:T(8,128)(2,1)} %param.10) | copy-start | bytes 589828
  68.1 46.2 %copy-start.8 = (f32[256]{0:T(256)S(1)}, f32[256]{0:T(256)}, u32[]{:S(2)}) copy-start(f32[256]{0:T(256)} %param.19) | copy-start | bytes 3076
  75.3 12.7 %all-to-all-start.2 = ((f32[16,8,128]{2,1,0:T(8,128)}), f32[16,8,128]{2,1,0:T(8,128)S(1)}, u32[]{:S(2)}, u32[]{:S(2)}) async-start(f32[16,8,128]{2,1,0:T(8,128)} %get-tuple-element.15), calls=%async_computation.2 | async-start | bytes 131072 | tf_op jit(solution)/shard_map/all_to_all | solution.py:285
  80.2 20.6 %collective-permute-start.4 = (f32[288,256]{1,0:T(8,128)}, f32[288,256]{1,0:T(8,128)S(1)}, u32[]{:S(2)}, u32[]{:S(2)}) collective-permute-start(f32[288,256]{1,0:T(8,128)} %get-tuple-element.16.middle_ref), channel_id=1, source_target_pairs={{0,16},{16,32},{32,48},{48,64},{64,80},{80,96},{96,112},{112,128},... | collective-permute-start | bytes 884744 | tf_op jit(solution)/shard_map/ppermute | solution.py:22
  88.0 0.6 copy-start.10
  90.2 19.7 %all-to-all-start.3 = ((f32[32,8,128]{2,1,0:T(8,128)}), f32[32,8,128]{2,1,0:T(8,128)S(1)}, u32[]{:S(2)}, u32[]{:S(2)}) async-start(f32[32,8,128]{2,1,0:T(8,128)} %shard_map.105), calls=%async_computation.3 | async-start | bytes 262144 | tf_op jit(solution)/shard_map/all_to_all | solution.py:294
  109.9 1.0 copy-start.3
  114.4 2.1 %copy-start.1 = (bf16[29,256,256]{2,1,0:T(8,128)(2,1)S(1)}, bf16[29,256,256]{2,1,0:T(8,128)(2,1)}, u32[]{:S(2)}) copy-start(bf16[29,256,256]{2,1,0:T(8,128)(2,1)} %all-gather.5.cloned.1.call-done.weight_ref) | copy-start | bytes 11403268
Sparse Core Ops, SparseCore 0:
  9.5 58.5 all-gather.2
  70.3 44.0 all-gather.4

commit v8 on v6

--- a/solution.py
+++ b/solution.py
@@ -229,20 +229,19 @@
     for dt in range(3):
         for dy in range(3):
             weight = weight_ref[9 * dt + 3 * dy : 9 * dt + 3 * dy + 3].reshape(3 * chans, chans)
-            for t in range(2):
-
-                def window(dx, dy=dy, first=dt + t):
-                    start = first * 144 + (dx // 2) * 16
-                    return copies[2 * dy + dx % 2, start : start + 128, :]
-
-                lhs = jnp.concatenate([window(dx) for dx in range(3)], axis=1)
-                product = jnp.dot(lhs, weight, preferred_element_type=jnp.float32)
-                for j in range(chans // 128):
-                    part = product[:, 128 * j : 128 * (j + 1)]
-                    if dt == 0 and dy == 0:
-                        total[j, 128 * t : 128 * t + 128, :] = part
-                    else:
-                        total[j, 128 * t : 128 * t + 128, :] += part
+
+            def window(dx, dy=dy, dt=dt):
+                starts = [(dt + t) * 144 + (dx // 2) * 16 for t in range(2)]
+                return jnp.concatenate([copies[2 * dy + dx % 2, at : at + 128, :] for at in starts], axis=0)
+
+            lhs = jnp.concatenate([window(dx) for dx in range(3)], axis=1)
+            product = jnp.dot(lhs, weight, preferred_element_type=jnp.float32)
+            for j in range(chans // 128):
+                part = product[:, 128 * j : 128 * (j + 1)]
+                if dt == 0 and dy == 0:
+                    total[j, :256, :] = part
+                else:
+                    total[j, :256, :] += part
 
     for t in range(2):
         for y in range(6):

time: 126 us -> 126 us (level)
  no operation moved by 1% of the time
where the time goes in v8:
time: 126 us; the launch traced here: 125 us
  starting transfers between devices  53.1 us (42%)
  waiting for transfers between devices  29.6 us (23%)
  Pallas kernels  18.9 us (15%)
  between operations  13.6 us (11%)
  local copies, waits for them, and re-layouts  7.37 us (6%)
  other arithmetic  2.75 us (2%)
    all_to_all x2, starting transfers between devices, shared(): return (lax.all_to_all(stats, TM, 0, 0, tiled=True), beside)  22 us
    all_to_all x2, starting transfers between devices, shared(): stats = lax.all_to_all(stats, ('row', 'col'), 0, 0, tiled=True)  15.8 us
    all_to_all x2, waiting for transfers between devices, shared(): return (lax.all_to_all(stats, TM, 0, 0, tiled=True), beside)  14.9 us
    ppermute x4, starting transfers between devices, moved(): return lax.ppermute(block, axis, route)  12.7 us
    all_to_all x2, waiting for transfers between devices, shared(): stats = lax.all_to_all(stats, ('row', 'col'), 0, 0, tiled=True)  12.1 us
    pallas_call x1, Pallas kernels, per_device(): pl.pallas_call(functools.partial(conv1_kernel, float(positions)), out_sha...  7.57 us
    unnamed x22, local copies, waits for them, and re-layouts  5.71 us
    pallas_call x2, Pallas kernels, shared(): pl.pallas_call(functools.partial(merge_kernel, count), out_shape=jax.Shap...  3.08 us
  transfers between devices with their start and end apart: 11, of which 5 were waited for; matrix products, arithmetic and copies ran while one was open for 4% of the time, Pallas kernels for 14%

profile of v8, /device:TPU:1, one launch (start us, length us, event | category | flops | bytes accessed | tf_op | source)
XLA Modules:
  0.0 125.2 jit_solution(3851430500580808959)
XLA Ops:
  6.5 0.0 copy-start.4
  6.5 0.0 copy-start.5
  6.5 0.0 all-gather.3.cloned.1.call-start
  6.5 0.7 all-gather.3.cloned.1.call-update
  7.3 0.0 all-gather.5.cloned.1.call-start
  7.3 1.7 %pad_maximum_fusion.1 = bf16[29,16,256]{2,1,0:T(8,128)(2,1)} fusion(bf16[2,16,256]{2,1,0:T(8,128)(2,1)} %bitcast.23, bf16[27,16,256]{2,1,0:T(8,128)(2,1)} %param.18), kind=kLoop, calls=%fused_computation.1 | loop fusion | flops 118784 | bytes 475136 | tf_op jit(solution)/shard_map/concatenate | solution.py:282
  9.0 0.0 all-gather.5.cloned.1.call-update
  9.0 0.9 fusion
  9.9 4.0 %collective-permute-start = (bf16[2,2,16,512]{3,2,1,0:T(8,128)(2,1)S(1)}, bf16[2,2,16,512]{3,2,1,0:T(8,128)(2,1)S(1)}, u32[]{:S(2)}, u32[]{:S(2)}) collective-permute-start(bf16[2,2,16,512]{3,2,1,0:T(8,128)(2,1)S(1)} %get-tuple-element.22), channel_id=1, source_target_pairs={{0,2},{2,4},{4,6},{6,8},{8,10},{10,12},{12,14},{1,3},{3,5},{5,7},{... | collective-permute-start | bytes 196616 | tf_op jit(solution)/shard_map/ppermute | solution.py:22
  13.9 1.3 %collective-permute-start.1 = (bf16[2,2,16,512]{3,2,1,0:T(8,128)(2,1)S(1)}, bf16[2,2,16,512]{3,2,1,0:T(8,128)(2,1)S(1)}, u32[]{:S(2)}, u32[]{:S(2)}) collective-permute-start(bf16[2,2,16,512]{3,2,1,0:T(8,128)(2,1)S(1)} %get-tuple-element.21), channel_id=1, source_target_pairs={{2,0},{4,2},{6,4},{8,6},{10,8},{12,10},{14,12},{3,1},{5,3},{7,5},{... | collective-permute-start | bytes 196616 | tf_op jit(solution)/shard_map/ppermute | solution.py:22
  15.2 1.7 %shard_map.100 = f32[16,8,128]{2,1,0:T(8,128)} custom-call(bf16[192,512]{1,0:T(8,128)(2,1)} %bitcast.16), custom_call_target="tpu_custom_call" | custom-call | tf_op jit(solution)/shard_map/pallas_call | solution.py:296
  16.9 10.3 %all-to-all-start = ((f32[16,8,128]{2,1,0:T(8,128)}), f32[16,8,128]{2,1,0:T(8,128)S(1)}, u32[]{:S(2)}, u32[]{:S(2)}) async-start(f32[16,8,128]{2,1,0:T(8,128)} %shard_map.100), calls=%async_computation | async-start | bytes 131072 | tf_op jit(solution)/shard_map/all_to_all | solution.py:285
  27.2 0.8 slice_bitcast_fusion.1
  28.0 0.0 collective-permute-done
  28.0 0.0 collective-permute-done.1
  28.0 7.1 %all-to-all-done.parts_ref = f32[16,8,128]{2,1,0:T(8,128)S(1)} async-done(((f32[16,8,128]{2,1,0:T(8,128)}), f32[16,8,128]{2,1,0:T(8,128)S(1)}, u32[]{:S(2)}, u32[]{:S(2)}) %all-to-all-start) | async-done | bytes 65568 | tf_op jit(solution)/shard_map/all_to_all | solution.py:285
  35.1 0.0 copy-start.9
  35.1 1.0 pad_maximum_fusion.own_ref
  36.1 4.6 %collective-permute-start.2 = (bf16[2,10,16,512]{3,2,1,0:T(8,128)(2,1)S(1)}, bf16[2,10,16,512]{3,2,1,0:T(8,128)(2,1)S(1)}, u32[]{:S(2)}, u32[]{:S(2)}) collective-permute-start(bf16[2,10,16,512]{3,2,1,0:T(8,128)(2,1)S(1)} %pad_maximum_fusion.own_ref), channel_id=1, source_target_pairs={{0,16},{16,32},{32,48},{48,64},{64,80},{80,96},{96,112},{112,128},... | collective-permute-start | bytes 983048 | tf_op jit(solution)/shard_map/ppermute | solution.py:22
  40.7 0.0 copy-done.9
  40.7 1.5 %shard_map.101 = f32[32,8,128]{2,1,0:T(8,128)} custom-call(f32[16,8,128]{2,1,0:T(8,128)} %copy-done.9), custom_call_target="tpu_custom_call" | custom-call | tf_op jit(solution)/shard_map/pallas_call | solution.py:288
  42.3 12.2 %all-to-all-start.1 = ((f32[32,8,128]{2,1,0:T(8,128)}), f32[32,8,128]{2,1,0:T(8,128)S(1)}, u32[]{:S(2)}, u32[]{:S(2)}) async-start(f32[32,8,128]{2,1,0:T(8,128)} %shard_map.101), calls=%async_computation.1 | async-start | bytes 262144 | tf_op jit(solution)/shard_map/all_to_all | solution.py:294
  54.4 0.1 pad_add_fusion.place_ref
  54.5 0.0 collective-permute-done.2.earlier_ref
  54.5 0.8 shard_map.102
  55.3 2.5 %collective-permute-start.3 = (bf16[4,2,16,512]{3,2,1,0:T(8,128)(2,1)S(1)}, bf16[4,2,16,512]{3,2,1,0:T(8,128)(2,1)S(1)}, u32[]{:S(2)}, u32[]{:S(2)}) collective-permute-start(bf16[4,2,16,512]{3,2,1,0:T(8,128)(2,1)S(1)} %shard_map.102), channel_id=1, source_target_pairs={{0,1},{1,0},{2,3},{3,2},{4,5},{5,4},{6,7},{7,6},{8,9},{9,8},{10,11... | collective-permute-start | bytes 393224 | tf_op jit(solution)/shard_map/ppermute | solution.py:26
  57.8 5.7 %all-to-all-done.1.parts_ref = f32[32,8,128]{2,1,0:T(8,128)S(1)} async-done(((f32[32,8,128]{2,1,0:T(8,128)}), f32[32,8,128]{2,1,0:T(8,128)S(1)}, u32[]{:S(2)}, u32[]{:S(2)}) %all-to-all-start.1) | async-done | bytes 131104 | tf_op jit(solution)/shard_map/all_to_all | solution.py:294
  63.6 0.0 collective-permute-done.3.border_ref
  63.6 0.0 copy-done.4
  63.6 0.0 copy-done.5
  63.6 2.6 %shard_map.103.copies_ref = bf16[6,640,512]{2,1,0:T(8,128)(2,1)S(1)} custom-call(s32[3]{0:T(128)S(1)} %pad_add_fusion.place_ref, f32[32,8,128]{2,1,0:T(8,128)S(1)} %all-to-all-done.1.parts_ref, f32[1,512]{1,0:T(1,128)S(1)} %bitcast.18, f32[1,512]{1,0:T(1,128)S(1)} %bitcast.19, bf16[2,10,16,512]{3,2,1,0:T(8,128)(2,1)S(1)} %collective-permute-done.2.earlier_ref, ...), custom_call_target="tpu_custom_call" | custom-call | tf_op jit(solution)/shard_map/pallas_call | solution.py:319
  66.2 0.0 copy-start
  66.2 2.0 %copy-done = bf16[6,640,512]{2,1,0:T(8,128)(2,1)} copy-done((bf16[6,640,512]{2,1,0:T(8,128)(2,1)}, bf16[6,640,512]{2,1,0:T(8,128)(2,1)S(1)}, u32[]{:S(2)}) %copy-start) | copy-done | bytes 3932184
  68.2 0.0 all-gather.3.cloned.1.call-done.gathered_ref
  68.2 0.0 copy-start.6
  68.2 0.0 copy-start.7
  68.2 0.0 copy-start.2
  68.2 0.0 copy-start.8
  68.2 7.6 %shard_map.104 = (f32[288,256]{1,0:T(8,128)}, f32[16,8,128]{2,1,0:T(8,128)}) custom-call(f32[1,256]{1,0:T(1,128)} %bitcast.24, bf16[6,640,512]{2,1,0:T(8,128)(2,1)} %copy-done, bf16[27,512,256]{2,1,0:T(8,128)(2,1)} %all-gather.3.cloned.1.call-done.gathered_ref), custom_call_target="tpu_custom_call" | custom-call | tf_op jit(solution)/shard_map/pallas_call | solution.py:328
  75.8 5.4 %all-to-all-start.2 = ((f32[16,8,128]{2,1,0:T(8,128)}), f32[16,8,128]{2,1,0:T(8,128)S(1)}, u32[]{:S(2)}, u32[]{:S(2)}) async-start(f32[16,8,128]{2,1,0:T(8,128)} %get-tuple-element.15), calls=%async_computation.2 | async-start | bytes 131072 | tf_op jit(solution)/shard_map/all_to_all | solution.py:285
  81.2 2.9 %collective-permute-start.4 = (f32[288,256]{1,0:T(8,128)}, f32[288,256]{1,0:T(8,128)S(1)}, u32[]{:S(2)}, u32[]{:S(2)}) collective-permute-start(f32[288,256]{1,0:T(8,128)} %get-tuple-element.16.middle_ref), channel_id=1, source_target_pairs={{0,16},{16,32},{32,48},{48,64},{64,80},{80,96},{96,112},{112,128},... | collective-permute-start | bytes 884744 | tf_op jit(solution)/shard_map/ppermute | solution.py:22
  84.1 5.0 %all-to-all-done.2.parts_ref = f32[16,8,128]{2,1,0:T(8,128)S(1)} async-done(((f32[16,8,128]{2,1,0:T(8,128)}), f32[16,8,128]{2,1,0:T(8,128)S(1)}, u32[]{:S(2)}, u32[]{:S(2)}) %all-to-all-start.2) | async-done | bytes 65568 | tf_op jit(solution)/shard_map/all_to_all | solution.py:285
  89.1 0.0 copy-start.10
  89.1 0.6 copy-done.10
  89.7 1.5 %shard_map.105 = f32[32,8,128]{2,1,0:T(8,128)} custom-call(f32[16,8,128]{2,1,0:T(8,128)} %copy-done.10), custom_call_target="tpu_custom_call" | custom-call | tf_op jit(solution)/shard_map/pallas_call | solution.py:288
  91.3 9.9 %all-to-all-start.3 = ((f32[32,8,128]{2,1,0:T(8,128)}), f32[32,8,128]{2,1,0:T(8,128)S(1)}, u32[]{:S(2)}, u32[]{:S(2)}) async-start(f32[32,8,128]{2,1,0:T(8,128)} %shard_map.105), calls=%async_computation.3 | async-start | bytes 262144 | tf_op jit(solution)/shard_map/all_to_all | solution.py:294
  101.1 0.0 collective-permute-done.4.earlier_ref
  101.1 9.1 %all-to-all-done.3.parts_ref = f32[32,8,128]{2,1,0:T(8,128)S(1)} async-done(((f32[32,8,128]{2,1,0:T(8,128)}), f32[32,8,128]{2,1,0:T(8,128)S(1)}, u32[]{:S(2)}, u32[]{:S(2)}) %all-to-all-start.3) | async-done | bytes 131104 | tf_op jit(solution)/shard_map/all_to_all | solution.py:294
  110.3 0.0 copy-done.6
  110.3 0.0 copy-done.7
  110.3 0.0 copy-start.3
  110.3 1.0 copy-done.3
  111.3 1.4 %shard_map.106.copies = bf16[6,576,256]{2,1,0:T(8,128)(2,1)S(1)} custom-call(s32[3]{0:T(128)S(1)} %pad_add_fusion.place_ref, f32[32,8,128]{2,1,0:T(8,128)S(1)} %all-to-all-done.3.parts_ref, f32[1,256]{1,0:T(1,128)S(1)} %bitcast.20, f32[1,256]{1,0:T(1,128)S(1)} %bitcast.21, f32[288,256]{1,0:T(8,128)S(1)} %collective-permute-done.4.earlier_ref, ...), custom_call_target="tpu_custom_call" | custom-call | tf_op jit(solution)/shard_map/pallas_call | solution.py:347
  112.6 1.9 %all-gather.5.cloned.1.call-done.weight_ref = bf16[29,256,256]{2,1,0:T(8,128)(2,1)} async-done(((bf16[29,16,256]{2,1,0:T(8,128)(2,1)}), bf16[29,256,256]{2,1,0:T(8,128)(2,1)}) %all-gather.5.cloned.1.call-update) | async-done | bytes 3801104 | tf_op jit(solution)/shard_map/all_gather | solution.py:282
  114.5 0.0 copy-done.2
  114.5 0.0 copy-done.8
  114.5 0.0 copy-start.1
  114.5 2.1 %copy-done.1 = bf16[29,256,256]{2,1,0:T(8,128)(2,1)S(1)} copy-done((bf16[29,256,256]{2,1,0:T(8,128)(2,1)S(1)}, bf16[29,256,256]{2,1,0:T(8,128)(2,1)}, u32[]{:S(2)}) %copy-start.1) | copy-done | bytes 3801112
  116.6 1.8 %shard_map.107 = bf16[192,256]{1,0:T(8,128)(2,1)} custom-call(bf16[6,576,256]{2,1,0:T(8,128)(2,1)S(1)} %shard_map.106.copies, f32[1,256]{1,0:T(1,128)S(1)} %bitcast.22, bf16[192,512]{1,0:T(8,128)(2,1)S(1)} %bitcast.17, bf16[29,256,256]{2,1,0:T(8,128)(2,1)S(1)} %copy-done.1), custom_call_target="tpu_custom_call" | custom-call | tf_op jit(solution)/shard_map/pallas_call | solution.py:356
  (1 shorter events, 0.0 us)
Async XLA Ops:
  6.5 57.1 %copy-start.4 = (f32[512]{0:T(512)S(1)}, f32[512]{0:T(512)}, u32[]{:S(2)}) copy-start(f32[512]{0:T(512)} %param.11) | copy-start | bytes 6148
  6.5 57.1 %copy-start.5 = (f32[512]{0:T(512)S(1)}, f32[512]{0:T(512)}, u32[]{:S(2)}) copy-start(f32[512]{0:T(512)} %param.12) | copy-start | bytes 6148
  6.5 61.7 %all-gather.3.cloned.1.call-start = ((), (), s32[]{:S(2)}) async-start(), calls=%async_computation.4 | async-start | bytes 7520256 | tf_op jit(solution)/shard_map/all_gather | solution.py:279
  7.3 107.3 %all-gather.5.cloned.1.call-start = ((), (), s32[]{:S(2)}) async-start(), calls=%async_computation.5 | async-start | bytes 4038656 | tf_op jit(solution)/shard_map/all_gather | solution.py:282
  9.9 18.1 %collective-permute-start = (bf16[2,2,16,512]{3,2,1,0:T(8,128)(2,1)S(1)}, bf16[2,2,16,512]{3,2,1,0:T(8,128)(2,1)S(1)}, u32[]{:S(2)}, u32[]{:S(2)}) collective-permute-start(bf16[2,2,16,512]{3,2,1,0:T(8,128)(2,1)S(1)} %get-tuple-element.22), channel_id=1, source_target_pairs={{0,2},{2,4},{4,6},{6,8},{8,10},{10,12},{12,14},{1,3},{3,5},{5,7},{... | collective-permute-start | bytes 196616 | tf_op jit(solution)/shard_map/ppermute | solution.py:22
  13.9 14.1 %collective-permute-start.1 = (bf16[2,2,16,512]{3,2,1,0:T(8,128)(2,1)S(1)}, bf16[2,2,16,512]{3,2,1,0:T(8,128)(2,1)S(1)}, u32[]{:S(2)}, u32[]{:S(2)}) collective-permute-start(bf16[2,2,16,512]{3,2,1,0:T(8,128)(2,1)S(1)} %get-tuple-element.21), channel_id=1, source_target_pairs={{2,0},{4,2},{6,4},{8,6},{10,8},{12,10},{14,12},{3,1},{5,3},{7,5},{... | collective-permute-start | bytes 196616 | tf_op jit(solution)/shard_map/ppermute | solution.py:22
  16.9 18.2 %all-to-all-start = ((f32[16,8,128]{2,1,0:T(8,128)}), f32[16,8,128]{2,1,0:T(8,128)S(1)}, u32[]{:S(2)}, u32[]{:S(2)}) async-start(f32[16,8,128]{2,1,0:T(8,128)} %shard_map.100), calls=%async_computation | async-start | bytes 131072 | tf_op jit(solution)/shard_map/all_to_all | solution.py:285
  35.1 5.6 %copy-start.9 = (f32[16,8,128]{2,1,0:T(8,128)}, f32[16,8,128]{2,1,0:T(8,128)S(1)}, u32[]{:S(2)}) copy-start(f32[16,8,128]{2,1,0:T(8,128)S(1)} %all-to-all-done.parts_ref) | copy-start | bytes 196612
  36.1 18.4 %collective-permute-start.2 = (bf16[2,10,16,512]{3,2,1,0:T(8,128)(2,1)S(1)}, bf16[2,10,16,512]{3,2,1,0:T(8,128)(2,1)S(1)}, u32[]{:S(2)}, u32[]{:S(2)}) collective-permute-start(bf16[2,10,16,512]{3,2,1,0:T(8,128)(2,1)S(1)} %pad_maximum_fusion.own_ref), channel_id=1, source_target_pairs={{0,16},{16,32},{32,48},{48,64},{64,80},{80,96},{96,112},{112,128},... | collective-permute-start | bytes 983048 | tf_op jit(solution)/shard_map/ppermute | solution.py:22
  42.3 21.3 %all-to-all-start.1 = ((f32[32,8,128]{2,1,0:T(8,128)}), f32[32,8,128]{2,1,0:T(8,128)S(1)}, u32[]{:S(2)}, u32[]{:S(2)}) async-start(f32[32,8,128]{2,1,0:T(8,128)} %shard_map.101), calls=%async_computation.1 | async-start | bytes 262144 | tf_op jit(solution)/shard_map/all_to_all | solution.py:294
  55.3 8.3 %collective-permute-start.3 = (bf16[4,2,16,512]{3,2,1,0:T(8,128)(2,1)S(1)}, bf16[4,2,16,512]{3,2,1,0:T(8,128)(2,1)S(1)}, u32[]{:S(2)}, u32[]{:S(2)}) collective-permute-start(bf16[4,2,16,512]{3,2,1,0:T(8,128)(2,1)S(1)} %shard_map.102), channel_id=1, source_target_pairs={{0,1},{1,0},{2,3},{3,2},{4,5},{5,4},{6,7},{7,6},{8,9},{9,8},{10,11... | collective-permute-start | bytes 393224 | tf_op jit(solution)/shard_map/ppermute | solution.py:26
  66.2 2.0 %copy-start = (bf16[6,640,512]{2,1,0:T(8,128)(2,1)}, bf16[6,640,512]{2,1,0:T(8,128)(2,1)S(1)}, u32[]{:S(2)}) copy-start(bf16[6,640,512]{2,1,0:T(8,128)(2,1)S(1)} %shard_map.103.copies_ref) | copy-start | bytes 11796484
  68.2 42.1 %copy-start.6 = (f32[256]{0:T(256)S(1)}, f32[256]{0:T(256)}, u32[]{:S(2)}) copy-start(f32[256]{0:T(256)} %param.16) | copy-start | bytes 3076
  68.2 42.1 %copy-start.7 = (f32[256]{0:T(256)S(1)}, f32[256]{0:T(256)}, u32[]{:S(2)}) copy-start(f32[256]{0:T(256)} %param.17) | copy-start | bytes 3076
  68.2 46.3 %copy-start.2 = (bf16[2,6,16,512]{3,2,1,0:T(8,128)(2,1)S(1)}, bf16[2,6,16,512]{3,2,1,0:T(8,128)(2,1)}, u32[]{:S(2)}) copy-start(bf16[2,6,16,512]{3,2,1,0:T(8,128)(2,1)} %param.10) | copy-start | bytes 589828
  68.2 46.3 %copy-start.8 = (f32[256]{0:T(256)S(1)}, f32[256]{0:T(256)}, u32[]{:S(2)}) copy-start(f32[256]{0:T(256)} %param.19) | copy-start | bytes 3076
  75.8 13.3 %all-to-all-start.2 = ((f32[16,8,128]{2,1,0:T(8,128)}), f32[16,8,128]{2,1,0:T(8,128)S(1)}, u32[]{:S(2)}, u32[]{:S(2)}) async-start(f32[16,8,128]{2,1,0:T(8,128)} %get-tuple-element.15), calls=%async_computation.2 | async-start | bytes 131072 | tf_op jit(solution)/shard_map/all_to_all | solution.py:285
  81.2 19.9 %collective-permute-start.4 = (f32[288,256]{1,0:T(8,128)}, f32[288,256]{1,0:T(8,128)S(1)}, u32[]{:S(2)}, u32[]{:S(2)}) collective-permute-start(f32[288,256]{1,0:T(8,128)} %get-tuple-element.16.middle_ref), channel_id=1, source_target_pairs={{0,16},{16,32},{32,48},{48,64},{64,80},{80,96},{96,112},{112,128},... | collective-permute-start | bytes 884744 | tf_op jit(solution)/shard_map/ppermute | solution.py:22
  89.1 0.6 copy-start.10
  91.3 19.0 %all-to-all-start.3 = ((f32[32,8,128]{2,1,0:T(8,128)}), f32[32,8,128]{2,1,0:T(8,128)S(1)}, u32[]{:S(2)}, u32[]{:S(2)}) async-start(f32[32,8,128]{2,1,0:T(8,128)} %shard_map.105), calls=%async_computation.3 | async-start | bytes 262144 | tf_op jit(solution)/shard_map/all_to_all | solution.py:294
  110.3 1.0 copy-start.3
  114.5 2.1 %copy-start.1 = (bf16[29,256,256]{2,1,0:T(8,128)(2,1)S(1)}, bf16[29,256,256]{2,1,0:T(8,128)(2,1)}, u32[]{:S(2)}) copy-start(bf16[29,256,256]{2,1,0:T(8,128)(2,1)} %all-gather.5.cloned.1.call-done.weight_ref) | copy-start | bytes 11403268
Sparse Core Ops, SparseCore 0:
  9.5 58.5 all-gather.2
  70.3 44.2 all-gather.4

commit v9 on v6

--- a/solution.py
+++ b/solution.py
@@ -166,16 +166,21 @@
         pltpu.make_async_copy(gathered_ref.at[3 * i : 3 * i + 3], weights.at[3 * i : 3 * i + 3], arrived.at[6 + i])
         for i in range(9)
     ]
-    for dy in range(3):
+
+    def start(dy):
         for copy in [*layouts[2 * dy : 2 * dy + 2], *fetches[dy::3]]:
             copy.start()
+
+    start(0)
+    start(1)
     middle_ref[...] = jnp.broadcast_to(bias_ref[...], middle_ref.shape)
     depth = 3 * weights.shape[1]
     for dy in range(3):
-        for copy in layouts[2 * dy : 2 * dy + 2]:
+        for copy in [*layouts[2 * dy : 2 * dy + 2], *fetches[dy::3]]:
             copy.wait()
+        if dy == 0:
+            start(2)
         for dt in range(3):
-            fetches[3 * dt + dy].wait()
             weight = weights[9 * dt + 3 * dy : 9 * dt + 3 * dy + 3].reshape(depth, weights.shape[2])
 
             def window(dx, dy=dy, dt=dt):

time: 126 us -> 126 us (level)
  no operation moved by 1% of the time
where the time goes in v9:
time: 126 us; the launch traced here: 125 us
  starting transfers between devices  53.1 us (42%)
  waiting for transfers between devices  29.7 us (24%)
  Pallas kernels  18.8 us (15%)
  between operations  13.6 us (11%)
  local copies, waits for them, and re-layouts  7.37 us (6%)
  other arithmetic  2.75 us (2%)
    all_to_all x2, starting transfers between devices, shared(): return (lax.all_to_all(stats, TM, 0, 0, tiled=True), beside)  22 us
    all_to_all x2, starting transfers between devices, shared(): stats = lax.all_to_all(stats, ('row', 'col'), 0, 0, tiled=True)  15.8 us
    all_to_all x2, waiting for transfers between devices, shared(): return (lax.all_to_all(stats, TM, 0, 0, tiled=True), beside)  14.9 us
    ppermute x4, starting transfers between devices, moved(): return lax.ppermute(block, axis, route)  12.7 us
    all_to_all x2, waiting for transfers between devices, shared(): stats = lax.all_to_all(stats, ('row', 'col'), 0, 0, tiled=True)  12.1 us
    pallas_call x1, Pallas kernels, per_device(): pl.pallas_call(functools.partial(conv1_kernel, float(positions)), out_sha...  7.5 us
    unnamed x22, local copies, waits for them, and re-layouts  5.71 us
    pallas_call x2, Pallas kernels, shared(): pl.pallas_call(functools.partial(merge_kernel, count), out_shape=jax.Shap...  3.08 us
  transfers between devices with their start and end apart: 11, of which 5 were waited for; matrix products, arithmetic and copies ran while one was open for 4% of the time, Pallas kernels for 14%

profile of v9, /device:TPU:1, one launch (start us, length us, event | category | flops | bytes accessed | tf_op | source)
XLA Modules:
  0.0 125.2 jit_solution(5672510274368726730)
XLA Ops:
  6.5 0.0 copy-start.4
  6.5 0.0 copy-start.5
  6.5 0.0 all-gather.3.cloned.1.call-start
  6.5 0.7 all-gather.3.cloned.1.call-update
  7.3 0.0 all-gather.5.cloned.1.call-start
  7.3 1.7 %pad_maximum_fusion.1 = bf16[29,16,256]{2,1,0:T(8,128)(2,1)} fusion(bf16[2,16,256]{2,1,0:T(8,128)(2,1)} %bitcast.23, bf16[27,16,256]{2,1,0:T(8,128)(2,1)} %param.18), kind=kLoop, calls=%fused_computation.1 | loop fusion | flops 118784 | bytes 475136 | tf_op jit(solution)/shard_map/concatenate | solution.py:288
  9.0 0.0 all-gather.5.cloned.1.call-update
  9.0 0.9 fusion
  9.9 4.0 %collective-permute-start = (bf16[2,2,16,512]{3,2,1,0:T(8,128)(2,1)S(1)}, bf16[2,2,16,512]{3,2,1,0:T(8,128)(2,1)S(1)}, u32[]{:S(2)}, u32[]{:S(2)}) collective-permute-start(bf16[2,2,16,512]{3,2,1,0:T(8,128)(2,1)S(1)} %get-tuple-element.22), channel_id=1, source_target_pairs={{0,2},{2,4},{4,6},{6,8},{8,10},{10,12},{12,14},{1,3},{3,5},{5,7},{... | collective-permute-start | bytes 196616 | tf_op jit(solution)/shard_map/ppermute | solution.py:22
  13.9 1.3 %collective-permute-start.1 = (bf16[2,2,16,512]{3,2,1,0:T(8,128)(2,1)S(1)}, bf16[2,2,16,512]{3,2,1,0:T(8,128)(2,1)S(1)}, u32[]{:S(2)}, u32[]{:S(2)}) collective-permute-start(bf16[2,2,16,512]{3,2,1,0:T(8,128)(2,1)S(1)} %get-tuple-element.21), channel_id=1, source_target_pairs={{2,0},{4,2},{6,4},{8,6},{10,8},{12,10},{14,12},{3,1},{5,3},{7,5},{... | collective-permute-start | bytes 196616 | tf_op jit(solution)/shard_map/ppermute | solution.py:22
  15.2 1.7 %shard_map.100 = f32[16,8,128]{2,1,0:T(8,128)} custom-call(bf16[192,512]{1,0:T(8,128)(2,1)} %bitcast.16), custom_call_target="tpu_custom_call" | custom-call | tf_op jit(solution)/shard_map/pallas_call | solution.py:302
  16.9 10.3 %all-to-all-start = ((f32[16,8,128]{2,1,0:T(8,128)}), f32[16,8,128]{2,1,0:T(8,128)S(1)}, u32[]{:S(2)}, u32[]{:S(2)}) async-start(f32[16,8,128]{2,1,0:T(8,128)} %shard_map.100), calls=%async_computation | async-start | bytes 131072 | tf_op jit(solution)/shard_map/all_to_all | solution.py:291
  27.2 0.8 slice_bitcast_fusion.1
  28.0 0.0 collective-permute-done
  28.0 0.0 collective-permute-done.1
  28.0 7.1 %all-to-all-done.parts_ref = f32[16,8,128]{2,1,0:T(8,128)S(1)} async-done(((f32[16,8,128]{2,1,0:T(8,128)}), f32[16,8,128]{2,1,0:T(8,128)S(1)}, u32[]{:S(2)}, u32[]{:S(2)}) %all-to-all-start) | async-done | bytes 65568 | tf_op jit(solution)/shard_map/all_to_all | solution.py:291
  35.1 0.0 copy-start.9
  35.1 1.0 pad_maximum_fusion.own_ref
  36.1 4.6 %collective-permute-start.2 = (bf16[2,10,16,512]{3,2,1,0:T(8,128)(2,1)S(1)}, bf16[2,10,16,512]{3,2,1,0:T(8,128)(2,1)S(1)}, u32[]{:S(2)}, u32[]{:S(2)}) collective-permute-start(bf16[2,10,16,512]{3,2,1,0:T(8,128)(2,1)S(1)} %pad_maximum_fusion.own_ref), channel_id=1, source_target_pairs={{0,16},{16,32},{32,48},{48,64},{64,80},{80,96},{96,112},{112,128},... | collective-permute-start | bytes 983048 | tf_op jit(solution)/shard_map/ppermute | solution.py:22
  40.7 0.0 copy-done.9
  40.7 1.5 %shard_map.101 = f32[32,8,128]{2,1,0:T(8,128)} custom-call(f32[16,8,128]{2,1,0:T(8,128)} %copy-done.9), custom_call_target="tpu_custom_call" | custom-call | tf_op jit(solution)/shard_map/pallas_call | solution.py:294
  42.3 12.2 %all-to-all-start.1 = ((f32[32,8,128]{2,1,0:T(8,128)}), f32[32,8,128]{2,1,0:T(8,128)S(1)}, u32[]{:S(2)}, u32[]{:S(2)}) async-start(f32[32,8,128]{2,1,0:T(8,128)} %shard_map.101), calls=%async_computation.1 | async-start | bytes 262144 | tf_op jit(solution)/shard_map/all_to_all | solution.py:300
  54.4 0.1 pad_add_fusion.place_ref
  54.5 0.0 collective-permute-done.2.earlier_ref
  54.5 0.8 shard_map.102
  55.3 2.5 %collective-permute-start.3 = (bf16[4,2,16,512]{3,2,1,0:T(8,128)(2,1)S(1)}, bf16[4,2,16,512]{3,2,1,0:T(8,128)(2,1)S(1)}, u32[]{:S(2)}, u32[]{:S(2)}) collective-permute-start(bf16[4,2,16,512]{3,2,1,0:T(8,128)(2,1)S(1)} %shard_map.102), channel_id=1, source_target_pairs={{0,1},{1,0},{2,3},{3,2},{4,5},{5,4},{6,7},{7,6},{8,9},{9,8},{10,11... | collective-permute-start | bytes 393224 | tf_op jit(solution)/shard_map/ppermute | solution.py:26
  57.8 5.7 %all-to-all-done.1.parts_ref = f32[32,8,128]{2,1,0:T(8,128)S(1)} async-done(((f32[32,8,128]{2,1,0:T(8,128)}), f32[32,8,128]{2,1,0:T(8,128)S(1)}, u32[]{:S(2)}, u32[]{:S(2)}) %all-to-all-start.1) | async-done | bytes 131104 | tf_op jit(solution)/shard_map/all_to_all | solution.py:300
  63.6 0.0 collective-permute-done.3.border_ref
  63.6 0.0 copy-done.4
  63.6 0.0 copy-done.5
  63.6 2.6 %shard_map.103.copies_ref = bf16[6,640,512]{2,1,0:T(8,128)(2,1)S(1)} custom-call(s32[3]{0:T(128)S(1)} %pad_add_fusion.place_ref, f32[32,8,128]{2,1,0:T(8,128)S(1)} %all-to-all-done.1.parts_ref, f32[1,512]{1,0:T(1,128)S(1)} %bitcast.18, f32[1,512]{1,0:T(1,128)S(1)} %bitcast.19, bf16[2,10,16,512]{3,2,1,0:T(8,128)(2,1)S(1)} %collective-permute-done.2.earlier_ref, ...), custom_call_target="tpu_custom_call" | custom-call | tf_op jit(solution)/shard_map/pallas_call | solution.py:325
  66.2 0.0 copy-start
  66.2 2.0 %copy-done = bf16[6,640,512]{2,1,0:T(8,128)(2,1)} copy-done((bf16[6,640,512]{2,1,0:T(8,128)(2,1)}, bf16[6,640,512]{2,1,0:T(8,128)(2,1)S(1)}, u32[]{:S(2)}) %copy-start) | copy-done | bytes 3932184
  68.2 0.0 all-gather.3.cloned.1.call-done.gathered_ref
  68.2 0.0 copy-start.6
  68.2 0.0 copy-start.7
  68.2 0.0 copy-start.2
  68.2 0.0 copy-start.8
  68.2 7.5 %shard_map.104 = (f32[288,256]{1,0:T(8,128)}, f32[16,8,128]{2,1,0:T(8,128)}) custom-call(f32[1,256]{1,0:T(1,128)} %bitcast.24, bf16[6,640,512]{2,1,0:T(8,128)(2,1)} %copy-done, bf16[27,512,256]{2,1,0:T(8,128)(2,1)} %all-gather.3.cloned.1.call-done.gathered_ref), custom_call_target="tpu_custom_call" | custom-call | tf_op jit(solution)/shard_map/pallas_call | solution.py:334
  75.8 5.4 %all-to-all-start.2 = ((f32[16,8,128]{2,1,0:T(8,128)}), f32[16,8,128]{2,1,0:T(8,128)S(1)}, u32[]{:S(2)}, u32[]{:S(2)}) async-start(f32[16,8,128]{2,1,0:T(8,128)} %get-tuple-element.15), calls=%async_computation.2 | async-start | bytes 131072 | tf_op jit(solution)/shard_map/all_to_all | solution.py:291
  81.2 2.9 %collective-permute-start.4 = (f32[288,256]{1,0:T(8,128)}, f32[288,256]{1,0:T(8,128)S(1)}, u32[]{:S(2)}, u32[]{:S(2)}) collective-permute-start(f32[288,256]{1,0:T(8,128)} %get-tuple-element.16.middle_ref), channel_id=1, source_target_pairs={{0,16},{16,32},{32,48},{48,64},{64,80},{80,96},{96,112},{112,128},... | collective-permute-start | bytes 884744 | tf_op jit(solution)/shard_map/ppermute | solution.py:22
  84.0 5.0 %all-to-all-done.2.parts_ref = f32[16,8,128]{2,1,0:T(8,128)S(1)} async-done(((f32[16,8,128]{2,1,0:T(8,128)}), f32[16,8,128]{2,1,0:T(8,128)S(1)}, u32[]{:S(2)}, u32[]{:S(2)}) %all-to-all-start.2) | async-done | bytes 65568 | tf_op jit(solution)/shard_map/all_to_all | solution.py:291
  89.0 0.0 copy-start.10
  89.0 0.6 copy-done.10
  89.7 1.5 %shard_map.105 = f32[32,8,128]{2,1,0:T(8,128)} custom-call(f32[16,8,128]{2,1,0:T(8,128)} %copy-done.10), custom_call_target="tpu_custom_call" | custom-call | tf_op jit(solution)/shard_map/pallas_call | solution.py:294
  91.2 9.8 %all-to-all-start.3 = ((f32[32,8,128]{2,1,0:T(8,128)}), f32[32,8,128]{2,1,0:T(8,128)S(1)}, u32[]{:S(2)}, u32[]{:S(2)}) async-start(f32[32,8,128]{2,1,0:T(8,128)} %shard_map.105), calls=%async_computation.3 | async-start | bytes 262144 | tf_op jit(solution)/shard_map/all_to_all | solution.py:300
  101.1 0.0 collective-permute-done.4.earlier_ref
  101.1 9.1 %all-to-all-done.3.parts_ref = f32[32,8,128]{2,1,0:T(8,128)S(1)} async-done(((f32[32,8,128]{2,1,0:T(8,128)}), f32[32,8,128]{2,1,0:T(8,128)S(1)}, u32[]{:S(2)}, u32[]{:S(2)}) %all-to-all-start.3) | async-done | bytes 131104 | tf_op jit(solution)/shard_map/all_to_all | solution.py:300
  110.2 0.0 copy-done.6
  110.2 0.0 copy-done.7
  110.2 0.0 copy-start.3
  110.2 1.0 copy-done.3
  111.2 1.4 %shard_map.106.copies = bf16[6,576,256]{2,1,0:T(8,128)(2,1)S(1)} custom-call(s32[3]{0:T(128)S(1)} %pad_add_fusion.place_ref, f32[32,8,128]{2,1,0:T(8,128)S(1)} %all-to-all-done.3.parts_ref, f32[1,256]{1,0:T(1,128)S(1)} %bitcast.20, f32[1,256]{1,0:T(1,128)S(1)} %bitcast.21, f32[288,256]{1,0:T(8,128)S(1)} %collective-permute-done.4.earlier_ref, ...), custom_call_target="tpu_custom_call" | custom-call | tf_op jit(solution)/shard_map/pallas_call | solution.py:353
  112.6 1.9 %all-gather.5.cloned.1.call-done.weight_ref = bf16[29,256,256]{2,1,0:T(8,128)(2,1)} async-done(((bf16[29,16,256]{2,1,0:T(8,128)(2,1)}), bf16[29,256,256]{2,1,0:T(8,128)(2,1)}) %all-gather.5.cloned.1.call-update) | async-done | bytes 3801104 | tf_op jit(solution)/shard_map/all_gather | solution.py:288
  114.5 0.0 copy-done.2
  114.5 0.0 copy-done.8
  114.5 0.0 copy-start.1
  114.5 2.1 %copy-done.1 = bf16[29,256,256]{2,1,0:T(8,128)(2,1)S(1)} copy-done((bf16[29,256,256]{2,1,0:T(8,128)(2,1)S(1)}, bf16[29,256,256]{2,1,0:T(8,128)(2,1)}, u32[]{:S(2)}) %copy-start.1) | copy-done | bytes 3801112
  116.6 1.8 %shard_map.107 = bf16[192,256]{1,0:T(8,128)(2,1)} custom-call(bf16[6,576,256]{2,1,0:T(8,128)(2,1)S(1)} %shard_map.106.copies, f32[1,256]{1,0:T(1,128)S(1)} %bitcast.22, bf16[192,512]{1,0:T(8,128)(2,1)S(1)} %bitcast.17, bf16[29,256,256]{2,1,0:T(8,128)(2,1)S(1)} %copy-done.1), custom_call_target="tpu_custom_call" | custom-call | tf_op jit(solution)/shard_map/pallas_call | solution.py:362
  (1 shorter events, 0.0 us)
Async XLA Ops:
  6.5 57.1 %copy-start.4 = (f32[512]{0:T(512)S(1)}, f32[512]{0:T(512)}, u32[]{:S(2)}) copy-start(f32[512]{0:T(512)} %param.11) | copy-start | bytes 6148
  6.5 57.1 %copy-start.5 = (f32[512]{0:T(512)S(1)}, f32[512]{0:T(512)}, u32[]{:S(2)}) copy-start(f32[512]{0:T(512)} %param.12) | copy-start | bytes 6148
  6.5 61.7 %all-gather.3.cloned.1.call-start = ((), (), s32[]{:S(2)}) async-start(), calls=%async_computation.4 | async-start | bytes 7520256 | tf_op jit(solution)/shard_map/all_gather | solution.py:285
  7.3 107.2 %all-gather.5.cloned.1.call-start = ((), (), s32[]{:S(2)}) async-start(), calls=%async_computation.5 | async-start | bytes 4038656 | tf_op jit(solution)/shard_map/all_gather | solution.py:288
  9.9 18.1 %collective-permute-start = (bf16[2,2,16,512]{3,2,1,0:T(8,128)(2,1)S(1)}, bf16[2,2,16,512]{3,2,1,0:T(8,128)(2,1)S(1)}, u32[]{:S(2)}, u32[]{:S(2)}) collective-permute-start(bf16[2,2,16,512]{3,2,1,0:T(8,128)(2,1)S(1)} %get-tuple-element.22), channel_id=1, source_target_pairs={{0,2},{2,4},{4,6},{6,8},{8,10},{10,12},{12,14},{1,3},{3,5},{5,7},{... | collective-permute-start | bytes 196616 | tf_op jit(solution)/shard_map/ppermute | solution.py:22
  13.9 14.1 %collective-permute-start.1 = (bf16[2,2,16,512]{3,2,1,0:T(8,128)(2,1)S(1)}, bf16[2,2,16,512]{3,2,1,0:T(8,128)(2,1)S(1)}, u32[]{:S(2)}, u32[]{:S(2)}) collective-permute-start(bf16[2,2,16,512]{3,2,1,0:T(8,128)(2,1)S(1)} %get-tuple-element.21), channel_id=1, source_target_pairs={{2,0},{4,2},{6,4},{8,6},{10,8},{12,10},{14,12},{3,1},{5,3},{7,5},{... | collective-permute-start | bytes 196616 | tf_op jit(solution)/shard_map/ppermute | solution.py:22
  16.9 18.2 %all-to-all-start = ((f32[16,8,128]{2,1,0:T(8,128)}), f32[16,8,128]{2,1,0:T(8,128)S(1)}, u32[]{:S(2)}, u32[]{:S(2)}) async-start(f32[16,8,128]{2,1,0:T(8,128)} %shard_map.100), calls=%async_computation | async-start | bytes 131072 | tf_op jit(solution)/shard_map/all_to_all | solution.py:291
  35.1 5.6 %copy-start.9 = (f32[16,8,128]{2,1,0:T(8,128)}, f32[16,8,128]{2,1,0:T(8,128)S(1)}, u32[]{:S(2)}) copy-start(f32[16,8,128]{2,1,0:T(8,128)S(1)} %all-to-all-done.parts_ref) | copy-start | bytes 196612
  36.1 18.4 %collective-permute-start.2 = (bf16[2,10,16,512]{3,2,1,0:T(8,128)(2,1)S(1)}, bf16[2,10,16,512]{3,2,1,0:T(8,128)(2,1)S(1)}, u32[]{:S(2)}, u32[]{:S(2)}) collective-permute-start(bf16[2,10,16,512]{3,2,1,0:T(8,128)(2,1)S(1)} %pad_maximum_fusion.own_ref), channel_id=1, source_target_pairs={{0,16},{16,32},{32,48},{48,64},{64,80},{80,96},{96,112},{112,128},... | collective-permute-start | bytes 983048 | tf_op jit(solution)/shard_map/ppermute | solution.py:22
  42.3 21.3 %all-to-all-start.1 = ((f32[32,8,128]{2,1,0:T(8,128)}), f32[32,8,128]{2,1,0:T(8,128)S(1)}, u32[]{:S(2)}, u32[]{:S(2)}) async-start(f32[32,8,128]{2,1,0:T(8,128)} %shard_map.101), calls=%async_computation.1 | async-start | bytes 262144 | tf_op jit(solution)/shard_map/all_to_all | solution.py:300
  55.3 8.3 %collective-permute-start.3 = (bf16[4,2,16,512]{3,2,1,0:T(8,128)(2,1)S(1)}, bf16[4,2,16,512]{3,2,1,0:T(8,128)(2,1)S(1)}, u32[]{:S(2)}, u32[]{:S(2)}) collective-permute-start(bf16[4,2,16,512]{3,2,1,0:T(8,128)(2,1)S(1)} %shard_map.102), channel_id=1, source_target_pairs={{0,1},{1,0},{2,3},{3,2},{4,5},{5,4},{6,7},{7,6},{8,9},{9,8},{10,11... | collective-permute-start | bytes 393224 | tf_op jit(solution)/shard_map/ppermute | solution.py:26
  66.2 2.0 %copy-start = (bf16[6,640,512]{2,1,0:T(8,128)(2,1)}, bf16[6,640,512]{2,1,0:T(8,128)(2,1)S(1)}, u32[]{:S(2)}) copy-start(bf16[6,640,512]{2,1,0:T(8,128)(2,1)S(1)} %shard_map.103.copies_ref) | copy-start | bytes 11796484
  68.2 42.0 %copy-start.6 = (f32[256]{0:T(256)S(1)}, f32[256]{0:T(256)}, u32[]{:S(2)}) copy-start(f32[256]{0:T(256)} %param.16) | copy-start | bytes 3076
  68.2 42.0 %copy-start.7 = (f32[256]{0:T(256)S(1)}, f32[256]{0:T(256)}, u32[]{:S(2)}) copy-start(f32[256]{0:T(256)} %param.17) | copy-start | bytes 3076
  68.2 46.3 %copy-start.2 = (bf16[2,6,16,512]{3,2,1,0:T(8,128)(2,1)S(1)}, bf16[2,6,16,512]{3,2,1,0:T(8,128)(2,1)}, u32[]{:S(2)}) copy-start(bf16[2,6,16,512]{3,2,1,0:T(8,128)(2,1)} %param.10) | copy-start | bytes 589828
  68.2 46.3 %copy-start.8 = (f32[256]{0:T(256)S(1)}, f32[256]{0:T(256)}, u32[]{:S(2)}) copy-start(f32[256]{0:T(256)} %param.19) | copy-start | bytes 3076
  75.8 13.3 %all-to-all-start.2 = ((f32[16,8,128]{2,1,0:T(8,128)}), f32[16,8,128]{2,1,0:T(8,128)S(1)}, u32[]{:S(2)}, u32[]{:S(2)}) async-start(f32[16,8,128]{2,1,0:T(8,128)} %get-tuple-element.15), calls=%async_computation.2 | async-start | bytes 131072 | tf_op jit(solution)/shard_map/all_to_all | solution.py:291
  81.2 19.9 %collective-permute-start.4 = (f32[288,256]{1,0:T(8,128)}, f32[288,256]{1,0:T(8,128)S(1)}, u32[]{:S(2)}, u32[]{:S(2)}) collective-permute-start(f32[288,256]{1,0:T(8,128)} %get-tuple-element.16.middle_ref), channel_id=1, source_target_pairs={{0,16},{16,32},{32,48},{48,64},{64,80},{80,96},{96,112},{112,128},... | collective-permute-start | bytes 884744 | tf_op jit(solution)/shard_map/ppermute | solution.py:22
  89.0 0.6 copy-start.10
  91.2 19.0 %all-to-all-start.3 = ((f32[32,8,128]{2,1,0:T(8,128)}), f32[32,8,128]{2,1,0:T(8,128)S(1)}, u32[]{:S(2)}, u32[]{:S(2)}) async-start(f32[32,8,128]{2,1,0:T(8,128)} %shard_map.105), calls=%async_computation.3 | async-start | bytes 262144 | tf_op jit(solution)/shard_map/all_to_all | solution.py:300
  110.2 1.0 copy-start.3
  114.5 2.1 %copy-start.1 = (bf16[29,256,256]{2,1,0:T(8,128)(2,1)S(1)}, bf16[29,256,256]{2,1,0:T(8,128)(2,1)}, u32[]{:S(2)}) copy-start(bf16[29,256,256]{2,1,0:T(8,128)(2,1)} %all-gather.5.cloned.1.call-done.weight_ref) | copy-start | bytes 11403268
Sparse Core Ops, SparseCore 0:
  9.5 58.5 all-gather.2
  70.3 44.1 all-gather.4
